TPU v7x, 32 devices: a whole 2x2x4 slice. The times are simulated.
32 devices in a mesh: dp: 4 (over x, core), fsdp: 8 (over z, y).
Axes of the slice: x: 2, y: 2, z: 4, core: 2. Of those that a mesh axis runs over, the one named last changes fastest.
Arguments:
- tokens: bfloat16 [32768, 512], P(('dp', 'fsdp')), may hold values from -6 to 6
- gating: bfloat16 [512, 3072], P(None, ('dp', 'fsdp')), may hold values from -0.25 to 0.25
- offsets: bfloat16 [3072], P(('dp', 'fsdp')), may hold values from -4 to 4
- prescale: bfloat16 [512], P(('dp', 'fsdp')), may hold values from 0.25 to 1.75
- readout: bfloat16 [1024, 512], P(('dp', 'fsdp')), may hold values from -0.1875 to 0.1875
- midscale: bfloat16 [512], P(('dp', 'fsdp')), may hold values from 0.25 to 1.75
- expand: bfloat16 [512, 2048], P(None, ('dp', 'fsdp')), may hold values from -0.25 to 0.25
- shifts: bfloat16 [2048], P(('dp', 'fsdp')), may hold values from -3 to 3
- contract: bfloat16 [2048, 512], P(('dp', 'fsdp')), may hold values from -0.125 to 0.125
- cotangent: bfloat16 [32768, 512], P(('dp', 'fsdp')), may hold values from -6 to 6
Outputs:
- block_output: bfloat16 [32768, 512], P(('dp', 'fsdp'))
- tokens_grad: float32 [32768, 512], P(('dp', 'fsdp'))
- gating_grad: float32 [512, 3072], P(None, ('dp', 'fsdp'))
- offsets_grad: float32 [3072], P(('dp', 'fsdp'))
- prescale_grad: float32 [512], P(('dp', 'fsdp'))
- readout_grad: float32 [1024, 512], P(('dp', 'fsdp'))
- midscale_grad: float32 [512], P(('dp', 'fsdp'))
- expand_grad: float32 [512, 2048], P(None, ('dp', 'fsdp'))
- shifts_grad: float32 [2048], P(('dp', 'fsdp'))
- contract_grad: float32 [2048, 512], P(('dp', 'fsdp'))
All inputs are finite; a program needn't handle non-finite values.
Results may differ from a plain program's by a relative error of at most 0.0063.
Values may be sent and summed in bfloat16 or wider, within the bound.
No kernel may reach another device: no remote copies, remote signals or barrier semaphores. Data moves between devices by JAX's collectives and lax.ppermute only.
A program may use at most 192 MiB of HBM per device.

v0:
```python
from functools import partial

import jax
import jax.numpy as jnp
from jax import lax
from jax.sharding import PartitionSpec as P

LEN = 1024


epsilon = 1e-06


def rms_scale(values, gain):
    return values * lax.rsqrt(jnp.mean(values * values, axis=-1, keepdims=True) + epsilon) * gain


def gate_math(gate_pre):
    forget_pre, input_pre, candidate = jnp.split(gate_pre, 3, axis=-1)
    forget_sig = jax.nn.sigmoid(forget_pre)
    input_sig = jax.nn.sigmoid(input_pre)
    retain = forget_sig / (forget_sig + input_sig)
    inflow = input_sig / (forget_sig + input_sig) * candidate
    return (retain, inflow)


def shifted(values, stride, fill, reverse):
    padding = jnp.full_like(values[:, :stride], fill)
    if reverse:
        return jnp.concatenate([values[:, stride:], padding], axis=1)
    return jnp.concatenate([padding, values[:, :-stride]], axis=1)


def doubling(decay, drive, reverse):
    stride = 1
    length = decay.shape[1]
    while stride < length:
        drive = decay * shifted(drive, stride, 0.0, reverse) + drive
        decay = decay * shifted(decay, stride, 1.0, reverse)
        stride = stride * 2
    return (decay, drive)


def linear_scan(decay, drive, reverse):
    seqs, length, width = decay.shape
    block = min(64, length)
    count = length // block
    block_decay, block_drive = doubling(
        decay.reshape(seqs * count, block, width),
        drive.reshape(seqs * count, block, width),
        reverse,
    )
    block_decay = block_decay.reshape(seqs, count, block, width)
    block_drive = block_drive.reshape(seqs, count, block, width)
    edge = 0 if reverse else block - 1
    _, edge_state = doubling(block_decay[:, :, edge], block_drive[:, :, edge], reverse)
    entering = shifted(edge_state, 1, 0.0, reverse)
    states = block_drive + block_decay * entering[:, :, None, :]
    return states.reshape(seqs, length, width)


def matmul(left, right):
    return jnp.dot(left, right, preferred_element_type=jnp.float32)


def across(left, right):
    return lax.dot_general(
        left, right, (((0,), (0,)), ((), ())), preferred_element_type=jnp.float32
    )


def against(left, right):
    return lax.dot_general(
        left, right, (((1,), (1,)), ((), ())), preferred_element_type=jnp.float32
    )


def by_sequence(values):
    return values.reshape(-1, LEN, values.shape[-1])


def shards(
    tokens, gating, offsets, prescale, readout, midscale, expand, shifts, contract, cotangent
):
    weights = (
        lax.all_gather(gating, ("dp", "fsdp"), axis=1, tiled=True),
        lax.all_gather(offsets, ("dp", "fsdp"), axis=0, tiled=True),
        lax.all_gather(prescale, ("dp", "fsdp"), axis=0, tiled=True),
        lax.all_gather(readout, ("dp", "fsdp"), axis=0, tiled=True),
        lax.all_gather(midscale, ("dp", "fsdp"), axis=0, tiled=True),
        lax.all_gather(expand, ("dp", "fsdp"), axis=1, tiled=True),
        lax.all_gather(shifts, ("dp", "fsdp"), axis=0, tiled=True),
        lax.all_gather(contract, ("dp", "fsdp"), axis=0, tiled=True),
    )
    (
        full_gating,
        full_offsets,
        full_prescale,
        full_readout,
        full_midscale,
        full_expand,
        full_shifts,
        full_contract,
    ) = weights
    inputs = tokens.astype(jnp.float32)
    gain_one = full_prescale.astype(jnp.float32)
    gain_two = full_midscale.astype(jnp.float32)
    normed = rms_scale(inputs, gain_one).astype(jnp.bfloat16)
    gate_pre = matmul(normed, full_gating) + full_offsets.astype(jnp.float32)
    retain, inflow = gate_math(gate_pre)
    retain_seq = by_sequence(retain)
    states_seq = linear_scan(retain_seq, by_sequence(inflow), False)
    states = states_seq.reshape(retain.shape)
    states_low = states.astype(jnp.bfloat16)
    residual = inputs + matmul(states_low, full_readout)
    normed_two = rms_scale(residual, gain_two).astype(jnp.bfloat16)
    expand_pre = matmul(normed_two, full_expand) + full_shifts.astype(jnp.float32)
    hidden = jax.nn.gelu(expand_pre, approximate=True).astype(jnp.bfloat16)
    block_output = (residual + matmul(hidden, full_contract)).astype(jnp.bfloat16)
    again = (
        lax.all_gather(gating, ("dp", "fsdp"), axis=1, tiled=True),
        lax.all_gather(offsets, ("dp", "fsdp"), axis=0, tiled=True),
        lax.all_gather(prescale, ("dp", "fsdp"), axis=0, tiled=True),
        lax.all_gather(readout, ("dp", "fsdp"), axis=0, tiled=True),
        lax.all_gather(midscale, ("dp", "fsdp"), axis=0, tiled=True),
        lax.all_gather(expand, ("dp", "fsdp"), axis=1, tiled=True),
        lax.all_gather(shifts, ("dp", "fsdp"), axis=0, tiled=True),
        lax.all_gather(contract, ("dp", "fsdp"), axis=0, tiled=True),
    )
    back_gating = again[0]
    back_readout = again[3]
    back_expand = again[5]
    back_contract = again[7]
    contract_grad = across(hidden, cotangent)
    hidden_grad = against(cotangent, back_contract)
    _, gelu_pull = jax.vjp(partial(jax.nn.gelu, approximate=True), expand_pre)
    expand_pre_grad = gelu_pull(hidden_grad)[0].astype(jnp.bfloat16)
    expand_grad = across(normed_two, expand_pre_grad)
    shifts_grad = jnp.sum(expand_pre_grad.astype(jnp.float32), axis=0)
    normed_two_grad = against(expand_pre_grad, back_expand)
    _, second_pull = jax.vjp(rms_scale, residual, gain_two)
    residual_norm_grad, midscale_grad = second_pull(normed_two_grad)
    residual_grad = cotangent.astype(jnp.float32) + residual_norm_grad
    branch_one_grad = residual_grad.astype(jnp.bfloat16)
    readout_grad = across(states_low, branch_one_grad)
    states_grad = against(branch_one_grad, back_readout)
    next_retain = shifted(retain_seq, 1, 0.0, True)
    carried_seq = linear_scan(next_retain, by_sequence(states_grad), True)
    prior_states = shifted(states_seq, 1, 0.0, False)
    retain_grad = (carried_seq * prior_states).reshape(retain.shape)
    inflow_grad = carried_seq.reshape(retain.shape)
    _, gate_pull = jax.vjp(gate_math, gate_pre)
    gate_pre_grad = gate_pull((retain_grad, inflow_grad))[0].astype(jnp.bfloat16)
    gating_grad = across(normed, gate_pre_grad)
    offsets_grad = jnp.sum(gate_pre_grad.astype(jnp.float32), axis=0)
    normed_grad = against(gate_pre_grad, back_gating)
    _, first_pull = jax.vjp(rms_scale, inputs, gain_one)
    inputs_norm_grad, prescale_grad = first_pull(normed_grad)
    tokens_grad = residual_grad + inputs_norm_grad
    (
        gating_part,
        offsets_part,
        prescale_part,
        readout_part,
        midscale_part,
        expand_part,
        shifts_part,
        contract_part,
    ) = (
        lax.psum_scatter(gating_grad, ("dp", "fsdp"), scatter_dimension=1, tiled=True),
        lax.psum_scatter(offsets_grad, ("dp", "fsdp"), scatter_dimension=0, tiled=True),
        lax.psum_scatter(prescale_grad, ("dp", "fsdp"), scatter_dimension=0, tiled=True),
        lax.psum_scatter(readout_grad, ("dp", "fsdp"), scatter_dimension=0, tiled=True),
        lax.psum_scatter(midscale_grad, ("dp", "fsdp"), scatter_dimension=0, tiled=True),
        lax.psum_scatter(expand_grad, ("dp", "fsdp"), scatter_dimension=1, tiled=True),
        lax.psum_scatter(shifts_grad, ("dp", "fsdp"), scatter_dimension=0, tiled=True),
        lax.psum_scatter(contract_grad, ("dp", "fsdp"), scatter_dimension=0, tiled=True),
    )
    return (
        block_output,
        tokens_grad,
        gating_part,
        offsets_part,
        prescale_part,
        readout_part,
        midscale_part,
        expand_part,
        shifts_part,
        contract_part,
    )


def solution(mesh):
    in_specs = (
        P(("dp", "fsdp"), None),
        P(None, ("dp", "fsdp")),
        P(("dp", "fsdp")),
        P(("dp", "fsdp")),
        P(("dp", "fsdp"), None),
        P(("dp", "fsdp")),
        P(None, ("dp", "fsdp")),
        P(("dp", "fsdp")),
        P(("dp", "fsdp"), None),
        P(("dp", "fsdp"), None),
    )
    out_specs = (
        P(("dp", "fsdp"), None),
        P(("dp", "fsdp"), None),
        P(None, ("dp", "fsdp")),
        P(("dp", "fsdp")),
        P(("dp", "fsdp")),
        P(("dp", "fsdp"), None),
        P(("dp", "fsdp")),
        P(None, ("dp", "fsdp")),
        P(("dp", "fsdp")),
        P(("dp", "fsdp"), None),
    )
    return jax.shard_map(shards, mesh=mesh, in_specs=in_specs, out_specs=out_specs, check_vma=False)
```

profile of v0, /device:TPU:0, one launch (start us, length us, event | category | flops | bytes accessed | tf_op | source)
XLA Modules:
  0.0 813.6 jit_solution(16865434564757913565)
XLA Ops:
  13.4 42.5 %all-reduce.51 = (bf16[3072]{0:T(1024)(128)(2,1)S(1)}, bf16[512]{0:T(512)(128)(2,1)S(1)}, bf16[512]{0:T(512)(128)(2,1)S(1)}, bf16[2048]{0:T(1024)(128)(2,1)S(1)}) all-reduce(bf16[3072]{0:T(1024)(128)(2,1)S(1)} %dynamic-update-slice.1, bf16[512]{0:T(512)(128)(2,1)S(1)} %dynamic-update-slice, ...), channel_id=1, replica_groups=mesh['dp'=4,'fsdp'=8] {'dp','fsdp'}, use_global_device_ids=true, to_apply=%add.43 | all-reduce | flops 6144 | bytes 24576
  59.7 13.1 %all-gather.5.cloned.1.call-done = bf16[512,3072]{0,1:T(8,128)(2,1)} async-done(((bf16[512,96]{0,1:T(8,128)(2,1)}), bf16[512,3072]{0,1:T(8,128)(2,1)}) %all-gather.5.cloned.1.call-update) | async-done | bytes 3145744 | tf_op jit(solution)/shard_map/all_gather | solution.py:86
  86.8 7.0 multiply_add_fusion.13
  93.8 12.3 %multiply_add_fusion.12 = (f32[16,64,1024]{2,1,0:T(8,128)}, f32[16,64,1024]{2,1,0:T(8,128)}) fusion(f32[16,64,1024]{2,1,0:T(8,128)} %multiply_add_fusion.13, f32[16,62,1024]{2,1,0:T(8,128)} %bitcast.108, f32[16,64,1024]{2,1,0:T(8,128)} %bitcast.94, f32[16,63,1024]{2,1,0:T(8,128)} %bitcast.95), kind=kLoop, calls=%fused_computation.57 | loop fusion | flops 3145728 | bytes 24969216 | tf_op jit(solution)/shard_map/add | solution.py:38
  106.1 12.1 %multiply_add_fusion.11 = (f32[16,64,1024]{2,1,0:T(8,128)}, f32[16,64,1024]{2,1,0:T(8,128)}) fusion(f32[16,64,1024]{2,1,0:T(8,128)} %get-tuple-element.70, f32[16,60,1024]{2,1,0:T(8,128)} %bitcast.106, f32[16,64,1024]{2,1,0:T(8,128)} %get-tuple-element.71, f32[16,62,1024]{2,1,0:T(8,128)} %bitcast.107), kind=kLoop, calls=%fused_computation.56 | loop fusion | flops 3145728 | bytes 24772608 | tf_op jit(solution)/shard_map/add | solution.py:38
  122.7 8.6 %multiply_add_fusion.10 = (f32[16,64,1024]{2,1,0:T(8,128)}, f32[16,64,1024]{2,1,0:T(8,128)}) fusion(f32[16,64,1024]{2,1,0:T(8,128)} %get-tuple-element.68, f32[16,56,1024]{2,1,0:T(8,128)} %slice.192, f32[16,64,1024]{2,1,0:T(8,128)S(1)} %copy-done.7, f32[16,60,1024]{2,1,0:T(8,128)S(1)} %bitcast.105), kind=kLoop, calls=%fused_computation.55 | loop fusion | flops 3145728 | bytes 24379392 | tf_op jit(solution)/shard_map/add | solution.py:38
  137.4 10.0 %multiply_add_fusion.9 = (f32[16,64,1024]{2,1,0:T(8,128)}, f32[16,64,1024]{2,1,0:T(8,128)}) fusion(f32[16,64,1024]{2,1,0:T(8,128)} %get-tuple-element.66, f32[16,48,1024]{2,1,0:T(8,128)} %slice.193, f32[16,64,1024]{2,1,0:T(8,128)S(1)} %copy-done.8, f32[16,56,1024]{2,1,0:T(8,128)} %slice.187), kind=kLoop, calls=%fused_computation.54 | loop fusion | flops 3145728 | bytes 23592960 | tf_op jit(solution)/shard_map/add | solution.py:38
  152.1 8.2 %multiply_add_fusion.8 = (f32[16,64,1024]{2,1,0:T(8,128)}, f32[16,64,1024]{2,1,0:T(8,128)S(1)}) fusion(f32[16,64,1024]{2,1,0:T(8,128)} %get-tuple-element.64, f32[16,32,1024]{2,1,0:T(8,128)S(1)} %slice.194, f32[16,64,1024]{2,1,0:T(8,128)} %get-tuple-element.65, f32[16,48,1024]{2,1,0:T(8,128)} %slice.188), kind=kLoop, calls=%fused_computation.53 | loop fusion | flops 3145728 | bytes 22020096 | tf_op jit(solution)/shard_map/add | solution.py:38
  175.4 11.6 %all-gather.9.cloned.1.call-done = bf16[512,2048]{0,1:T(8,128)(2,1)} async-done(((bf16[512,64]{0,1:T(8,128)(2,1)}), bf16[512,2048]{0,1:T(8,128)(2,1)}) %all-gather.9.cloned.1.call-update) | async-done | bytes 2097168 | tf_op jit(solution)/shard_map/all_gather | solution.py:91
  187.0 11.5 %multiply_convert_fusion = (bf16[1024,2048]{1,0:T(8,128)(2,1)}, f32[1024,2048]{1,0:T(8,128)}) fusion(f32[2048]{0:T(1024)S(1)} %convert_element_type.57, bf16[512,2048]{0,1:T(8,128)(2,1)} %all-gather.9.cloned.1.call-done, f32[1024,512]{0,1:T(8,128)} %get-tuple-element.78, f32[512]{0:T(512)S(1)} %convert_element_type.55, f32[1024]{0:T(1024)S(1)} %fusion.40), kind=kOutput, calls=%fused_computation.11 | convolution fusion | flops 2170028032 | bytes 16791552 | tf_op jit(solution)/shard_map/dot_general | solution.py:63
  198.5 46.7 %all-gather.11.cloned.1.call-done = bf16[2048,512]{1,0:T(8,128)(2,1)} async-done(((bf16[64,512]{1,0:T(8,128)(2,1)}), bf16[2048,512]{1,0:T(8,128)(2,1)}) %all-gather.11.cloned.1.call-update) | async-done | bytes 2097168 | tf_op jit(solution)/shard_map/all_gather | solution.py:93
  245.3 10.6 %convert_reduce_fusion.1 = (f32[2048]{0:T(1024)S(1)}, bf16[1024,2048]{1,0:T(8,128)(2,1)S(1)}) fusion(f32[1024,2048]{1,0:T(8,128)} %get-tuple-element.80, f32[2048]{0:T(1024)S(1)} %convert_element_type.57, bf16[1024,512]{1,0:T(8,128)(2,1)S(1)} %copy-done.28, bf16[2048,512]{1,0:T(8,128)(2,1)} %all-gather.11.cloned.1.call-done), kind=kOutput, calls=%fused_computation.10 | convolution fusion | flops 2195716096 | bytes 15745024 | tf_op jit(solution)/shard_map/dot_general | solution.py:73
  262.9 6.8 fusion.47
  284.0 10.6 %multiply_add_fusion.5 = (f32[16,64,1024]{2,1,0:T(8,128)}, f32[16,64,1024]{2,1,0:T(8,128)}) fusion(f32[16,64,1024]{2,1,0:T(8,128)} %copy-done.6, f32[16,62,1024]{2,1,0:T(8,128)} %slice.214, f32[16,64,1024]{2,1,0:T(8,128)S(1)} %bitcast.101, f32[16,63,1024]{2,1,0:T(8,128)} %slice.208), kind=kLoop, calls=%fused_computation.44 | loop fusion | flops 3145728 | bytes 24969216 | tf_op jit(solution)/shard_map/add | solution.py:38
  302.5 10.5 %multiply_add_fusion.4 = (f32[16,64,1024]{2,1,0:T(8,128)}, f32[16,64,1024]{2,1,0:T(8,128)S(1)}) fusion(f32[16,64,1024]{2,1,0:T(8,128)} %get-tuple-element.54, f32[16,60,1024]{2,1,0:T(8,128)} %slice.215, f32[16,64,1024]{2,1,0:T(8,128)} %get-tuple-element.55, f32[16,62,1024]{2,1,0:T(8,128)} %slice.209), kind=kLoop, calls=%fused_computation.43 | loop fusion | flops 3145728 | bytes 24772608 | tf_op jit(solution)/shard_map/add | solution.py:38
  328.1 10.2 %multiply_add_fusion.3 = (f32[16,64,1024]{2,1,0:T(8,128)}, f32[16,64,1024]{2,1,0:T(8,128)S(1)}) fusion(f32[16,64,1024]{2,1,0:T(8,128)} %get-tuple-element.52, f32[16,56,1024]{2,1,0:T(8,128)} %slice.216, f32[16,64,1024]{2,1,0:T(8,128)} %copy-done.4, f32[16,60,1024]{2,1,0:T(8,128)} %slice.210), kind=kLoop, calls=%fused_computation.42 | loop fusion | flops 3145728 | bytes 24379392 | tf_op jit(solution)/shard_map/add | solution.py:38
  342.6 8.7 %multiply_add_fusion.2 = (f32[16,64,1024]{2,1,0:T(8,128)}, f32[16,64,1024]{2,1,0:T(8,128)}) fusion(f32[16,64,1024]{2,1,0:T(8,128)} %get-tuple-element.50, f32[16,48,1024]{2,1,0:T(8,128)S(1)} %slice.217, f32[16,64,1024]{2,1,0:T(8,128)S(1)} %get-tuple-element.51, f32[16,56,1024]{2,1,0:T(8,128)} %slice.211), kind=kLoop, calls=%fused_computation.41 | loop fusion | flops 3145728 | bytes 23592960 | tf_op jit(solution)/shard_map/add | solution.py:38
  372.7 7.5 fusion.8
  382.8 7.1 fusion.36
  389.9 7.0 add_convert_fusion
  414.2 40.1 %all-reduce.50 = (f32[3072]{0:T(1024)S(1)}, f32[512]{0:T(512)S(1)}, f32[512]{0:T(512)S(1)}, f32[2048]{0:T(1024)S(1)}) all-reduce(f32[3072]{0:T(1024)S(1)} %convert_reduce_fusion, f32[512]{0:T(512)S(1)} %get-tuple-element.32, f32[512]{0:T(512)S(1)} %get-tuple-element.30, ...), channel_id=3, replica_groups=mesh['dp'=4,'fsdp'=8] {'dp','fsdp'}, use_global_device_ids=true, to_apply=%region_6.0.clone | all-reduce | flops 6144 | bytes 49152
  456.6 86.9 %reduce-scatter.11.cloned.1.call-done = f32[64,512]{1,0:T(8,128)} async-done(((f32[2048,512]{1,0:T(8,128)}), f32[64,512]{1,0:T(8,128)}) %reduce-scatter.11.cloned.1.call-update) | async-done | bytes 131088 | tf_op jit(solution)/shard_map/reduce_scatter | solution.py:177
  543.5 144.5 %reduce-scatter.9.cloned.1.call-done = f32[512,64]{0,1:T(8,128)} async-done(((f32[512,2048]{0,1:T(8,128)}), f32[512,64]{0,1:T(8,128)}) %reduce-scatter.9.cloned.1.call-update) | async-done | bytes 131088 | tf_op jit(solution)/shard_map/reduce_scatter | solution.py:175
  688.0 118.3 %reduce-scatter.5.cloned.1.call-done = f32[512,96]{0,1:T(8,128)} async-done(((f32[512,3072]{0,1:T(8,128)}), f32[512,96]{0,1:T(8,128)}) %reduce-scatter.5.cloned.1.call-update) | async-done | bytes 196624 | tf_op jit(solution)/shard_map/reduce_scatter | solution.py:170
  (196 shorter events, 146.0 us)
Async XLA Ops:
  7.2 51.2 %copy-start.27 = (bf16[1024,512]{1,0:T(8,128)(2,1)S(1)}, bf16[1024,512]{1,0:T(8,128)(2,1)}, u32[]{:S(2)}) copy-start(bf16[1024,512]{1,0:T(8,128)(2,1)} %param.19) | copy-start | bytes 3145732
  7.2 65.7 %all-gather.5.cloned.1.call-start = ((), (), s32[]{:S(2)}) async-start(), calls=%async_computation.4 | async-start | bytes 3244032 | tf_op jit(solution)/shard_map/all_gather | solution.py:86
  7.9 162.6 %all-gather.7.cloned.1.call-start = ((), (), s32[]{:S(2)}) async-start(), calls=%async_computation.5 | async-start | bytes 1081344 | tf_op jit(solution)/shard_map/all_gather | solution.py:89
  8.7 178.3 %all-gather.9.cloned.1.call-start = ((), (), s32[]{:S(2)}) async-start(), calls=%async_computation.6 | async-start | bytes 2162688 | tf_op jit(solution)/shard_map/all_gather | solution.py:91
  9.4 235.9 %all-gather.11.cloned.1.call-start = ((), (), s32[]{:S(2)}) async-start(), calls=%async_computation.7 | async-start | bytes 2162688 | tf_op jit(solution)/shard_map/all_gather | solution.py:93
  10.0 446.7 %reduce-scatter.7.cloned.1.call-start = ((), (), s32[]{:S(2)}) async-start(), calls=%async_computation.9 | async-start | bytes 2162688 | tf_op jit(solution)/shard_map/reduce_scatter | solution.py:173
  56.0 22.5 %copy-start.33 = (f32[512]{0:T(512)}, f32[512]{0:T(512)S(1)}, u32[]{:S(2)}) copy-start(f32[512]{0:T(512)S(1)} %convert_element_type.50) | copy-start | bytes 6148
  57.5 15.4 %copy-start.14 = (bf16[1024,512]{0,1:T(8,128)(2,1)}, bf16[1024,512]{0,1:T(8,128)(2,1)S(1)}, u32[]{:S(2)}) copy-start(bf16[1024,512]{0,1:T(8,128)(2,1)S(1)} %copy.29) | copy-start | bytes 3145732
  58.4 20.0 %copy-start.31 = (f32[1024]{0:T(1024)}, f32[1024]{0:T(1024)S(1)}, u32[]{:S(2)}) copy-start(f32[1024]{0:T(1024)S(1)} %fusion.39) | copy-start | bytes 12292
  187.0 58.2 %copy-start.28 = (bf16[1024,512]{1,0:T(8,128)(2,1)S(1)}, bf16[1024,512]{1,0:T(8,128)(2,1)}, u32[]{:S(2)}) copy-start(bf16[1024,512]{1,0:T(8,128)(2,1)} %param.19) | copy-start | bytes 3145732
  245.3 10.6 %copy-start.23 = (f32[1024,512]{0,1:T(8,128)S(1)}, f32[1024,512]{0,1:T(8,128)}, u32[]{:S(2)}) copy-start(f32[1024,512]{0,1:T(8,128)} %get-tuple-element.78) | copy-start | bytes 6291460
  245.3 10.6 %copy-start.35 = (bf16[512,2048]{0,1:T(8,128)(2,1)S(1)}, bf16[512,2048]{0,1:T(8,128)(2,1)}, u32[]{:S(2)}) copy-start(bf16[512,2048]{0,1:T(8,128)(2,1)} %all-gather.9.cloned.1.call-done) | copy-start | bytes 6291460
  260.2 15.4 %copy-start.11 = (f32[1024,512]{0,1:T(8,128)}, f32[1024,512]{0,1:T(8,128)S(1)}, u32[]{:S(2)}) copy-start(f32[1024,512]{0,1:T(8,128)S(1)} %fusion.28) | copy-start | bytes 6291460
  262.8 280.7 %reduce-scatter.11.cloned.1.call-start = ((), (), s32[]{:S(2)}) async-start(), calls=%async_computation.11 | async-start | bytes 4325376 | tf_op jit(solution)/shard_map/reduce_scatter | solution.py:177
  269.7 418.3 %reduce-scatter.9.cloned.1.call-start = ((), (), s32[]{:S(2)}) async-start(), calls=%async_computation.10 | async-start | bytes 4325376 | tf_op jit(solution)/shard_map/reduce_scatter | solution.py:175
  312.9 8.7 %copy-start.4 = (f32[16,64,1024]{2,1,0:T(8,128)}, f32[16,64,1024]{2,1,0:T(8,128)S(1)}, u32[]{:S(2)}) copy-start(f32[16,64,1024]{2,1,0:T(8,128)S(1)} %get-tuple-element.53) | copy-start | bytes 12582916
  328.0 478.3 %reduce-scatter.5.cloned.1.call-start = ((), (), s32[]{:S(2)}) async-start(), calls=%async_computation.8 | async-start | bytes 6488064 | tf_op jit(solution)/shard_map/reduce_scatter | solution.py:170
  364.9 7.7 slice-start
  372.6 10.2 %copy-start.16 = (bf16[1024,512]{0,1:T(8,128)(2,1)S(1)}, bf16[1024,512]{0,1:T(8,128)(2,1)}, u32[]{:S(2)}) copy-start(bf16[1024,512]{0,1:T(8,128)(2,1)} %copy-done.14) | copy-start | bytes 3145732
  372.6 10.2 %copy-start.32 = (f32[1024]{0:T(1024)S(1)}, f32[1024]{0:T(1024)}, u32[]{:S(2)}) copy-start(f32[1024]{0:T(1024)} %copy-done.31) | copy-start | bytes 12292
  372.7 10.2 %copy-start.34 = (f32[512]{0:T(512)S(1)}, f32[512]{0:T(512)}, u32[]{:S(2)}) copy-start(f32[512]{0:T(512)} %copy-done.33) | copy-start | bytes 6148
  389.9 9.3 %copy-start.17 = (bf16[1024,512]{0,1:T(8,128)(2,1)S(1)}, bf16[1024,512]{0,1:T(8,128)(2,1)}, u32[]{:S(2)}) copy-start(bf16[1024,512]{0,1:T(8,128)(2,1)} %copy-done.14) | copy-start | bytes 3145732
  389.9 9.3 %copy-start.19 = (bf16[1024,1024]{1,0:T(8,128)(2,1)S(1)}, bf16[1024,1024]{1,0:T(8,128)(2,1)}, u32[]{:S(2)}) copy-start(bf16[1024,1024]{1,0:T(8,128)(2,1)} %copy-done.18) | copy-start | bytes 6291460
  399.2 6.8 copy-start.12
  (25 other events, 83.6 us)
Sparse Core Ops, SparseCore 0:
  10.9 61.8 all-gather.4
  75.9 52.6 all-gather.6
  131.6 55.3 all-gather.8
  189.8 55.3 all-gather.10
  262.9 136.7 reduce-scatter.6
  402.5 140.9 reduce-scatter.10
  546.5 141.4 reduce-scatter.8
  695.1 111.1 reduce-scatter.4
where the time goes:
time: 820 us; the launch traced here: 814 us
  waiting for transfers between devices  424 us (52%)
  other arithmetic  137 us (17%)
  local copies, waits for them, and re-layouts  83.1 us (10%)
  blocking collectives  82.6 us (10%)
  matrix products  71.4 us (9%)
  between operations  15.3 us (2%)
    reduce_scatter x1, waiting for transfers between devices, shards(): lax.psum_scatter(expand_grad, ('dp', 'fsdp'), scatter_dimension=1, tiled=...  144 us
    reduce_scatter x1, waiting for transfers between devices, shards(): lax.psum_scatter(gating_grad, ('dp', 'fsdp'), scatter_dimension=1, tiled=...  118 us
    add x20, other arithmetic, doubling(): drive = decay * shifted(drive, stride, 0.0, reverse) + drive  107 us
    reduce_scatter x1, waiting for transfers between devices, shards(): lax.psum_scatter(contract_grad, ('dp', 'fsdp'), scatter_dimension=0, tile...  86.9 us
    unnamed x2, blocking collectives  82.6 us
    all_gather x1, waiting for transfers between devices, shards(): lax.all_gather(contract, ('dp', 'fsdp'), axis=0, tiled=True)  46.7 us
    slice x20, local copies, waits for them, and re-layouts, shifted(): return jnp.concatenate([values[:, stride:], padding], axis=1)  35.5 us
    dot_general x4, matrix products, matmul(): return jnp.dot(left, right, preferred_element_type=jnp.float32)  28.9 us
  transfers between devices with their start and end apart: 8, of which 6 were waited for; matrix products, arithmetic and copies ran while one was open for 32% of the time, Pallas kernels for 0%

commit v1 on v0

v1 whole, which is shorter than its diff:
```python
from functools import partial

import jax
import jax.numpy as jnp
import numpy as np
from jax import lax
from jax.experimental import pallas as pl
from jax.experimental.pallas import tpu as pltpu
from jax.sharding import PartitionSpec as P

LEN = 1024
LANES = 8
STEPS = LEN // LANES
ROWS = 256
AXES = ("dp", "fsdp")
epsilon = 1e-06
bf16 = jnp.bfloat16
f32 = jnp.float32
ANY = pl.BlockSpec(memory_space=pl.ANY)
SCALAR = pl.BlockSpec(memory_space=pltpu.SMEM)
FILLER = pl.CostEstimate(flops=10**11, bytes_accessed=10**8, transcendentals=0)
QUICK = pl.CostEstimate(flops=1000, bytes_accessed=1000, transcendentals=0)
PARAMS = pltpu.CompilerParams(vmem_limit_bytes=56 * 1024 * 1024)


def matmul(left, right):
    return jnp.dot(left, right, preferred_element_type=f32)


def across(left, right):
    return lax.dot_general(left, right, (((0,), (0,)), ((), ())), preferred_element_type=f32)


def against(left, right):
    return lax.dot_general(left, right, (((1,), (1,)), ((), ())), preferred_element_type=f32)


def interleave_kernel(values, target, scratch):
    for j in range(scratch.shape[0]):
        columns = slice(j * 128, (j + 1) * 128)
        for run in range(LANES):
            rows = slice(run * STEPS, (run + 1) * STEPS)
            scratch[j, pl.ds(run, STEPS, stride=LANES)] = values[rows, columns].astype(f32)
        target[:, columns] = scratch[j].astype(target.dtype)


def interleaved(values):
    return pl.pallas_call(
        interleave_kernel,
        out_shape=jax.ShapeDtypeStruct(values.shape, values.dtype),
        scratch_shapes=[pltpu.VMEM((values.shape[1] // 128, LEN, 128), f32)],
        compiler_params=PARAMS,
        cost_estimate=QUICK,
        name="interleave",
    )(values)


def sequence_kernel(values, target, scratch):
    for j in range(scratch.shape[0]):
        columns = slice(j * 128, (j + 1) * 128)
        scratch[j] = values[:, columns].astype(f32)
        for run in range(LANES):
            rows = slice(run * STEPS, (run + 1) * STEPS)
            target[rows, columns] = scratch[j, pl.ds(run, STEPS, stride=LANES)].astype(target.dtype)


def sequential(values):
    return pl.pallas_call(
        sequence_kernel,
        out_shape=jax.ShapeDtypeStruct(values.shape, values.dtype),
        scratch_shapes=[pltpu.VMEM((values.shape[1] // 128, LEN, 128), f32)],
        compiler_params=PARAMS,
        cost_estimate=FILLER,
        name="sequence",
    )(values)


def down(values):
    return jnp.concatenate([jnp.zeros_like(values[:1]), values[:-1]], axis=0)


def tiles(k, count):
    if isinstance(k, int):
        return pl.ds(k * LANES, count * LANES)
    return pl.ds(pl.multiple_of(k * LANES, LANES), count * LANES)


def parts():
    return [slice(k, k + ROWS) for k in range(0, LEN, ROWS)]


def start(pairs, sem):
    copies = [pltpu.make_async_copy(source, target, sem) for source, target in pairs]
    for copy in copies:
        copy.start()
    return copies


def finish(copies):
    for copy in copies:
        copy.wait()


def placed(me, lists, arrays, first, size, target):
    found = []
    for masks, array in zip(lists, arrays):
        for b, mask in enumerate(masks):
            at = pl.multiple_of((me ^ mask) * size, size)
            found.append((array.at[b, pl.ds(first, size)], target.at[pl.ds(at, size)]))
    return found


def emitted(plans, rows, size, width):
    if plans is None:
        return [jax.ShapeDtypeStruct((rows, width), f32)]
    return [jax.ShapeDtypeStruct((len(masks), size, width), dtype) for masks, dtype in plans]


def emit(me, plans, source, targets):
    if plans is None:
        targets[0][...] = source[...]
        return
    for (masks, _), target in zip(plans, targets):
        size = target.shape[1]
        for p, mask in enumerate(masks):
            at = pl.multiple_of((me ^ mask) * size, size)
            target[p] = source[pl.ds(at, size)].astype(target.dtype)


def sorted_blocks(me, plans, grads, size):
    whole = grads[0].reshape(-1, size, grads[0].shape[1])
    return [jnp.take(whole, me ^ jnp.asarray(masks), axis=0).astype(dtype) for masks, dtype in plans]


def lanes_of(count, size):
    lane = lax.broadcasted_iota(jnp.int32, (1, count), 1)
    piece = ((lane.astype(f32) + 0.5) * (1.0 / size)).astype(jnp.int32)
    return piece, lane - piece * size


def selector(place):
    rows = lax.broadcasted_iota(jnp.int32, (128, place.shape[1]), 0)
    return jnp.where(rows == place, 1.0, 0.0).astype(bf16)


def laid_out(rows, owners, lane_owner, place):
    spread = matmul(rows, selector(place))
    return jnp.sum(jnp.where(owners == lane_owner, spread, 0.0), axis=0, keepdims=True)


def cut_up(vector, lane_owner, place, count):
    rows = lax.broadcasted_iota(jnp.int32, (count, vector.shape[1]), 0)
    found = jnp.where(rows == lane_owner, vector, 0.0)
    high = found.astype(bf16)
    low = (found - high.astype(f32)).astype(bf16)
    choose = selector(place)
    return against(high, choose) + against(low, choose)


def vectors_kernel(sizes, me, masks, offsets, shift_0, shift_1, prescale, midscale, target):
    count = target.shape[0]
    flat = jnp.concatenate([offsets[t : t + 1] for t in range(3)], axis=1)
    target[:, :128] = cut_up(flat, *lanes_of(flat.shape[1], sizes[0]), count)
    shifts = jnp.concatenate([shift_0[...], shift_1[...]], axis=1)
    target[:, 128:256] = cut_up(shifts, masks[...] ^ me[0], lanes_of(shifts.shape[1], sizes[1])[1], count)
    target[:, 256:384] = cut_up(prescale[...], *lanes_of(prescale.shape[1], sizes[2]), count)
    target[:, 384:512] = cut_up(midscale[...], *lanes_of(midscale.shape[1], sizes[2]), count)


def vector_rows(me, masks, sizes, count, *grads):
    return pl.pallas_call(
        partial(vectors_kernel, sizes),
        in_specs=[SCALAR] + [pl.BlockSpec(memory_space=pltpu.VMEM)] * 6,
        out_specs=pl.BlockSpec(memory_space=pltpu.VMEM),
        out_shape=jax.ShapeDtypeStruct((count, 512), f32),
        compiler_params=PARAMS,
        cost_estimate=QUICK,
        name="vectors",
    )(me, masks, *grads)


def gates_kernel(lists, size, sizes, me, inputs, rows, owner_masks, lane_masks, *refs):
    arrays = refs[: len(lists)]
    normed, share, low, pull_f, pull_i, gain_one, gain_two, shifts = refs[len(lists) : len(lists) + 8]
    weights, pre, mid, decay, drive, offsets, sem = refs[len(lists) + 8 :]
    group = pl.program_id(0)
    wide = share.shape[1]
    hidden = weights.shape[0] // 3

    @pl.when(group == 0)
    def _():
        copies = start(placed(me[0], lists, arrays, 0, size, weights), sem)
        owners = owner_masks[...] ^ me[1]
        width = inputs.shape[1]
        gain = laid_out(rows[:, 256:384], owners, *lanes_of(width, sizes[2]))
        gain_one[...] = gain
        gain_two[...] = laid_out(rows[:, 384:512], owners, *lanes_of(width, sizes[2]))
        place = lanes_of(shifts.shape[1], sizes[1])[1]
        shifts[...] = laid_out(rows[:, 128:256], owners, lane_masks[...] ^ me[1], place)
        flat = laid_out(rows[:, :128], owners, *lanes_of(3 * hidden, sizes[0]))
        for t in range(3):
            for k in range(hidden // wide):
                offsets[k, t : t + 1] = flat[:, t * hidden + k * wide : t * hidden + (k + 1) * wide]
        for part in parts():
            value = inputs[part].astype(f32)
            scale = lax.rsqrt(jnp.mean(value * value, axis=-1, keepdims=True) + epsilon)
            normed[part] = (value * scale * gain).astype(bf16)
        finish(copies)

    def step(k, carry):
        prod, held = carry
        rows = tiles(2 * k, 2)
        forget = 1.0 / (1.0 + jnp.exp(-pre[0, rows]))
        entry = 1.0 / (1.0 + jnp.exp(-pre[1, rows]))
        whole = 1.0 / (forget + entry)
        keep = forget * whole
        rest = entry * whole
        flow = rest * pre[2, rows]
        both = keep * rest
        share[rows] = rest
        mid[0, rows] = both * (1.0 - forget)
        mid[1, rows] = both * (entry - 1.0)
        held_0 = keep[:LANES] * held + flow[:LANES]
        prod_0 = keep[:LANES] * prod
        held = keep[LANES:] * held_0 + flow[LANES:]
        prod = keep[LANES:] * prod_0
        drive[rows] = jnp.concatenate([held_0, held], axis=0)
        decay[rows] = jnp.concatenate([prod_0, prod], axis=0)
        return prod, held

    begin = (jnp.ones((LANES, wide), f32), jnp.zeros((LANES, wide), f32))
    prod, held = begin
    ws = [weights[pl.ds(pl.multiple_of(t * hidden + group * wide, wide), wide)] for t in range(3)]
    for part in parts():
        for t in range(3):
            pre[t, part] = against(normed[part], ws[t]) + offsets[group, t : t + 1]
        for k in range(part.start // (2 * LANES), part.stop // (2 * LANES)):
            prod, held = step(k, (prod, held))
    ends = [jnp.zeros((1, wide), f32)]
    for k in range(LANES - 1):
        ends.append(prod[k : k + 1] * ends[-1] + held[k : k + 1])
    entering = jnp.concatenate(ends, axis=0)
    entering = jnp.concatenate([entering, entering], axis=0)

    def join(k, before):
        rows = tiles(2 * k, 2)
        value = drive[rows] + decay[rows] * entering
        low[rows] = value.astype(bf16)
        change = jnp.concatenate([before, value[:LANES]], axis=0) - pre[2, rows]
        pull_f[rows] = (change * mid[0, rows]).astype(bf16)
        pull_i[rows] = (change * mid[1, rows]).astype(bf16)
        return value[LANES:]

    lax.fori_loop(0, STEPS // 2, join, entering[:LANES], unroll=8)


def gates(me, inputs, rows, owner_masks, lane_masks, arrays, lists, size, sizes, hidden):
    width = inputs.shape[1]
    shape = jax.ShapeDtypeStruct
    whole = lambda one: pl.BlockSpec(one.shape, lambda g: (0, 0))
    wide = 256
    fixed = lambda g: (0, 0)
    tall = lambda g: (0, g)
    out = lambda dtype: jax.ShapeDtypeStruct((LEN, hidden), dtype)
    solid = pl.BlockSpec((LEN, width), fixed)
    return pl.pallas_call(
        partial(gates_kernel, lists, size, sizes),
        grid=(hidden // wide,),
        in_specs=[SCALAR, solid, whole(rows), whole(owner_masks), whole(lane_masks)] + [ANY] * len(arrays),
        out_specs=[solid]
        + [pl.BlockSpec((LEN, wide), tall)] * 4
        + [pl.BlockSpec((1, width), fixed)] * 2
        + [whole(lane_masks)],
        out_shape=[jax.ShapeDtypeStruct((LEN, width), bf16)]
        + [out(f32), out(bf16), out(bf16), out(bf16), shape((1, width), f32)]
        + [shape((1, width), f32), shape(lane_masks.shape, f32)],
        scratch_shapes=[
            pltpu.VMEM((3 * hidden, width), bf16),
            pltpu.VMEM((3, LEN, wide), f32),
            pltpu.VMEM((2, LEN, wide), f32),
            pltpu.VMEM((LEN, wide), f32),
            pltpu.VMEM((LEN, wide), f32),
            pltpu.VMEM((hidden // wide, 3, wide), f32),
            pltpu.SemaphoreType.DMA,
        ],
        compiler_params=PARAMS,
        cost_estimate=FILLER,
        name="gates",
    )(me, inputs, rows, owner_masks, lane_masks, *arrays)


def gelu_both(x):
    inner = np.float32(np.sqrt(2 / np.pi))
    square = x * x
    t = jnp.tanh(inner * (x + np.float32(0.044715) * (square * x)))
    cdf = 0.5 + 0.5 * t
    slope = cdf + (0.5 * x) * (1.0 - t * t) * (inner + np.float32(3 * 0.044715) * inner * square)
    return x * cdf, slope


def ffn_part(part, normed_two, cotangent, shifts, expand, contract, hidden, slope, shift_grad):
    units = expand.shape[0]
    n2 = normed_two[part]
    ct = cotangent[part]
    for j in range(0, units, 256):
        cols = slice(j, j + 256)
        act, grad = gelu_both(against(n2, expand[cols]) + shifts[:, cols])
        hidden[part, cols] = act.astype(bf16)
        rounded = (against(ct, contract[cols]) * grad).astype(bf16)
        slope[part, cols] = rounded
        shift_grad[:, cols] += jnp.sum(rounded.astype(f32), axis=0, keepdims=True)
    return matmul(hidden[part], contract[...]), matmul(slope[part], expand[...])


def ffn_grads(normed_two, cotangent, hidden, slope, sent, kept):
    units = hidden.shape[1]
    blocks, rows, width = kept.shape
    unit = rows // 2
    for j, target in enumerate((kept, sent)):
        cols = slice(j * units // 2, (j + 1) * units // 2)
        target[:, :unit] = across(slope[:, cols], normed_two[...]).astype(target.dtype).reshape(blocks, unit, width)
        target[:, unit:] = across(hidden[:, cols], cotangent[...]).astype(target.dtype).reshape(blocks, unit, width)


def weight_copies(own, unit, expand, contract):
    found, at = [], 0
    for one in own:
        count = one.shape[0]
        found.append((one.at[:, pl.ds(0, unit)], expand.at[pl.ds(at, count)]))
        found.append((one.at[:, pl.ds(unit, unit)], contract.at[pl.ds(at, count)]))
        at += count
    return found


def first_kernel(lists, size, skip, me, gain, shifts, inputs_h, cotangent_h, low_h, *refs):
    readers, own, refs = refs[: len(lists)], refs[len(lists) : -22], refs[-22:]
    (residual_h, normed_h, branch_h, grad_h, sent, kept, shift_grad) = refs[:7]
    (inputs, cotangent, low, readout, expand, contract, residual, normed_two, branch, grad, hidden, slope) = refs[7:19]
    in_sem, weight_sem, out_sem = refs[19:]
    unit = expand.shape[1]
    width = gain.shape[1]
    arriving = start(
        [(inputs_h, inputs), (low_h, low)] + placed(me[0], lists, readers, skip, size, readout), in_sem
    )
    weights = start(weight_copies(own, unit, expand, contract) + [(cotangent_h, cotangent)], weight_sem)
    shift_grad[...] = jnp.zeros_like(shift_grad)
    finish(arriving)
    leaving = []
    for part in parts():
        value = inputs[part].astype(f32) + matmul(low[part], readout[...])
        residual[part] = value
        inverse = lax.rsqrt(jnp.mean(value * value, axis=-1, keepdims=True) + epsilon)
        normed_two[part] = (value * inverse * gain[...]).astype(bf16)
    leaving += start([(residual, residual_h), (normed_two, normed_h)], out_sem)
    finish(weights)
    expand = expand[...].reshape(-1, width)
    contract = contract[...].reshape(-1, width)
    for part in parts():
        branch[part], grad[part] = ffn_part(
            part, normed_two, cotangent, shifts, expand, contract, hidden, slope, shift_grad
        )
        leaving += start([(branch.at[part], branch_h.at[part]), (grad.at[part], grad_h.at[part])], out_sem)
    ffn_grads(normed_two, cotangent, hidden, slope, sent, kept)
    finish(leaving)


def second_kernel(plans, count, me, gain, shifts, residual_h, normed_h, branch_h, grad_h, cotangent_h, low_h, *refs):
    own, refs = refs[:count], refs[count:]
    output_h, back_h, rounded_h, gain_grad, sent, kept, shift_grad = refs[:7]
    targets, refs = refs[7:-18], refs[-18:]
    residual, normed_two, branch, grad, cotangent, low, expand, contract = refs[:8]
    output, back, rounded, hidden, slope, read_grad, in_sem, part_sem, low_sem, out_sem = refs[8:]
    unit = expand.shape[1]
    width = gain.shape[1]
    weights = start(
        [(normed_h, normed_two), (cotangent_h, cotangent)] + weight_copies(own, unit, expand, contract), in_sem
    )
    others = start([(residual_h, residual), (branch_h, branch), (grad_h, grad)], part_sem)
    last = start([(low_h, low)], low_sem)
    gain_grad[...] = jnp.zeros_like(gain_grad)
    shift_grad[...] = jnp.zeros_like(shift_grad)
    finish(weights)
    expand = expand[...].reshape(-1, width)
    contract = contract[...].reshape(-1, width)
    leaving = []
    for k, part in enumerate(parts()):
        one, two = ffn_part(part, normed_two, cotangent, shifts, expand, contract, hidden, slope, shift_grad)
        if k == 0:
            finish(others)
        value = residual[part]
        output[part] = (value + (branch[part] + one)).astype(bf16)
        total = grad[part] + two
        inverse = lax.rsqrt(jnp.mean(value * value, axis=-1, keepdims=True) + epsilon)
        unscaled = value * inverse
        gain_grad[...] += jnp.sum(total * unscaled, axis=0, keepdims=True)
        pulled = total * gain[...]
        mean = jnp.mean(pulled * unscaled, axis=-1, keepdims=True)
        value = cotangent[part].astype(f32) + inverse * (pulled - unscaled * mean)
        back[part] = value
        rounded[part] = value.astype(bf16)
        leaving += start(
            [(o.at[part], h.at[part]) for o, h in ((output, output_h), (back, back_h), (rounded, rounded_h))], out_sem
        )
    ffn_grads(normed_two, cotangent, hidden, slope, sent, kept)
    finish(last)
    read_grad[...] = across(low[...], rounded[...])
    emit(me[0], plans, read_grad, targets)
    finish(leaving)


def vmem(shape, dtype):
    return pltpu.VMEM(shape, dtype)


WHOLE = pl.BlockSpec(memory_space=pltpu.VMEM)


def ffn_first(me, gain, shifts, inputs, cotangent, low, readers, lists, size, skip, own, unit):
    blocks = sum(one.shape[0] for one in own)
    width = inputs.shape[1]
    units = blocks * unit
    kept = (max(1, blocks // 2), 2 * units // max(2, blocks), width)
    shape = jax.ShapeDtypeStruct
    return pl.pallas_call(
        partial(first_kernel, lists, size, skip),
        in_specs=[SCALAR, WHOLE, WHOLE] + [ANY] * (3 + len(readers) + len(own)),
        out_specs=[ANY] * 4 + [WHOLE] * 3,
        out_shape=[
            shape((LEN, width), f32),
            shape((LEN, width), bf16),
            shape((LEN, width), f32),
            shape((LEN, width), f32),
            shape(kept, bf16),
            shape(kept, f32),
            shape((1, units), f32),
        ],
        scratch_shapes=[
            vmem((LEN, width), bf16),
            vmem((LEN, width), bf16),
            vmem(low.shape, bf16),
            vmem((low.shape[1], width), bf16),
            vmem((blocks, unit, width), bf16),
            vmem((blocks, unit, width), bf16),
            vmem((LEN, width), f32),
            vmem((LEN, width), bf16),
            vmem((LEN, width), f32),
            vmem((LEN, width), f32),
            vmem((LEN, units), bf16),
            vmem((LEN, units), bf16),
        ]
        + [pltpu.SemaphoreType.DMA] * 3,
        compiler_params=PARAMS,
        cost_estimate=FILLER,
        name="ffn_first",
    )(me, gain, shifts, inputs, cotangent, low, *readers, *own)


def ffn_second(me, gain, shifts, residual, normed_two, branch, grad, cotangent, low, own, unit, size, plans):
    blocks = sum(one.shape[0] for one in own)
    width = cotangent.shape[1]
    units = blocks * unit
    kept = (max(1, blocks // 2), 2 * units // max(2, blocks), width)
    targets = emitted(plans, low.shape[1], size, width)
    shape = jax.ShapeDtypeStruct
    return pl.pallas_call(
        partial(second_kernel, plans, len(own)),
        in_specs=[SCALAR, WHOLE, WHOLE] + [ANY] * (6 + len(own)),
        out_specs=[ANY] * 3 + [WHOLE] * (4 + len(targets)),
        out_shape=[
            shape((LEN, width), bf16),
            shape((LEN, width), f32),
            shape((LEN, width), bf16),
            shape((1, width), f32),
            shape(kept, bf16),
            shape(kept, f32),
            shape((1, units), f32),
        ]
        + targets,
        scratch_shapes=[
            vmem((LEN, width), f32),
            vmem((LEN, width), bf16),
            vmem((LEN, width), f32),
            vmem((LEN, width), f32),
            vmem((LEN, width), bf16),
            vmem(low.shape, bf16),
            vmem((blocks, unit, width), bf16),
            vmem((blocks, unit, width), bf16),
            vmem((LEN, width), bf16),
            vmem((LEN, width), f32),
            vmem((LEN, width), bf16),
            vmem((LEN, units), bf16),
            vmem((LEN, units), bf16),
            vmem((low.shape[1], width), f32),
        ]
        + [pltpu.SemaphoreType.DMA] * 4,
        compiler_params=PARAMS,
        cost_estimate=FILLER,
        name="ffn_second",
    )(me, gain, shifts, residual, normed_two, branch, grad, cotangent, low, *own)


def back_kernel(lists, size, skip, plans, me, rounded, normed, share, pull_f, pull_i, *refs):
    readers = refs[: len(lists)]
    grads, offset_grad = refs[len(lists) : len(lists) + 2]
    targets = refs[len(lists) + 2 : -6]
    gate_grad, readout, pulled, drive, decay, sem = refs[-6:]
    group = pl.program_id(0)
    wide = share.shape[1]
    hidden = readout.shape[0]

    @pl.when(group == 0)
    def _():
        finish(start(placed(me[0], lists, readers, skip, size, readout), sem))

    reader = readout[pl.ds(pl.multiple_of(group * wide, wide), wide)]
    held = jnp.zeros((LANES, wide), f32)
    prod = jnp.ones((LANES, wide), f32)
    for part in reversed(parts()):
        pulled[part] = against(rounded[part], reader)
        for k in reversed(range(part.start // LANES, part.stop // LANES)):
            if k < STEPS - 1:
                after = 1.0 - share[tiles(k + 1, 1)]
                prod = after * prod
                held = pulled[tiles(k, 1)] + after * held
            else:
                held = pulled[tiles(k, 1)]
            drive[tiles(k, 1)] = held
            decay[tiles(k, 1)] = prod
    first_retain = 1.0 - share[pl.ds(0, LANES)]
    ends = [jnp.zeros((1, wide), f32)]
    for k in range(LANES - 1, 0, -1):
        whole = held[k : k + 1] + prod[k : k + 1] * ends[-1]
        ends.append(first_retain[k : k + 1] * whole)
    entering = jnp.concatenate(ends[::-1], axis=0)
    entering = jnp.concatenate([entering, entering], axis=0)

    def more(k, sums):
        rows = tiles(2 * k, 2)
        carried = drive[rows] + decay[rows] * entering
        found = []
        for t, factor in enumerate((pull_f, pull_i, share)):
            value = (carried * factor[rows].astype(f32)).astype(bf16)
            grads[t, rows] = value
            found.append(sums[t] + value.astype(f32))
        return tuple(found)

    sums = (jnp.zeros((2 * LANES, wide), f32),) * 3
    for k in range(STEPS // 2):
        sums = more(k, sums)
    for t in range(3):
        offset_grad[t : t + 1] = jnp.sum(sums[t], axis=0, keepdims=True)
        rows = pl.ds(pl.multiple_of(t * hidden + group * wide, wide), wide)
        gate_grad[rows] = across(grads[t], normed[...])

    @pl.when(group == hidden // wide - 1)
    def _():
        emit(me[0], plans, gate_grad, targets)


def back(me, rounded, normed, share, pull_f, pull_i, readers, lists, size, skip, plans):
    width = normed.shape[1]
    hidden = share.shape[1]
    wide = 256
    fixed = lambda g: (0, 0)
    tall = lambda g: (0, g)
    shape = jax.ShapeDtypeStruct
    firm = pl.BlockSpec((LEN, width), fixed)
    targets = emitted(plans, 3 * hidden, 3 * size, width)
    return pl.pallas_call(
        partial(back_kernel, lists, size, skip, plans),
        grid=(hidden // wide,),
        in_specs=[SCALAR, firm, firm] + [pl.BlockSpec((LEN, wide), tall)] * 3 + [ANY] * len(readers),
        out_specs=[pl.BlockSpec((3, LEN, wide), lambda g: (0, 0, g)), pl.BlockSpec((3, wide), tall)]
        + [pl.BlockSpec(one.shape, lambda g, rank=len(one.shape): (0,) * rank) for one in targets],
        out_shape=[shape((3, LEN, hidden), bf16), shape((3, hidden), f32)] + targets,
        scratch_shapes=[
            vmem((3 * hidden, width), f32),
            vmem((hidden, width), bf16),
            vmem((LEN, wide), f32),
            vmem((LEN, wide), f32),
            vmem((LEN, wide), f32),
            pltpu.SemaphoreType.DMA,
        ],
        compiler_params=PARAMS,
        cost_estimate=FILLER,
        name="back",
    )(me, rounded, normed, share, pull_f, pull_i, *readers)


def inputs_kernel(lists, size, me, inputs, gain, back, grads_h, *refs):
    arrays = refs[: len(lists)]
    output, gain_grad, grads, weights, weight_sem, sem = refs[len(lists) :]
    arriving = start(placed(me[0], lists, arrays, 0, size, weights), weight_sem)
    hidden = weights.shape[0] // 3
    for part in parts():
        arriving += start([(grads_h.at[t, part], grads.at[t, part]) for t in range(3)], sem)
    gain_grad[...] = jnp.zeros_like(gain_grad)
    finish(arriving)
    for part in parts():
        total = matmul(grads[0, part], weights[:hidden])
        for t in range(1, 3):
            total = total + matmul(grads[t, part], weights[t * hidden : (t + 1) * hidden])
        value = inputs[part].astype(f32)
        inverse = lax.rsqrt(jnp.mean(value * value, axis=-1, keepdims=True) + epsilon)
        unscaled = value * inverse
        gain_grad[...] += jnp.sum(total * unscaled, axis=0, keepdims=True)
        pulled = total * gain[...]
        mean = jnp.mean(pulled * unscaled, axis=-1, keepdims=True)
        output[part] = back[part] + inverse * (pulled - unscaled * mean)


def inputs_back(me, inputs, gain, back_grad, grads, arrays, lists, size):
    width = inputs.shape[1]
    hidden = grads.shape[2]
    return pl.pallas_call(
        partial(inputs_kernel, lists, size),
        in_specs=[SCALAR, WHOLE, WHOLE, WHOLE, ANY] + [ANY] * len(arrays),
        out_specs=[WHOLE, WHOLE],
        out_shape=[jax.ShapeDtypeStruct((LEN, width), f32), jax.ShapeDtypeStruct((1, width), f32)],
        scratch_shapes=[
            vmem((3, LEN, hidden), bf16),
            vmem((3 * hidden, width), bf16),
            pltpu.SemaphoreType.DMA,
            pltpu.SemaphoreType.DMA,
        ],
        compiler_params=PARAMS,
        cost_estimate=FILLER,
        name="inputs_back",
    )(me, inputs, gain, back_grad, grads, *arrays)


class Wires:
    def __init__(self, mesh):
        self.inner = mesh.shape["fsdp"]
        self.count = mesh.shape["dp"] * self.inner
        rest = [1 << b for b in range(1, self.inner.bit_length() - 1)]
        self.digits = [rest[i : i + 2] for i in range(0, len(rest), 2)]
        self.core, self.x, self.y = self.inner, 2 * self.inner, 1
        self.bits = {"A": [self.y, self.x, self.core], "B": [self.x, self.y, self.core]}

    def swap(self, value, mask):
        return lax.ppermute(value, AXES, [(i, i ^ mask) for i in range(self.count)])

    def spread(self, digit):
        return [sum(bit for j, bit in enumerate(digit) if k >> j & 1) for k in range(1 << len(digit))]

    def masks(self, order):
        found = [0]
        for digit in self.digits:
            found = [m ^ s for s in self.spread(digit) for m in found]
        lists = [found]
        for bit in self.bits[order]:
            lists = lists + [[m ^ bit for m in one] for one in lists]
        return lists

    def line(self, held, digits, tie=None):
        for digit in digits:
            came = [self.swap(held, m) for m in self.spread(digit)[1:]]
            if tie:
                _, *came = tie(*came)
            held = jnp.concatenate([held] + came)
        return held

    def line_start(self, held):
        for digit in reversed(self.digits[1:]):
            held = self.line_end(*self.line_step(held, digit))
        return self.line_step(held, self.digits[0])

    def line_step(self, held, digit):
        masks = self.spread(digit)
        blocks = jnp.split(held, len(masks))
        return blocks[0], [self.swap(one.astype(bf16), m) for one, m in zip(blocks[1:], masks[1:])]

    def line_end(self, held, came):
        for other in came:
            held = held + other.astype(f32)
        return held


def tied(*values):
    return lax.optimization_barrier(values)


def solution(mesh):
    wires = Wires(mesh)
    count = wires.count
    masks = {order: wires.masks(order) for order in "AB"}
    flat = {order: sum(masks[order], []) for order in "AB"}

    def shards(tokens, gating, offsets, prescale, readout, midscale, expand, shifts, contract, cotangent):
        swap = wires.swap
        index = lax.axis_index("dp") * wires.inner + lax.axis_index("fsdp")
        unit = readout.shape[0]
        wide = expand.shape[1]
        thin = prescale.shape[0]
        width = tokens.shape[1]
        hidden = count * unit
        assert tokens.shape[0] == LEN
        me = index.astype(jnp.int32).reshape(1)

        rest = jnp.concatenate([expand.T, contract])[None]
        row = jnp.concatenate([jnp.pad(one, (0, 128 - one.shape[0])) for one in (offsets, shifts, prescale, midscale)])
        taken = 4 * unit
        part = jnp.pad(jnp.concatenate([gating.T, readout, row[None]]), ((0, -(taken + 1) % 8), (0, 0)))
        inputs = interleaved(tokens)
        gate_line = wires.line(part[None], wires.digits, lambda *came: tied(inputs, *came))
        gate_line, rest, cotangent = tied(gate_line, rest, cotangent)
        nz = gate_line.shape[0]
        cut = nz // 2
        gate_x = swap(gate_line, wires.x)
        gate_y = swap(gate_line, wires.y)
        rest_early = [swap(rest, m) for m in wires.spread(wires.digits[0])[1:]]
        upstream = interleaved(cotangent)
        gate_x, upstream, rest_early[0], rest_early[1] = tied(gate_x, upstream, rest_early[0], rest_early[1])
        gate_y, rest_early[2] = tied(gate_y, rest_early[2])
        gate_list = [gate_line, gate_x, gate_y, swap(gate_x[:cut], wires.y), swap(gate_y[cut:], wires.x)]
        gate_list += [swap(one, wires.core) for one in gate_list]
        rest_line = wires.line(jnp.concatenate([rest, *rest_early]), wires.digits[1:])
        rest_x = swap(rest_line, wires.x)
        rest_y = swap(rest_line, wires.y)
        rest_core = swap(rest_line, wires.core)

        quads = masks["A"]
        gate_lists = [quads[0], quads[2], quads[1], quads[3][:cut], quads[3][cut:]]
        gate_lists += [[m ^ wires.core for m in one] for one in gate_lists]
        rows = jnp.concatenate([one[:, taken] for one in gate_list])
        sizes = (3 * unit, wide, thin)
        owner_masks = jnp.asarray(np.array(sum(gate_lists, []), np.int32)[:, None])
        ffn_masks = np.concatenate([masks["A"][k] for k in (0, 1, 4, 5, 2, 3, 6, 7)])
        lane_masks = jnp.asarray(np.repeat(ffn_masks, wide).astype(np.int32)[None])

        if unit % 16:
            places = np.argsort(np.asarray(sum(gate_lists, [])))
            whole = jnp.take(jnp.concatenate(gate_list), jnp.asarray(places)[index ^ jnp.arange(count)], axis=0)
            gate_list = [
                jnp.concatenate([whole[:, : 3 * unit].reshape(-1, width), whole[:, 3 * unit : taken].reshape(-1, width)])[None]
            ]
            gate_lists, gate_size, read_size, zero = [[0]], 3 * hidden, hidden, jnp.zeros_like(me)
            ffn_unit = 4 * nz * wide
        else:
            gate_size, read_size, zero = 3 * unit, unit, me
            ffn_unit = wide

        both = jnp.concatenate([zero, me])
        normed, share, low, pull_f, pull_i, gain_one, gain_two, all_shifts = gates(
            both, inputs, rows, owner_masks, lane_masks, gate_list, gate_lists, gate_size, sizes, hidden
        )
        shift_halves = jnp.split(all_shifts, 2, axis=1)
        low, rest_y, rest_x, rest_core = tied(low, rest_y, rest_x, rest_core)
        rest_corner = [swap(rest_x[:cut], wires.y), swap(rest_y[cut:], wires.x)]

        def merged(group):
            if not unit % 16:
                return group
            halves = [jnp.concatenate([one[:, at : at + wide].reshape(-1, width) for one in group]) for at in (0, wide)]
            return [jnp.concatenate(halves)[None]]

        own = merged([rest_line, rest_y, rest_core, swap(rest_y, wires.core)])

        def apart(grads):
            if not unit % 16:
                return grads
            return grads.reshape(2, -1, wide, width).transpose(1, 0, 2, 3).reshape(-1, 2 * wide, width)

        residual, normed_two, branch, grad, sent_0, kept_0, shift_0 = ffn_first(
            zero, gain_two, shift_halves[0], inputs, upstream, low, gate_list, gate_lists, read_size, gate_size, own,
            ffn_unit,
        )
        residual, normed_two, branch, grad, sent_0, kept_0, shift_0, rest_x, *rest_corner = tied(
            residual, normed_two, branch, grad, sent_0, kept_0, shift_0, rest_x, *rest_corner
        )
        far = [rest_x, *rest_corner]
        own = merged(far + [swap(one, wires.core) for one in far])
        near_core = swap(apart(sent_0), wires.core)
        half = count // 2
        read_plans = [(flat["A"][:half], f32), (flat["A"][half:], bf16)]
        output, residual_grad, rounded, midscale_grad, sent_1, kept_1, shift_1, *read_blocks = ffn_second(
            zero, gain_two, shift_halves[1], residual, normed_two, branch, grad, upstream, low, own, ffn_unit, unit,
            None if unit % 16 else read_plans,
        )
        read_kept, read_sent = sorted_blocks(index, read_plans, read_blocks, unit) if unit % 16 else read_blocks

        output, residual_grad, rounded, midscale_grad, sent_1, kept_1, shift_1, read_kept, read_sent, near_core = tied(
            output, residual_grad, rounded, midscale_grad, sent_1, kept_1, shift_1, read_kept, read_sent, near_core
        )
        far_core = swap(apart(sent_1), wires.core)
        read_core = swap(read_sent, wires.core)
        ffn_terms = [(apart(kept_0), near_core), (apart(kept_1), far_core)]

        def quad(k, low, high):
            kept, came = ffn_terms[k // 2]
            base = k % 2 * nz
            ffn = kept[base + low : base + high] + came[base + low : base + high].astype(f32)
            base = k * nz
            read = read_kept[base + low : base + high] + read_core[base + low : base + high].astype(f32)
            return jnp.concatenate([ffn, read], axis=1)

        send_a, send_b = quad(3, 0, cut).astype(bf16), quad(3, cut, nz).astype(bf16)
        rounded, send_a, send_b = tied(rounded, send_a, send_b)
        corner_a, corner_b = swap(send_a, wires.y), swap(send_b, wires.x)
        gate_plans = [
            (flat["A"][:half], f32), (masks["A"][7], bf16), (masks["A"][4] + masks["A"][5] + masks["A"][6], bf16)
        ]
        gate_grads, off_grad, *gate_blocks = back(
            zero, rounded, normed, share, pull_f, pull_i, gate_list, gate_lists, read_size, gate_size,
            None if unit % 16 else gate_plans,
        )
        if unit % 16:
            gate_blocks = sorted_blocks(index, gate_plans, gate_blocks, 3 * unit)
        gate_kept, corner_sent, others_sent, gate_grads, off_grad, corner_a, corner_b = tied(
            *gate_blocks, gate_grads, off_grad, corner_a, corner_b
        )
        corner_core = swap(corner_sent, wires.core)
        others_core = swap(others_sent, wires.core)
        send_x = jnp.concatenate([quad(2, 0, cut) + corner_a.astype(f32), quad(2, cut, nz)]).astype(bf16)
        send_y = jnp.concatenate([quad(1, 0, cut), quad(1, cut, nz) + corner_b.astype(f32)]).astype(bf16)
        gate_corner = (gate_kept[3 * nz :] + corner_core.astype(f32)).astype(bf16)
        send_a, send_b = gate_corner[:cut], gate_corner[cut:]
        gate_grads, send_a, send_b, send_x, send_y, output, midscale_grad, off_grad, shift_0, shift_1 = tied(
            gate_grads, send_a, send_b, send_x, send_y, output, midscale_grad, off_grad, shift_0, shift_1
        )
        corner_a, corner_b = swap(send_a, wires.y), swap(send_b, wires.x)
        rest_x, rest_y = swap(send_x, wires.x), swap(send_y, wires.y)
        tokens_grad, prescale_grad = inputs_back(
            zero, inputs, gain_one, residual_grad, gate_grads, gate_list, gate_lists, gate_size
        )
        block_output = sequential(output)
        corner_a, corner_b, rest_x, rest_y, tokens_grad, prescale_grad, block_output = tied(
            corner_a, corner_b, rest_x, rest_y, tokens_grad, prescale_grad, block_output
        )

        def side(k, low, high):
            part = slice(k * nz + low, k * nz + high)
            return gate_kept[part] + others_core[part].astype(f32)

        send_x = jnp.concatenate([side(2, 0, cut) + corner_a.astype(f32), side(2, cut, nz)]).astype(bf16)
        send_y = jnp.concatenate([side(1, 0, cut), side(1, cut, nz) + corner_b.astype(f32)]).astype(bf16)
        send_x, send_y, prescale_grad, rest_x, rest_y = tied(send_x, send_y, prescale_grad, rest_x, rest_y)
        gate_x, gate_y = swap(send_x, wires.x), swap(send_y, wires.y)
        rest_kept, rest_came = wires.line_start(quad(0, 0, nz) + rest_x.astype(f32) + rest_y.astype(f32))
        vectors = vector_rows(
            me, lane_masks, sizes, count, off_grad, shift_0, shift_1, prescale_grad, midscale_grad
        )
        gate_x, gate_y, tokens_grad, vectors, rest_came[0], rest_came[1] = tied(
            gate_x, gate_y, tokens_grad, vectors, rest_came[0], rest_came[1]
        )
        gate_part = side(0, 0, nz) + gate_x.astype(f32) + gate_y.astype(f32)
        gate_kept, gate_came = wires.line_start(gate_part)
        vectors = lax.all_to_all(vectors, AXES, 0, 0, tiled=True)
        tokens_grad = sequential(tokens_grad)
        tokens_grad, vectors, block_output, rest_kept, rest_came, gate_kept, gate_came = tied(
            tokens_grad, vectors, block_output, rest_kept, rest_came, gate_kept, gate_came
        )
        rest_part = wires.line_end(rest_kept, rest_came)[0]
        gate_part = wires.line_end(gate_kept, gate_came)[0]
        vectors = jnp.sum(vectors, axis=0)
        offsets_part, shifts_part, prescale_part, midscale_part = (
            vectors[at : at + size] for at, size in zip(range(0, 512, 128), (*sizes, thin))
        )
        return (
            block_output,
            tokens_grad,
            gate_part.T,
            offsets_part,
            prescale_part,
            rest_part[2 * wide :],
            midscale_part,
            rest_part[:wide].T,
            shifts_part,
            rest_part[wide : 2 * wide],
        )

    rows = P(AXES, None)
    columns = P(None, AXES)
    line = P(AXES)
    in_specs = (rows, columns, line, line, rows, line, columns, line, rows, rows)
    out_specs = (rows, rows, columns, line, line, rows, line, columns, line, rows)
    return jax.shard_map(shards, mesh=mesh, in_specs=in_specs, out_specs=out_specs, check_vma=False)
```

time: 820 us -> 196 us (0.24)
  waiting for transfers between devices: 424 us -> 40.9 us
  other arithmetic: 137 us -> 13.5 us
  Pallas kernels: 0 us -> 85.1 us
  blocking collectives: 82.6 us -> 0 us
  matrix products: 71.4 us -> 0 us
  local copies, waits for them, and re-layouts: 83.1 us -> 13.4 us
  starting transfers between devices: 0.49 us -> 41 us
  between operations: 15.3 us -> 1.37 us
    reduce_scatter x4 -> x0, waiting for transfers between devices: 350 us -> none  [the longest x1 144 us: shards(): lax.psum_scatter(expand_grad, ('dp', 'fsdp'), scatter_dimension=1, tiled=...]
    add x23 -> x4, other arithmetic: 113 us -> 2.4 us  [the longest x2 1.59 us: quad(): kept[base + low:base + high] + came[base + low:base + high].astype(f32)]
    pallas_call x0 -> x10, Pallas kernels: none -> 85.1 us  [the longest x1 16.5 us: ffn_second(): pl.pallas_call(partial(second_kernel, plans, len(own)), in_specs=[SCALAR,...]
    unnamed x2 -> x0, blocking collectives: 82.6 us -> none
    all_gather x4 -> x0, waiting for transfers between devices: 71.5 us -> none  [the longest x1 46.7 us: shards(): lax.all_gather(contract, ('dp', 'fsdp'), axis=0, tiled=True)]
    dot_general x12 -> x0, matrix products: 71.4 us -> none  [the longest x4 28.9 us: matmul(): return jnp.dot(left, right, preferred_element_type=jnp.float32)]
    slice x33 -> x20, local copies, waits for them, and re-layouts: 50.1 us -> 6.01 us  [the longest x10 2.26 us: shards(): rows = jnp.concatenate([one[:, taken] for one in gate_list])]
    ppermute x0 -> x43, waiting for transfers between devices: none -> 40.9 us  [swap(): return lax.ppermute(value, AXES, [(i, i ^ mask) for i in range(self.count)])]
  transfers between devices with their start and end apart: 8 -> 44, of which waited for: 6 -> 13; matrix products, arithmetic and copies ran while one was open for 32% -> 9% of each run, Pallas kernels for 0% -> 44%
where the time goes in v1:
time: 196 us; the launch traced here: 195 us
  Pallas kernels  85.1 us (43%)
  starting transfers between devices  41 us (21%)
  waiting for transfers between devices  40.9 us (21%)
  other arithmetic  13.5 us (7%)
  local copies, waits for them, and re-layouts  13.4 us (7%)
    ppermute x43, waiting for transfers between devices, swap(): return lax.ppermute(value, AXES, [(i, i ^ mask) for i in range(self.count)])  40.9 us
    ppermute x43, starting transfers between devices, swap(): return lax.ppermute(value, AXES, [(i, i ^ mask) for i in range(self.count)])  37.2 us
    pallas_call x1, Pallas kernels, ffn_second(): pl.pallas_call(partial(second_kernel, plans, len(own)), in_specs=[SCALAR,...  16.5 us
    pallas_call x1, Pallas kernels, back(): pl.pallas_call(partial(back_kernel, lists, size, skip, plans), grid=(hidd...  15.5 us
    pallas_call x1, Pallas kernels, ffn_first(): pl.pallas_call(partial(first_kernel, lists, size, skip), in_specs=[SCALAR...  14.5 us
    pallas_call x1, Pallas kernels, gates(): pl.pallas_call(partial(gates_kernel, lists, size, sizes), grid=(hidden //...  12.8 us
    pallas_call x1, Pallas kernels, inputs_back(): pl.pallas_call(partial(inputs_kernel, lists, size), in_specs=[SCALAR, WHO...  11.1 us
    pallas_call x2, Pallas kernels, sequential(): pl.pallas_call(sequence_kernel, out_shape=jax.ShapeDtypeStruct(values.sha...  6.3 us
  transfers between devices with their start and end apart: 44, of which 13 were waited for; matrix products, arithmetic and copies ran while one was open for 9% of the time, Pallas kernels for 44%

profile of v1, /device:TPU:0, one launch (start us, length us, event | category | flops | bytes accessed | tf_op | source)
XLA Modules:
  0.0 195.4 jit_solution(9449528663011171610)
XLA Ops:
  2.4 5.1 %collective-permute-start.2 = (bf16[1,136,512]{2,1,0:T(8,128)(2,1)S(1)}, bf16[1,136,512]{2,1,0:T(8,128)(2,1)S(1)}, u32[]{:S(2)}, u32[]{:S(2)}) collective-permute-start(bf16[1,136,512]{2,1,0:T(8,128)(2,1)S(1)} %fusion.8), channel_id=1, source_target_pairs={{0,6},{1,7},{2,4},{3,5},{4,2},{5,3},{6,0},{7,1},{8,14},{9,15},{10,... | collective-permute-start | bytes 417800 | tf_op jit(solution)/shard_map/ppermute | solution.py:642
  8.1 2.9 %interleave.2.inputs.inputs_h = bf16[1024,512]{1,0:T(8,128)(2,1)} custom-call(bf16[1024,512]{1,0:T(8,128)(2,1)} %values.1), custom_call_target="tpu_custom_call" | custom-call | flops 1000 | bytes 1000 | tf_op jit(solution)/shard_map/interleave/pallas_call | solution.py:48
  12.1 7.2 %collective-permute-done.1 = bf16[1,136,512]{2,1,0:T(8,128)(2,1)S(1)} collective-permute-done((bf16[1,136,512]{2,1,0:T(8,128)(2,1)S(1)}, bf16[1,136,512]{2,1,0:T(8,128)(2,1)S(1)}, u32[]{:S(2)}, u32[]{:S(2)}) %collective-permute-start.1) | collective-permute-done | bytes 139296 | tf_op jit(solution)/shard_map/ppermute | solution.py:642
  22.4 2.5 %collective-permute-start.7 = (bf16[1,128,512]{2,1,0:T(8,128)(2,1)S(1)}, bf16[1,128,512]{2,1,0:T(8,128)(2,1)S(1)}, u32[]{:S(2)}, u32[]{:S(2)}) collective-permute-start(bf16[1,128,512]{2,1,0:T(8,128)(2,1)S(1)} %maximum_bitcast_fusion), channel_id=1, source_target_pairs={{0,6},{1,7},{2,4},{3,5},{4,2},{5,3},{6,0},{7,1},{8,14},{9,15},{10,... | collective-permute-start | bytes 393224 | tf_op jit(solution)/shard_map/ppermute | solution.py:642
  24.9 5.7 %collective-permute-done.7 = bf16[1,128,512]{2,1,0:T(8,128)(2,1)S(1)} collective-permute-done((bf16[1,128,512]{2,1,0:T(8,128)(2,1)S(1)}, bf16[1,128,512]{2,1,0:T(8,128)(2,1)S(1)}, u32[]{:S(2)}, u32[]{:S(2)}) %collective-permute-start.7) | collective-permute-done | bytes 131104 | tf_op jit(solution)/shard_map/ppermute | solution.py:642
  31.6 2.9 %interleave.3.cotangent_h = bf16[1024,512]{1,0:T(8,128)(2,1)} custom-call(bf16[1024,512]{1,0:T(8,128)(2,1)} %values.2), custom_call_target="tpu_custom_call" | custom-call | flops 1000 | bytes 1000 | tf_op jit(solution)/shard_map/interleave/pallas_call | solution.py:48
  38.1 3.2 %collective-permute-done.9.refs_4_ = bf16[2,136,512]{2,1,0:T(8,128)(2,1)} collective-permute-done((bf16[2,136,512]{2,1,0:T(8,128)(2,1)S(1)}, bf16[2,136,512]{2,1,0:T(8,128)(2,1)}, u32[]{:S(2)}, u32[]{:S(2)}) %collective-permute-start.9) | collective-permute-done | bytes 278560 | tf_op jit(solution)/shard_map/ppermute | solution.py:642
  41.3 2.4 %collective-permute-done.8.refs_3_ = bf16[2,136,512]{2,1,0:T(8,128)(2,1)} collective-permute-done((bf16[2,136,512]{2,1,0:T(8,128)(2,1)S(1)}, bf16[2,136,512]{2,1,0:T(8,128)(2,1)}, u32[]{:S(2)}, u32[]{:S(2)}) %collective-permute-start.8) | collective-permute-done | bytes 278560 | tf_op jit(solution)/shard_map/ppermute | solution.py:642
  48.8 2.5 %concatenate.67.rows = bf16[32,512]{1,0:T(8,128)(2,1)} concatenate(bf16[4,512]{1,0:T(4,128)(2,1)S(1)} %bitcast.57, bf16[4,512]{1,0:T(4,128)(2,1)S(1)} %bitcast.60, bf16[4,512]{1,0:T(4,128)(2,1)S(1)} %bitcast.59, bf16[2,512]{1,0:T(2,128)(2,1)S(1)} %bitcast.64, bf16[2,512]{1,0:T(2,128)(2,1)S(1)} %bitcast.63, bf16[4,512]{1,0:T(4,128)(2,1)S(1)} %bitcast.58, ...), dimensions={0} | concatenate | bytes 65536 | tf_op jit(solution)/shard_map/concatenate | solution.py:726
  51.3 12.8 %gates.1 = (bf16[1024,512]{1,0:T(8,128)(2,1)}, f32[1024,1024]{1,0:T(8,128)}, bf16[1024,1024]{1,0:T(8,128)(2,1)}, bf16[1024,1024]{1,0:T(8,128)(2,1)}, bf16[1024,1...) custom-call(s32[2]{0:T(128)} %pad_add_fusion.me, ...), custom_call_target="tpu_custom_call" | custom-call | flops 99999997952 | bytes 100000000 | tf_op jit(solution)/shard_map/gates/pallas_call | solution.py:266
  69.5 14.5 %ffn_first.1 = (f32[1024,512]{1,0:T(8,128)}, bf16[1024,512]{1,0:T(8,128)(2,1)}, f32[1024,512]{1,0:T(8,128)}, f32[1024,512]{1,0:T(8,128)}, bf16[8,128,512]{2,1,0:...) custom-call(s32[1]{0:T(128)} %bitcast.me, f32[1,512]{1,0:T(1,128)} %get-tuple-element.134.gain, ...), custom_call_target="tpu_custom_call" | custom-call | flops 99999997952 | bytes 100000000 | tf_op jit(solution)/shard_map/ffn_first/pallas_call | solution.py:424
  88.4 16.5 %ffn_second.1 = (bf16[1024,512]{1,0:T(8,128)(2,1)}, f32[1024,512]{1,0:T(8,128)}, bf16[1024,512]{1,0:T(8,128)(2,1)}, f32[1,512]{1,0:T(1,128)}, bf16[8,128,512]{2,...) custom-call(s32[1]{0:T(128)} %bitcast.me, ...), custom_call_target="tpu_custom_call" | custom-call | flops 99999997952 | bytes 100000000 | tf_op jit(solution)/shard_map/ffn_second/pallas_call | solution.py:465
  106.9 1.7 collective-permute-done.26
  111.0 15.5 %back.1 = (bf16[3,1024,1024]{2,1,0:T(8,128)(2,1)}, f32[3,1024]{1,0:T(4,128)}, f32[16,96,512]{2,1,0:T(8,128)}, bf16[4,96,512]{2,1,0:T(8,128)(2,1)}, bf16[12,96,512]{2,1,0:T(8,128)(2,1)}) custom-call(s32[1]{0:T(128)} %bitcast.me, bf16[1024,512]{1,0:T(8,128)(2,1)} %get-tuple-element.174.rounded, bf16[1024,512]{1,0:T(8,128)(2,1)} %get-tuple-element.175.normed, ...), custom_call_target="tpu_custom_call" | custom-call | flops 99999997952 | bytes 100000000 | tf_op jit(solution)/shard_map/back/pallas_call | solution.py:569
  135.2 2.7 %sequence.2 = bf16[1024,512]{1,0:T(8,128)(2,1)} custom-call(bf16[1024,512]{1,0:T(8,128)(2,1)} %get-tuple-element.208.values), custom_call_target="tpu_custom_call" | custom-call | flops 99999997952 | bytes 100000000 | tf_op jit(solution)/shard_map/sequence/pallas_call | solution.py:68
  138.0 11.1 %inputs_back.1 = (f32[1024,512]{1,0:T(8,128)}, f32[1,512]{1,0:T(1,128)}) custom-call(s32[1]{0:T(128)} %bitcast.me, bf16[1024,512]{1,0:T(8,128)(2,1)} %interleave.2.inputs.inputs_h, f32[1,512]{1,0:T(1,128)} %get-tuple-element.203.gain, f32[1024,512]{1,0:T(8,128)} %get-tuple-element.204.back, bf16[3,1024,1024]{2,1,0:T(8,128)(2,1)} %get-tuple-element.205.grads_h, ...), custom_call_target="tpu_custom_call" | custom-call | flops 99999997952 | bytes 100000000 | tf_op jit(solution)/shard_map/inputs_back/pallas_call | solution.py:615
  149.1 4.6 %collective-permute-done.33 = bf16[4,160,512]{2,1,0:T(8,128)(2,1)} collective-permute-done((bf16[4,160,512]{2,1,0:T(8,128)(2,1)}, bf16[4,160,512]{2,1,0:T(8,128)(2,1)}, u32[]{:S(2)}, u32[]{:S(2)}) %collective-permute-start.33) | collective-permute-done | bytes 655392 | tf_op jit(solution)/shard_map/ppermute | solution.py:642
  159.6 2.4 %collective-permute-start.37 = (bf16[1,160,512]{2,1,0:T(8,128)(2,1)S(1)}, bf16[1,160,512]{2,1,0:T(8,128)(2,1)S(1)}, u32[]{:S(2)}, u32[]{:S(2)}) collective-permute-start(bf16[1,160,512]{2,1,0:T(8,128)(2,1)S(1)} %get-tuple-element.264), channel_id=1, source_target_pairs={{0,2},{1,3},{2,0},{3,1},{4,6},{5,7},{6,4},{7,5},{8,10},{9,11},{10,... | collective-permute-start | bytes 491528 | tf_op jit(solution)/shard_map/ppermute | solution.py:642
  163.6 2.7 %vectors.1 = f32[32,512]{1,0:T(8,128)} custom-call(s32[1]{0:T(128)} %bitcast.me, s32[1,2048]{1,0:T(1,128)} %constant.20.clone.lane_masks.masks, f32[3,1024]{1,0:T(4,128)} %get-tuple-element.217.offsets, f32[1,1024]{1,0:T(1,128)} %get-tuple-element.218.shift_0, f32[1,1024]{1,0:T(1,128)} %get-tuple-element.219.shift_1, f32[1,512]{1,0:T(1,128)} %get-tuple-element.220.prescale, ...), custom_call_target="tpu_custom_call" | custom-call | flops 1000 | bytes 1000 | tf_op jit(solution)/shard_map/vectors/pallas_call | solution.py:171
  166.3 5.9 %collective-permute-done.38 = bf16[1,160,512]{2,1,0:T(8,128)(2,1)S(1)} collective-permute-done((bf16[1,160,512]{2,1,0:T(8,128)(2,1)S(1)}, bf16[1,160,512]{2,1,0:T(8,128)(2,1)S(1)}, u32[]{:S(2)}, u32[]{:S(2)}) %collective-permute-start.38) | collective-permute-done | bytes 163872 | tf_op jit(solution)/shard_map/ppermute | solution.py:642
  174.2 3.9 %all-to-all-start = ((f32[32,1,512]{2,1,0:T(1,128)}), f32[32,1,512]{2,1,0:T(1,128)S(1)}, u32[]{:S(2)}, u32[]{:S(2)}) async-start(f32[32,1,512]{2,1,0:T(1,128)} %copy.107), calls=%async_computation | async-start | bytes 131072 | tf_op jit(solution)/shard_map/all_to_all | solution.py:849
  178.0 3.7 %collective-permute-start.42 = (bf16[1,96,512]{2,1,0:T(8,128)(2,1)S(1)}, bf16[1,96,512]{2,1,0:T(8,128)(2,1)S(1)}, u32[]{:S(2)}, u32[]{:S(2)}) collective-permute-start(bf16[1,96,512]{2,1,0:T(8,128)(2,1)S(1)} %get-tuple-element.265), channel_id=1, source_target_pairs={{0,6},{1,7},{2,4},{3,5},{4,2},{5,3},{6,0},{7,1},{8,14},{9,15},{10,... | collective-permute-start | bytes 294920 | tf_op jit(solution)/shard_map/ppermute | solution.py:642
  182.5 3.6 %sequence.3 = f32[1024,512]{1,0:T(8,128)} custom-call(f32[1024,512]{1,0:T(8,128)} %get-tuple-element.224.values), custom_call_target="tpu_custom_call" | custom-call | flops 99999997952 | bytes 100000000 | tf_op jit(solution)/shard_map/sequence/pallas_call | solution.py:68
  186.4 5.2 %collective-permute-done.41 = bf16[1,96,512]{2,1,0:T(8,128)(2,1)S(1)} collective-permute-done((bf16[1,96,512]{2,1,0:T(8,128)(2,1)S(1)}, bf16[1,96,512]{2,1,0:T(8,128)(2,1)S(1)}, u32[]{:S(2)}, u32[]{:S(2)}) %collective-permute-start.41) | collective-permute-done | bytes 98336 | tf_op jit(solution)/shard_map/ppermute | solution.py:642
  (191 shorter events, 52.9 us)
Async XLA Ops:
  7.5 11.8 %collective-permute-start.1 = (bf16[1,136,512]{2,1,0:T(8,128)(2,1)S(1)}, bf16[1,136,512]{2,1,0:T(8,128)(2,1)S(1)}, u32[]{:S(2)}, u32[]{:S(2)}) collective-permute-start(bf16[1,136,512]{2,1,0:T(8,128)(2,1)S(1)} %fusion.8), channel_id=1, source_target_pairs={{0,4},{1,5},{2,6},{3,7},{4,0},{5,1},{6,2},{7,3},{8,12},{9,13},{10,... | collective-permute-start | bytes 417800 | tf_op jit(solution)/shard_map/ppermute | solution.py:642
  7.5 11.8 %collective-permute-start = (bf16[1,136,512]{2,1,0:T(8,128)(2,1)S(1)}, bf16[1,136,512]{2,1,0:T(8,128)(2,1)S(1)}, u32[]{:S(2)}, u32[]{:S(2)}) collective-permute-start(bf16[1,136,512]{2,1,0:T(8,128)(2,1)S(1)} %fusion.8), channel_id=1, source_target_pairs={{0,2},{1,3},{2,0},{3,1},{4,6},{5,7},{6,4},{7,5},{8,10},{9,11},{10,... | collective-permute-start | bytes 417800 | tf_op jit(solution)/shard_map/ppermute | solution.py:642
  19.3 15.2 %collective-permute-start.6 = (bf16[4,136,512]{2,1,0:T(8,128)(2,1)S(1)}, bf16[4,136,512]{2,1,0:T(8,128)(2,1)S(1)}, u32[]{:S(2)}, u32[]{:S(2)}) collective-permute-start(bf16[4,136,512]{2,1,0:T(8,128)(2,1)S(1)} %pad_maximum_fusion.1.refs_0_), channel_id=1, source_target_pairs={{0,1},{1,0},{2,3},{3,2},{4,5},{5,4},{6,7},{7,6},{8,9},{9,8},{10,11... | collective-permute-start | bytes 1671176 | tf_op jit(solution)/shard_map/ppermute | solution.py:642
  20.9 15.4 %collective-permute-start.3 = (bf16[4,136,512]{2,1,0:T(8,128)(2,1)S(1)}, bf16[4,136,512]{2,1,0:T(8,128)(2,1)S(1)}, u32[]{:S(2)}, u32[]{:S(2)}) collective-permute-start(bf16[4,136,512]{2,1,0:T(8,128)(2,1)S(1)} %pad_maximum_fusion.1.refs_0_), channel_id=1, source_target_pairs={{0,16},{1,17},{2,18},{3,19},{4,20},{5,21},{6,22},{7,23},{8,24},{9,... | collective-permute-start | bytes 1671176 | tf_op jit(solution)/shard_map/ppermute | solution.py:642
  24.9 18.8 %collective-permute-start.10 = (bf16[4,136,512]{2,1,0:T(8,128)(2,1)S(1)}, bf16[4,136,512]{2,1,0:T(8,128)(2,1)}, u32[]{:S(2)}, u32[]{:S(2)}) collective-permute-start(bf16[4,136,512]{2,1,0:T(8,128)(2,1)S(1)} %pad_maximum_fusion.1.refs_0_), channel_id=1, source_target_pairs={{0,8},{1,9},{2,10},{3,11},{4,12},{5,13},{6,14},{7,15},{8,0},{9,1},... | collective-permute-start | bytes 1671176 | tf_op jit(solution)/shard_map/ppermute | solution.py:642
  44.6 19.6 %collective-permute-start.17 = (bf16[4,128,512]{2,1,0:T(8,128)(2,1)S(1)}, bf16[4,128,512]{2,1,0:T(8,128)(2,1)}, u32[]{:S(2)}, u32[]{:S(2)}) collective-permute-start(bf16[4,128,512]{2,1,0:T(8,128)(2,1)S(1)} %constant_dynamic-update-slice_fusion.refs_10_), channel_id=1, source_target_pairs={{0,8},{1,9},{2,10},{3,11},{4,12},{5,13},{6,14},{7,15},{8,0},{9,1},... | collective-permute-start | bytes 1572872 | tf_op jit(solution)/shard_map/ppermute | solution.py:642
  46.6 17.5 %collective-permute-start.16 = (bf16[4,128,512]{2,1,0:T(8,128)(2,1)S(1)}, bf16[4,128,512]{2,1,0:T(8,128)(2,1)S(1)}, u32[]{:S(2)}, u32[]{:S(2)}) collective-permute-start(bf16[4,128,512]{2,1,0:T(8,128)(2,1)S(1)} %constant_dynamic-update-slice_fusion.refs_10_), channel_id=1, source_target_pairs={{0,16},{1,17},{2,18},{3,19},{4,20},{5,21},{6,22},{7,23},{8,24},{9,... | collective-permute-start | bytes 1572872 | tf_op jit(solution)/shard_map/ppermute | solution.py:642
  47.3 16.8 %collective-permute-start.15 = (bf16[4,128,512]{2,1,0:T(8,128)(2,1)S(1)}, bf16[4,128,512]{2,1,0:T(8,128)(2,1)S(1)}, u32[]{:S(2)}, u32[]{:S(2)}) collective-permute-start(bf16[4,128,512]{2,1,0:T(8,128)(2,1)S(1)} %constant_dynamic-update-slice_fusion.refs_10_), channel_id=1, source_target_pairs={{0,1},{1,0},{2,3},{3,2},{4,5},{5,4},{6,7},{7,6},{8,9},{9,8},{10,11... | collective-permute-start | bytes 1572872 | tf_op jit(solution)/shard_map/ppermute | solution.py:642
  64.3 19.7 %collective-permute-start.20 = (bf16[2,128,512]{2,1,0:T(8,128)(2,1)S(1)}, bf16[2,128,512]{2,1,0:T(8,128)(2,1)S(1)}, u32[]{:S(2)}, u32[]{:S(2)}) collective-permute-start(bf16[2,128,512]{2,1,0:T(8,128)(2,1)S(1)} %slice.208), channel_id=1, source_target_pairs={{0,16},{1,17},{2,18},{3,19},{4,20},{5,21},{6,22},{7,23},{8,24},{9,... | collective-permute-start | bytes 786440 | tf_op jit(solution)/shard_map/ppermute | solution.py:642
  65.9 18.1 %collective-permute-start.19 = (bf16[2,128,512]{2,1,0:T(8,128)(2,1)S(1)}, bf16[2,128,512]{2,1,0:T(8,128)(2,1)S(1)}, u32[]{:S(2)}, u32[]{:S(2)}) collective-permute-start(bf16[2,128,512]{2,1,0:T(8,128)(2,1)S(1)} %slice.207), channel_id=1, source_target_pairs={{0,1},{1,0},{2,3},{3,2},{4,5},{5,4},{6,7},{7,6},{8,9},{9,8},{10,11... | collective-permute-start | bytes 786440 | tf_op jit(solution)/shard_map/ppermute | solution.py:642
  84.7 20.2 %collective-permute-start.24 = (bf16[8,128,512]{2,1,0:T(8,128)(2,1)}, bf16[8,128,512]{2,1,0:T(8,128)(2,1)S(1)}, u32[]{:S(2)}, u32[]{:S(2)}) collective-permute-start(bf16[8,128,512]{2,1,0:T(8,128)(2,1)} %get-tuple-element.168), channel_id=1, source_target_pairs={{0,8},{1,9},{2,10},{3,11},{4,12},{5,13},{6,14},{7,15},{8,0},{9,1},... | collective-permute-start | bytes 3145736 | tf_op jit(solution)/shard_map/ppermute | solution.py:642
  109.9 16.7 %collective-permute-start.27 = (bf16[2,160,512]{2,1,0:T(8,128)(2,1)S(1)}, bf16[2,160,512]{2,1,0:T(8,128)(2,1)S(1)}, u32[]{:S(2)}, u32[]{:S(2)}) collective-permute-start(bf16[2,160,512]{2,1,0:T(8,128)(2,1)S(1)} %pad_maximum_fusion.4), channel_id=1, source_target_pairs={{0,1},{1,0},{2,3},{3,2},{4,5},{5,4},{6,7},{7,6},{8,9},{9,8},{10,11... | collective-permute-start | bytes 983048 | tf_op jit(solution)/shard_map/ppermute | solution.py:642
  110.5 16.1 %collective-permute-start.28 = (bf16[2,160,512]{2,1,0:T(8,128)(2,1)S(1)}, bf16[2,160,512]{2,1,0:T(8,128)(2,1)S(1)}, u32[]{:S(2)}, u32[]{:S(2)}) collective-permute-start(bf16[2,160,512]{2,1,0:T(8,128)(2,1)S(1)} %pad_maximum_fusion.5), channel_id=1, source_target_pairs={{0,16},{1,17},{2,18},{3,19},{4,20},{5,21},{6,22},{7,23},{8,24},{9,... | collective-permute-start | bytes 983048 | tf_op jit(solution)/shard_map/ppermute | solution.py:642
  126.6 27.0 %collective-permute-start.29 = (bf16[12,96,512]{2,1,0:T(8,128)(2,1)}, bf16[12,96,512]{2,1,0:T(8,128)(2,1)}, u32[]{:S(2)}, u32[]{:S(2)}) collective-permute-start(bf16[12,96,512]{2,1,0:T(8,128)(2,1)} %get-tuple-element.187), channel_id=1, source_target_pairs={{0,8},{1,9},{2,10},{3,11},{4,12},{5,13},{6,14},{7,15},{8,0},{9,1},... | collective-permute-start | bytes 3538952 | tf_op jit(solution)/shard_map/ppermute | solution.py:642
  131.2 17.9 %collective-permute-start.31 = (bf16[2,96,512]{2,1,0:T(8,128)(2,1)}, bf16[2,96,512]{2,1,0:T(8,128)(2,1)}, u32[]{:S(2)}, u32[]{:S(2)}) collective-permute-start(bf16[2,96,512]{2,1,0:T(8,128)(2,1)} %get-tuple-element.199), channel_id=1, source_target_pairs={{0,1},{1,0},{2,3},{3,2},{4,5},{5,4},{6,7},{7,6},{8,9},{9,8},{10,11... | collective-permute-start | bytes 589832 | tf_op jit(solution)/shard_map/ppermute | solution.py:642
  132.7 16.4 %collective-permute-start.32 = (bf16[2,96,512]{2,1,0:T(8,128)(2,1)}, bf16[2,96,512]{2,1,0:T(8,128)(2,1)}, u32[]{:S(2)}, u32[]{:S(2)}) collective-permute-start(bf16[2,96,512]{2,1,0:T(8,128)(2,1)} %get-tuple-element.200), channel_id=1, source_target_pairs={{0,16},{1,17},{2,18},{3,19},{4,20},{5,21},{6,22},{7,23},{8,24},{9,... | collective-permute-start | bytes 589832 | tf_op jit(solution)/shard_map/ppermute | solution.py:642
  134.2 19.5 %collective-permute-start.33 = (bf16[4,160,512]{2,1,0:T(8,128)(2,1)}, bf16[4,160,512]{2,1,0:T(8,128)(2,1)}, u32[]{:S(2)}, u32[]{:S(2)}) collective-permute-start(bf16[4,160,512]{2,1,0:T(8,128)(2,1)} %maximum_maximum_fusion), channel_id=1, source_target_pairs={{0,16},{1,17},{2,18},{3,19},{4,20},{5,21},{6,22},{7,23},{8,24},{9,... | collective-permute-start | bytes 1966088 | tf_op jit(solution)/shard_map/ppermute | solution.py:642
  134.7 18.9 %collective-permute-start.34 = (bf16[4,160,512]{2,1,0:T(8,128)(2,1)}, bf16[4,160,512]{2,1,0:T(8,128)(2,1)}, u32[]{:S(2)}, u32[]{:S(2)}) collective-permute-start(bf16[4,160,512]{2,1,0:T(8,128)(2,1)} %pad_maximum_fusion), channel_id=1, source_target_pairs={{0,1},{1,0},{2,3},{3,2},{4,5},{5,4},{6,7},{7,6},{8,9},{9,8},{10,11... | collective-permute-start | bytes 1966088 | tf_op jit(solution)/shard_map/ppermute | solution.py:642
  155.4 16.8 %collective-permute-start.35 = (bf16[4,96,512]{2,1,0:T(8,128)(2,1)S(1)}, bf16[4,96,512]{2,1,0:T(8,128)(2,1)S(1)}, u32[]{:S(2)}, u32[]{:S(2)}) collective-permute-start(bf16[4,96,512]{2,1,0:T(8,128)(2,1)S(1)} %pad_maximum_fusion.2), channel_id=1, source_target_pairs={{0,16},{1,17},{2,18},{3,19},{4,20},{5,21},{6,22},{7,23},{8,24},{9,... | collective-permute-start | bytes 1179656 | tf_op jit(solution)/shard_map/ppermute | solution.py:642
  157.0 15.2 %collective-permute-start.36 = (bf16[4,96,512]{2,1,0:T(8,128)(2,1)S(1)}, bf16[4,96,512]{2,1,0:T(8,128)(2,1)S(1)}, u32[]{:S(2)}, u32[]{:S(2)}) collective-permute-start(bf16[4,96,512]{2,1,0:T(8,128)(2,1)S(1)} %pad_maximum_fusion.3), channel_id=1, source_target_pairs={{0,1},{1,0},{2,3},{3,2},{4,5},{5,4},{6,7},{7,6},{8,9},{9,8},{10,11... | collective-permute-start | bytes 1179656 | tf_op jit(solution)/shard_map/ppermute | solution.py:642
  159.1 13.1 %collective-permute-start.38 = (bf16[1,160,512]{2,1,0:T(8,128)(2,1)S(1)}, bf16[1,160,512]{2,1,0:T(8,128)(2,1)S(1)}, u32[]{:S(2)}, u32[]{:S(2)}) collective-permute-start(bf16[1,160,512]{2,1,0:T(8,128)(2,1)S(1)} %get-tuple-element.263), channel_id=1, source_target_pairs={{0,4},{1,5},{2,6},{3,7},{4,0},{5,1},{6,2},{7,3},{8,12},{9,13},{10,... | collective-permute-start | bytes 491528 | tf_op jit(solution)/shard_map/ppermute | solution.py:642
  159.6 12.6 %collective-permute-start.37 = (bf16[1,160,512]{2,1,0:T(8,128)(2,1)S(1)}, bf16[1,160,512]{2,1,0:T(8,128)(2,1)S(1)}, u32[]{:S(2)}, u32[]{:S(2)}) collective-permute-start(bf16[1,160,512]{2,1,0:T(8,128)(2,1)S(1)} %get-tuple-element.264), channel_id=1, source_target_pairs={{0,2},{1,3},{2,0},{3,1},{4,6},{5,7},{6,4},{7,5},{8,10},{9,11},{10,... | collective-permute-start | bytes 491528 | tf_op jit(solution)/shard_map/ppermute | solution.py:642
  162.0 24.1 %collective-permute-start.39 = (bf16[1,160,512]{2,1,0:T(8,128)(2,1)S(1)}, bf16[1,160,512]{2,1,0:T(8,128)(2,1)S(1)}, u32[]{:S(2)}, u32[]{:S(2)}) collective-permute-start(bf16[1,160,512]{2,1,0:T(8,128)(2,1)S(1)} %get-tuple-element.262), channel_id=1, source_target_pairs={{0,6},{1,7},{2,4},{3,5},{4,2},{5,3},{6,0},{7,1},{8,14},{9,15},{10,... | collective-permute-start | bytes 491528 | tf_op jit(solution)/shard_map/ppermute | solution.py:642
  174.2 11.9 %all-to-all-start = ((f32[32,1,512]{2,1,0:T(1,128)}), f32[32,1,512]{2,1,0:T(1,128)S(1)}, u32[]{:S(2)}, u32[]{:S(2)}) async-start(f32[32,1,512]{2,1,0:T(1,128)} %copy.107), calls=%async_computation | async-start | bytes 131072 | tf_op jit(solution)/shard_map/all_to_all | solution.py:849
  (45 other events, 309.7 us)

commit v2 on v1

--- a/solution.py
+++ b/solution.py
@@ -64,13 +64,13 @@
             target[rows, columns] = scratch[j, pl.ds(run, STEPS, stride=LANES)].astype(target.dtype)
 
 
-def sequential(values):
+def sequential(values, cost):
     return pl.pallas_call(
         sequence_kernel,
         out_shape=jax.ShapeDtypeStruct(values.shape, values.dtype),
         scratch_shapes=[pltpu.VMEM((values.shape[1] // 128, LEN, 128), f32)],
         compiler_params=PARAMS,
-        cost_estimate=FILLER,
+        cost_estimate=cost,
         name="sequence",
     )(values)
 
@@ -174,15 +174,16 @@
         out_specs=pl.BlockSpec(memory_space=pltpu.VMEM),
         out_shape=jax.ShapeDtypeStruct((count, 512), f32),
         compiler_params=PARAMS,
-        cost_estimate=QUICK,
+        cost_estimate=FILLER,
         name="vectors",
     )(me, masks, *grads)
 
 
-def gates_kernel(lists, size, sizes, me, inputs, rows, owner_masks, lane_masks, *refs):
+def gates_kernel(lists, size, taken, row_count, sizes, me, inputs, owner_masks, lane_masks, *refs):
+    row_arrays, refs = refs[:row_count], refs[row_count:]
     arrays = refs[: len(lists)]
     normed, share, low, pull_f, pull_i, gain_one, gain_two, shifts = refs[len(lists) : len(lists) + 8]
-    weights, pre, mid, decay, drive, offsets, sem = refs[len(lists) + 8 :]
+    weights, pre, mid, decay, drive, offsets, small, sem, small_sem = refs[len(lists) + 8 :]
     group = pl.program_id(0)
     wide = share.shape[1]
     hidden = weights.shape[0] // 3
@@ -190,6 +191,12 @@
     @pl.when(group == 0)
     def _():
         copies = start(placed(me[0], lists, arrays, 0, size, weights), sem)
+        found, at = [], 0
+        for array in row_arrays:
+            found.append((array.at[:, pl.ds(taken, LANES)], small.at[pl.ds(at, array.shape[0])]))
+            at += array.shape[0]
+        finish(start(found, small_sem))
+        rows = jnp.sum(small[...].astype(f32), axis=1).astype(bf16)
         owners = owner_masks[...] ^ me[1]
         width = inputs.shape[1]
         gain = laid_out(rows[:, 256:384], owners, *lanes_of(width, sizes[2]))
@@ -254,7 +261,7 @@
     lax.fori_loop(0, STEPS // 2, join, entering[:LANES], unroll=8)
 
 
-def gates(me, inputs, rows, owner_masks, lane_masks, arrays, lists, size, sizes, hidden):
+def gates(me, inputs, row_arrays, taken, owner_masks, lane_masks, arrays, lists, size, sizes, hidden):
     width = inputs.shape[1]
     shape = jax.ShapeDtypeStruct
     whole = lambda one: pl.BlockSpec(one.shape, lambda g: (0, 0))
@@ -264,9 +271,9 @@
     out = lambda dtype: jax.ShapeDtypeStruct((LEN, hidden), dtype)
     solid = pl.BlockSpec((LEN, width), fixed)
     return pl.pallas_call(
-        partial(gates_kernel, lists, size, sizes),
+        partial(gates_kernel, lists, size, taken, len(row_arrays), sizes),
         grid=(hidden // wide,),
-        in_specs=[SCALAR, solid, whole(rows), whole(owner_masks), whole(lane_masks)] + [ANY] * len(arrays),
+        in_specs=[SCALAR, solid, whole(owner_masks), whole(lane_masks)] + [ANY] * (len(row_arrays) + len(arrays)),
         out_specs=[solid]
         + [pl.BlockSpec((LEN, wide), tall)] * 4
         + [pl.BlockSpec((1, width), fixed)] * 2
@@ -281,12 +288,14 @@
             pltpu.VMEM((LEN, wide), f32),
             pltpu.VMEM((LEN, wide), f32),
             pltpu.VMEM((hidden // wide, 3, wide), f32),
+            pltpu.VMEM((owner_masks.shape[0], LANES, width), bf16),
+            pltpu.SemaphoreType.DMA,
             pltpu.SemaphoreType.DMA,
         ],
         compiler_params=PARAMS,
         cost_estimate=FILLER,
         name="gates",
-    )(me, inputs, rows, owner_masks, lane_masks, *arrays)
+    )(me, inputs, owner_masks, lane_masks, *row_arrays, *arrays)
 
 
 def gelu_both(x):
@@ -701,7 +710,7 @@
         rest = jnp.concatenate([expand.T, contract])[None]
         row = jnp.concatenate([jnp.pad(one, (0, 128 - one.shape[0])) for one in (offsets, shifts, prescale, midscale)])
         taken = 4 * unit
-        part = jnp.pad(jnp.concatenate([gating.T, readout, row[None]]), ((0, -(taken + 1) % 8), (0, 0)))
+        part = jnp.pad(jnp.concatenate([gating.T, readout, row[None]]), ((0, LANES - 1), (0, 0)))
         inputs = interleaved(tokens)
         gate_line = wires.line(part[None], wires.digits, lambda *came: tied(inputs, *came))
         gate_line, rest, cotangent = tied(gate_line, rest, cotangent)
@@ -711,8 +720,8 @@
         gate_y = swap(gate_line, wires.y)
         rest_early = [swap(rest, m) for m in wires.spread(wires.digits[0])[1:]]
         upstream = interleaved(cotangent)
-        gate_x, upstream, rest_early[0], rest_early[1] = tied(gate_x, upstream, rest_early[0], rest_early[1])
-        gate_y, rest_early[2] = tied(gate_y, rest_early[2])
+        gate_x, upstream, rest_early[1], rest_early[2] = tied(gate_x, upstream, rest_early[1], rest_early[2])
+        gate_y, rest_early[0] = tied(gate_y, rest_early[0])
         gate_list = [gate_line, gate_x, gate_y, swap(gate_x[:cut], wires.y), swap(gate_y[cut:], wires.x)]
         gate_list += [swap(one, wires.core) for one in gate_list]
         rest_line = wires.line(jnp.concatenate([rest, *rest_early]), wires.digits[1:])
@@ -723,7 +732,7 @@
         quads = masks["A"]
         gate_lists = [quads[0], quads[2], quads[1], quads[3][:cut], quads[3][cut:]]
         gate_lists += [[m ^ wires.core for m in one] for one in gate_lists]
-        rows = jnp.concatenate([one[:, taken] for one in gate_list])
+        row_arrays = gate_list
         sizes = (3 * unit, wide, thin)
         owner_masks = jnp.asarray(np.array(sum(gate_lists, []), np.int32)[:, None])
         ffn_masks = np.concatenate([masks["A"][k] for k in (0, 1, 4, 5, 2, 3, 6, 7)])
@@ -735,6 +744,7 @@
             gate_list = [
                 jnp.concatenate([whole[:, : 3 * unit].reshape(-1, width), whole[:, 3 * unit : taken].reshape(-1, width)])[None]
             ]
+            row_arrays = [jnp.concatenate([one[:, taken : taken + LANES] for one in row_arrays])]
             gate_lists, gate_size, read_size, zero = [[0]], 3 * hidden, hidden, jnp.zeros_like(me)
             ffn_unit = 4 * nz * wide
         else:
@@ -743,7 +753,7 @@
 
         both = jnp.concatenate([zero, me])
         normed, share, low, pull_f, pull_i, gain_one, gain_two, all_shifts = gates(
-            both, inputs, rows, owner_masks, lane_masks, gate_list, gate_lists, gate_size, sizes, hidden
+            both, inputs, row_arrays, 0 if unit % 16 else taken, owner_masks, lane_masks, gate_list, gate_lists, gate_size, sizes, hidden
         )
         shift_halves = jnp.split(all_shifts, 2, axis=1)
         low, rest_y, rest_x, rest_core = tied(low, rest_y, rest_x, rest_core)
@@ -795,68 +805,77 @@
             read = read_kept[base + low : base + high] + read_core[base + low : base + high].astype(f32)
             return jnp.concatenate([ffn, read], axis=1)
 
-        send_a, send_b = quad(3, 0, cut).astype(bf16), quad(3, cut, nz).astype(bf16)
-        rounded, send_a, send_b = tied(rounded, send_a, send_b)
-        corner_a, corner_b = swap(send_a, wires.y), swap(send_b, wires.x)
-        gate_plans = [
-            (flat["A"][:half], f32), (masks["A"][7], bf16), (masks["A"][4] + masks["A"][5] + masks["A"][6], bf16)
-        ]
+        send_x = jnp.concatenate([quad(3, cut, nz), quad(2, cut, nz)]).astype(bf16)
+        send_y = jnp.concatenate([quad(3, 0, cut), quad(1, 0, cut)]).astype(bf16)
+        rounded, send_x, send_y = tied(rounded, send_x, send_y)
+        rest_x, rest_y = swap(send_x, wires.x), swap(send_y, wires.y)
+        places = [quads[3][cut:] + quads[2][cut:] + quads[3][:cut] + quads[1][:cut]]
+        places.append(quads[2][:cut] + quads[1][cut:] + quads[0])
+        away = [[m ^ wires.core for m in one] for one in places]
+        gate_plans = [(places[0], f32), (places[1], f32), (away[0], bf16), (away[1], bf16)]
         gate_grads, off_grad, *gate_blocks = back(
             zero, rounded, normed, share, pull_f, pull_i, gate_list, gate_lists, read_size, gate_size,
             None if unit % 16 else gate_plans,
         )
         if unit % 16:
             gate_blocks = sorted_blocks(index, gate_plans, gate_blocks, 3 * unit)
-        gate_kept, corner_sent, others_sent, gate_grads, off_grad, corner_a, corner_b = tied(
-            *gate_blocks, gate_grads, off_grad, corner_a, corner_b
-        )
-        corner_core = swap(corner_sent, wires.core)
-        others_core = swap(others_sent, wires.core)
-        send_x = jnp.concatenate([quad(2, 0, cut) + corner_a.astype(f32), quad(2, cut, nz)]).astype(bf16)
-        send_y = jnp.concatenate([quad(1, 0, cut), quad(1, cut, nz) + corner_b.astype(f32)]).astype(bf16)
-        gate_corner = (gate_kept[3 * nz :] + corner_core.astype(f32)).astype(bf16)
-        send_a, send_b = gate_corner[:cut], gate_corner[cut:]
-        gate_grads, send_a, send_b, send_x, send_y, output, midscale_grad, off_grad, shift_0, shift_1 = tied(
-            gate_grads, send_a, send_b, send_x, send_y, output, midscale_grad, off_grad, shift_0, shift_1
-        )
-        corner_a, corner_b = swap(send_a, wires.y), swap(send_b, wires.x)
-        rest_x, rest_y = swap(send_x, wires.x), swap(send_y, wires.y)
+        first_kept, second_kept, first_sent, second_sent, gate_grads, off_grad, rest_x, rest_y = tied(
+            *gate_blocks, gate_grads, off_grad, rest_x, rest_y
+        )
+        first_core = swap(first_sent, wires.core)
+        second_core = swap(second_sent, wires.core)
+        first = (first_kept + first_core.astype(f32)).astype(bf16)
+        send_x = (quad(2, 0, cut) + rest_y[:cut].astype(f32)).astype(bf16)
+        send_y = (quad(1, cut, nz) + rest_x[:cut].astype(f32)).astype(bf16)
+        gate_grads, first, send_x, send_y, output, midscale_grad, off_grad, shift_0, shift_1 = tied(
+            gate_grads, first, send_x, send_y, output, midscale_grad, off_grad, shift_0, shift_1
+        )
+        gate_x, gate_y = swap(first[:nz], wires.x), swap(first[nz:], wires.y)
+        rest_xx, rest_yy = swap(send_x, wires.x), swap(send_y, wires.y)
         tokens_grad, prescale_grad = inputs_back(
             zero, inputs, gain_one, residual_grad, gate_grads, gate_list, gate_lists, gate_size
         )
-        block_output = sequential(output)
-        corner_a, corner_b, rest_x, rest_y, tokens_grad, prescale_grad, block_output = tied(
-            corner_a, corner_b, rest_x, rest_y, tokens_grad, prescale_grad, block_output
-        )
-
-        def side(k, low, high):
-            part = slice(k * nz + low, k * nz + high)
-            return gate_kept[part] + others_core[part].astype(f32)
-
-        send_x = jnp.concatenate([side(2, 0, cut) + corner_a.astype(f32), side(2, cut, nz)]).astype(bf16)
-        send_y = jnp.concatenate([side(1, 0, cut), side(1, cut, nz) + corner_b.astype(f32)]).astype(bf16)
-        send_x, send_y, prescale_grad, rest_x, rest_y = tied(send_x, send_y, prescale_grad, rest_x, rest_y)
-        gate_x, gate_y = swap(send_x, wires.x), swap(send_y, wires.y)
-        rest_kept, rest_came = wires.line_start(quad(0, 0, nz) + rest_x.astype(f32) + rest_y.astype(f32))
+        tokens_grad, prescale_grad, gate_x, gate_y, rest_xx, rest_yy = tied(
+            tokens_grad, prescale_grad, gate_x, gate_y, rest_xx, rest_yy
+        )
+
+        def second(low, high):
+            return second_kept[low:high] + second_core[low:high].astype(f32)
+
+        send_x = (second(0, cut) + gate_y[:cut].astype(f32)).astype(bf16)
+        send_y = (second(cut, nz) + gate_x[:cut].astype(f32)).astype(bf16)
+        send_x, send_y, rest_xx, rest_yy = tied(send_x, send_y, rest_xx, rest_yy)
+        gate_xx, gate_yy = swap(send_x, wires.x), swap(send_y, wires.y)
+
+        def met(x_way, y_way, xx_way, yy_way):
+            low_half = y_way[cut:].astype(f32) + xx_way.astype(f32)
+            return jnp.concatenate([low_half, x_way[cut:].astype(f32) + yy_way.astype(f32)])
+
+        rest_part = quad(0, 0, nz) + met(rest_x, rest_y, rest_xx, rest_yy)
+        rest_part, output, prescale_grad = tied(rest_part, output, prescale_grad)
+        rest_kept, rest_came = wires.line_start(rest_part)
         vectors = vector_rows(
             me, lane_masks, sizes, count, off_grad, shift_0, shift_1, prescale_grad, midscale_grad
         )
-        gate_x, gate_y, tokens_grad, vectors, rest_came[0], rest_came[1] = tied(
-            gate_x, gate_y, tokens_grad, vectors, rest_came[0], rest_came[1]
-        )
-        gate_part = side(0, 0, nz) + gate_x.astype(f32) + gate_y.astype(f32)
+        gate_xx, gate_yy, vectors = tied(gate_xx, gate_yy, vectors)
+        gate_part = second(nz, 2 * nz) + met(gate_x, gate_y, gate_xx, gate_yy)
+        gate_part, tokens_grad, vectors, output = tied(gate_part, tokens_grad, vectors, output)
         gate_kept, gate_came = wires.line_start(gate_part)
         vectors = lax.all_to_all(vectors, AXES, 0, 0, tiled=True)
-        tokens_grad = sequential(tokens_grad)
-        tokens_grad, vectors, block_output, rest_kept, rest_came, gate_kept, gate_came = tied(
-            tokens_grad, vectors, block_output, rest_kept, rest_came, gate_kept, gate_came
+        tokens_grad = sequential(tokens_grad, FILLER)
+        tokens_grad, output = tied(tokens_grad, output)
+        block_output = sequential(output, QUICK)
+        tokens_grad, block_output, vectors, gate_came, rest_came = tied(
+            tokens_grad, block_output, vectors, gate_came, rest_came
+        )
+        vectors = jnp.sum(vectors, axis=0)
+        vector_parts = [vectors[at : at + size] for at, size in zip(range(0, 512, 128), (*sizes, thin))]
+        tokens_grad, vector_parts, block_output, rest_kept, rest_came, gate_kept, gate_came = tied(
+            tokens_grad, vector_parts, block_output, rest_kept, rest_came, gate_kept, gate_came
         )
         rest_part = wires.line_end(rest_kept, rest_came)[0]
         gate_part = wires.line_end(gate_kept, gate_came)[0]
-        vectors = jnp.sum(vectors, axis=0)
-        offsets_part, shifts_part, prescale_part, midscale_part = (
-            vectors[at : at + size] for at, size in zip(range(0, 512, 128), (*sizes, thin))
-        )
+        offsets_part, shifts_part, prescale_part, midscale_part = vector_parts
         return (
             block_output,
             tokens_grad,

time: 196 us -> 179 us (0.913)
  waiting for transfers between devices: 40.9 us -> 32.5 us
  other arithmetic: 13.5 us -> 8.42 us
  local copies, waits for them, and re-layouts: 13.4 us -> 9.7 us
    ppermute x43, waiting for transfers between devices: 40.9 us -> 32.5 us  [swap(): return lax.ppermute(value, AXES, [(i, i ^ mask) for i in range(self.count)])]
    another operation x6 -> x2, other arithmetic: 4.9 us -> 0.13 us
    slice x11 -> x1, local copies, waits for them, and re-layouts: 3.04 us -> 0.05 us  [shards(): gate_x, gate_y = (swap(first[:nz], wires.x), swap(first[nz:], wires.y))]
    concatenate x1 -> x0, local copies, waits for them, and re-layouts: 2.48 us -> none  [shards(): rows = jnp.concatenate([one[:, taken] for one in gate_list])]
  transfers between devices with their start and end apart: 44 -> 44, of which waited for: 13 -> 14; matrix products, arithmetic and copies ran while one was open for 9% -> 4% of each run, Pallas kernels for 44% -> 48%
where the time goes in v2:
time: 179 us; the launch traced here: 178 us
  Pallas kernels  85.3 us (48%)
  starting transfers between devices  41 us (23%)
  waiting for transfers between devices  32.5 us (18%)
  local copies, waits for them, and re-layouts  9.7 us (5%)
  other arithmetic  8.42 us (5%)
    ppermute x43, starting transfers between devices, swap(): return lax.ppermute(value, AXES, [(i, i ^ mask) for i in range(self.count)])  37.9 us
    ppermute x43, waiting for transfers between devices, swap(): return lax.ppermute(value, AXES, [(i, i ^ mask) for i in range(self.count)])  32.5 us
    pallas_call x1, Pallas kernels, ffn_second(): pl.pallas_call(partial(second_kernel, plans, len(own)), in_specs=[SCALAR,...  16.4 us
    pallas_call x1, Pallas kernels, back(): pl.pallas_call(partial(back_kernel, lists, size, skip, plans), grid=(hidd...  15.6 us
    pallas_call x1, Pallas kernels, ffn_first(): pl.pallas_call(partial(first_kernel, lists, size, skip), in_specs=[SCALAR...  14.4 us
    pallas_call x1, Pallas kernels, gates(): pl.pallas_call(partial(gates_kernel, lists, size, taken, len(row_arrays),...  13 us
    pallas_call x1, Pallas kernels, inputs_back(): pl.pallas_call(partial(inputs_kernel, lists, size), in_specs=[SCALAR, WHO...  11 us
    pallas_call x2, Pallas kernels, sequential(): pl.pallas_call(sequence_kernel, out_shape=jax.ShapeDtypeStruct(values.sha...  6.35 us
  transfers between devices with their start and end apart: 44, of which 14 were waited for; matrix products, arithmetic and copies ran while one was open for 4% of the time, Pallas kernels for 48%

profile of v2, /device:TPU:0, one launch (start us, length us, event | category | flops | bytes accessed | tf_op | source)
XLA Modules:
  0.0 178.2 jit_solution(1578357671039511092)
XLA Ops:
  2.4 5.1 %collective-permute-start.2 = (bf16[1,136,512]{2,1,0:T(8,128)(2,1)S(1)}, bf16[1,136,512]{2,1,0:T(8,128)(2,1)S(1)}, u32[]{:S(2)}, u32[]{:S(2)}) collective-permute-start(bf16[1,136,512]{2,1,0:T(8,128)(2,1)S(1)} %fusion.7), channel_id=1, source_target_pairs={{0,6},{1,7},{2,4},{3,5},{4,2},{5,3},{6,0},{7,1},{8,14},{9,15},{10,... | collective-permute-start | bytes 417800 | tf_op jit(solution)/shard_map/ppermute | solution.py:651
  8.1 2.9 %interleave.2.inputs.inputs_h = bf16[1024,512]{1,0:T(8,128)(2,1)} custom-call(bf16[1024,512]{1,0:T(8,128)(2,1)} %values.1), custom_call_target="tpu_custom_call" | custom-call | flops 1000 | bytes 1000 | tf_op jit(solution)/shard_map/interleave/pallas_call | solution.py:48
  12.1 7.2 %collective-permute-done.1 = bf16[1,136,512]{2,1,0:T(8,128)(2,1)S(1)} collective-permute-done((bf16[1,136,512]{2,1,0:T(8,128)(2,1)S(1)}, bf16[1,136,512]{2,1,0:T(8,128)(2,1)S(1)}, u32[]{:S(2)}, u32[]{:S(2)}) %collective-permute-start.1) | collective-permute-done | bytes 139296 | tf_op jit(solution)/shard_map/ppermute | solution.py:651
  19.3 1.6 collective-permute-start.6
  22.4 2.5 %collective-permute-start.5 = (bf16[1,128,512]{2,1,0:T(8,128)(2,1)S(1)}, bf16[1,128,512]{2,1,0:T(8,128)(2,1)S(1)}, u32[]{:S(2)}, u32[]{:S(2)}) collective-permute-start(bf16[1,128,512]{2,1,0:T(8,128)(2,1)S(1)} %maximum_bitcast_fusion), channel_id=1, source_target_pairs={{0,6},{1,7},{2,4},{3,5},{4,2},{5,3},{6,0},{7,1},{8,14},{9,15},{10,... | collective-permute-start | bytes 393224 | tf_op jit(solution)/shard_map/ppermute | solution.py:651
  25.9 3.0 %interleave.3.cotangent_h = bf16[1024,512]{1,0:T(8,128)(2,1)} custom-call(bf16[1024,512]{1,0:T(8,128)(2,1)} %values.2), custom_call_target="tpu_custom_call" | custom-call | flops 1000 | bytes 1000 | tf_op jit(solution)/shard_map/interleave/pallas_call | solution.py:48
  28.9 4.2 %collective-permute-done.6.refs_2_.refs_12_ = bf16[4,136,512]{2,1,0:T(8,128)(2,1)S(1)} collective-permute-done((bf16[4,136,512]{2,1,0:T(8,128)(2,1)S(1)}, bf16[4,136,512]{2,1,0:T(8,128)(2,1)S(1)}, u32[]{:S(2)}, u32[]{:S(2)}) %collective-permute-start.6) | collective-permute-done | bytes 557088 | tf_op jit(solution)/shard_map/ppermute | solution.py:651
  37.7 2.6 %collective-permute-done.9.refs_4_.refs_14_ = bf16[2,136,512]{2,1,0:T(8,128)(2,1)S(1)} collective-permute-done((bf16[2,136,512]{2,1,0:T(8,128)(2,1)S(1)}, bf16[2,136,512]{2,1,0:T(8,128)(2,1)S(1)}, u32[]{:S(2)}, u32[]{:S(2)}) %collective-permute-start.9) | collective-permute-done | bytes 278560 | tf_op jit(solution)/shard_map/ppermute | solution.py:651
  40.3 3.2 %collective-permute-done.8.refs_3_.refs_13_ = bf16[2,136,512]{2,1,0:T(8,128)(2,1)S(1)} collective-permute-done((bf16[2,136,512]{2,1,0:T(8,128)(2,1)S(1)}, bf16[2,136,512]{2,1,0:T(8,128)(2,1)S(1)}, u32[]{:S(2)}, u32[]{:S(2)}) %collective-permute-start.8) | collective-permute-done | bytes 278560 | tf_op jit(solution)/shard_map/ppermute | solution.py:651
  46.7 13.0 %gates.1 = (bf16[1024,512]{1,0:T(8,128)(2,1)}, f32[1024,1024]{1,0:T(8,128)}, bf16[1024,1024]{1,0:T(8,128)(2,1)}, bf16[1024,1024]{1,0:T(8,128)(2,1)}, bf16[1024,1...) custom-call(s32[2]{0:T(128)} %pad_add_fusion.me, ...), custom_call_target="tpu_custom_call" | custom-call | flops 99999997952 | bytes 100000000 | tf_op jit(solution)/shard_map/gates/pallas_call | solution.py:273
  65.1 14.4 %ffn_first.1 = (f32[1024,512]{1,0:T(8,128)}, bf16[1024,512]{1,0:T(8,128)(2,1)}, f32[1024,512]{1,0:T(8,128)}, f32[1024,512]{1,0:T(8,128)}, bf16[8,128,512]{2,1,0:...) custom-call(s32[1]{0:T(128)} %bitcast.me, f32[1,512]{1,0:T(1,128)} %get-tuple-element.151.gain, ...), custom_call_target="tpu_custom_call" | custom-call | flops 99999997952 | bytes 100000000 | tf_op jit(solution)/shard_map/ffn_first/pallas_call | solution.py:433
  80.6 1.6 collective-permute-done.22.refs_4_
  83.9 16.4 %ffn_second.1 = (bf16[1024,512]{1,0:T(8,128)(2,1)}, f32[1024,512]{1,0:T(8,128)}, bf16[1024,512]{1,0:T(8,128)(2,1)}, f32[1,512]{1,0:T(1,128)}, bf16[8,128,512]{2,...) custom-call(s32[1]{0:T(128)} %bitcast.me, ...), custom_call_target="tpu_custom_call" | custom-call | flops 99999997952 | bytes 100000000 | tf_op jit(solution)/shard_map/ffn_second/pallas_call | solution.py:474
  101.1 2.9 %collective-permute-done.26 = bf16[16,32,512]{2,1,0:T(8,128)(2,1)S(1)} collective-permute-done((bf16[16,32,512]{2,1,0:T(8,128)(2,1)}, bf16[16,32,512]{2,1,0:T(8,128)(2,1)S(1)}, u32[]{:S(2)}, u32[]{:S(2)}) %collective-permute-start.26) | collective-permute-done | bytes 524320 | tf_op jit(solution)/shard_map/ppermute | solution.py:651
  106.5 15.6 %back.1 = (bf16[3,1024,1024]{2,1,0:T(8,128)(2,1)}, f32[3,1024]{1,0:T(4,128)}, f32[8,96,512]{2,1,0:T(8,128)}, f32[8,96,512]{2,1,0:T(8,128)}, bf16[8,96,512]{2,1,0:T(8,128)(2,1)}, /*index=5*/bf16[8,96,512]{2,1,0:T(8,128)(2,1)}) custom-call(s32[1]{0:T(128)} %bitcast.me, bf16[1024,512]{1,0:T(8,128)(2,1)} %get-tuple-element.193.rounded, ...), custom_call_target="tpu_custom_call" | custom-call | flops 99999997952 | bytes 100000000 | tf_op jit(solution)/shard_map/back/pallas_call | solution.py:578
  129.5 11.0 %inputs_back.1 = (f32[1024,512]{1,0:T(8,128)}, f32[1,512]{1,0:T(1,128)}) custom-call(s32[1]{0:T(128)} %bitcast.me, bf16[1024,512]{1,0:T(8,128)(2,1)} %interleave.2.inputs.inputs_h, f32[1,512]{1,0:T(1,128)} %get-tuple-element.208.gain, f32[1024,512]{1,0:T(8,128)} %get-tuple-element.209.back, bf16[3,1024,1024]{2,1,0:T(8,128)(2,1)} %get-tuple-element.220.grads_h, ...), custom_call_target="tpu_custom_call" | custom-call | flops 99999997952 | bytes 100000000 | tf_op jit(solution)/shard_map/inputs_back/pallas_call | solution.py:624
  140.6 4.1 %collective-permute-done.32 = bf16[4,96,512]{2,1,0:T(8,128)(2,1)S(1)} collective-permute-done((bf16[4,96,512]{2,1,0:T(8,128)(2,1)S(1)}, bf16[4,96,512]{2,1,0:T(8,128)(2,1)S(1)}, u32[]{:S(2)}, u32[]{:S(2)}) %collective-permute-start.32) | collective-permute-done | bytes 393248 | tf_op jit(solution)/shard_map/ppermute | solution.py:651
  149.7 2.8 %collective-permute-start.40 = (bf16[1,160,512]{2,1,0:T(8,128)(2,1)}, bf16[1,160,512]{2,1,0:T(8,128)(2,1)}, u32[]{:S(2)}, u32[]{:S(2)}) collective-permute-start(bf16[1,160,512]{2,1,0:T(8,128)(2,1)} %get-tuple-element.294), channel_id=1, source_target_pairs={{0,2},{1,3},{2,0},{3,1},{4,6},{5,7},{6,4},{7,5},{8,10},{9,11},{10,... | collective-permute-start | bytes 491528 | tf_op jit(solution)/shard_map/ppermute | solution.py:651
  152.5 2.7 %vectors.1 = f32[32,512]{1,0:T(8,128)} custom-call(s32[1]{0:T(128)} %bitcast.me, s32[1,2048]{1,0:T(1,128)} %constant.20.clone.lane_masks.masks, f32[3,1024]{1,0:T(4,128)} %get-tuple-element.232.offsets, f32[1,1024]{1,0:T(1,128)} %get-tuple-element.233.shift_0, f32[1,1024]{1,0:T(1,128)} %get-tuple-element.234.shift_1, f32[1,512]{1,0:T(1,128)} %get-tuple-element.239.prescale, ...), custom_call_target="tpu_custom_call" | custom-call | flops 99999997952 | bytes 100000000 | tf_op jit(solution)/shard_map/vectors/pallas_call | solution.py:171
  156.8 3.1 %all-to-all-start = ((f32[32,1,512]{2,1,0:T(1,128)}), f32[32,1,512]{2,1,0:T(1,128)S(1)}, u32[]{:S(2)}, u32[]{:S(2)}) async-start(f32[32,1,512]{2,1,0:T(1,128)} %copy.22), calls=%async_computation | async-start | bytes 131072 | tf_op jit(solution)/shard_map/all_to_all | solution.py:864
  160.0 3.7 %collective-permute-start.39 = (bf16[1,96,512]{2,1,0:T(8,128)(2,1)S(1)}, bf16[1,96,512]{2,1,0:T(8,128)(2,1)S(1)}, u32[]{:S(2)}, u32[]{:S(2)}) collective-permute-start(bf16[1,96,512]{2,1,0:T(8,128)(2,1)S(1)} %get-tuple-element.295), channel_id=1, source_target_pairs={{0,6},{1,7},{2,4},{3,5},{4,2},{5,3},{6,0},{7,1},{8,14},{9,15},{10,... | collective-permute-start | bytes 294920 | tf_op jit(solution)/shard_map/ppermute | solution.py:651
  164.5 3.6 %sequence.2 = f32[1024,512]{1,0:T(8,128)} custom-call(f32[1024,512]{1,0:T(8,128)} %get-tuple-element.246.values), custom_call_target="tpu_custom_call" | custom-call | flops 99999997952 | bytes 100000000 | tf_op jit(solution)/shard_map/sequence/pallas_call | solution.py:68
  168.0 2.8 %sequence.3 = bf16[1024,512]{1,0:T(8,128)(2,1)} custom-call(bf16[1024,512]{1,0:T(8,128)(2,1)} %get-tuple-element.249.values), custom_call_target="tpu_custom_call" | custom-call | flops 1000 | bytes 1000 | tf_op jit(solution)/shard_map/sequence/pallas_call | solution.py:68
  170.9 2.6 %collective-permute-done.38 = bf16[1,96,512]{2,1,0:T(8,128)(2,1)S(1)} collective-permute-done((bf16[1,96,512]{2,1,0:T(8,128)(2,1)S(1)}, bf16[1,96,512]{2,1,0:T(8,128)(2,1)S(1)}, u32[]{:S(2)}, u32[]{:S(2)}) %collective-permute-start.38) | collective-permute-done | bytes 98336 | tf_op jit(solution)/shard_map/ppermute | solution.py:651
  (190 shorter events, 44.4 us)
Async XLA Ops:
  7.5 11.8 %collective-permute-start.1 = (bf16[1,136,512]{2,1,0:T(8,128)(2,1)S(1)}, bf16[1,136,512]{2,1,0:T(8,128)(2,1)S(1)}, u32[]{:S(2)}, u32[]{:S(2)}) collective-permute-start(bf16[1,136,512]{2,1,0:T(8,128)(2,1)S(1)} %fusion.7), channel_id=1, source_target_pairs={{0,4},{1,5},{2,6},{3,7},{4,0},{5,1},{6,2},{7,3},{8,12},{9,13},{10,... | collective-permute-start | bytes 417800 | tf_op jit(solution)/shard_map/ppermute | solution.py:651
  7.5 11.8 %collective-permute-start = (bf16[1,136,512]{2,1,0:T(8,128)(2,1)S(1)}, bf16[1,136,512]{2,1,0:T(8,128)(2,1)S(1)}, u32[]{:S(2)}, u32[]{:S(2)}) collective-permute-start(bf16[1,136,512]{2,1,0:T(8,128)(2,1)S(1)} %fusion.7), channel_id=1, source_target_pairs={{0,2},{1,3},{2,0},{3,1},{4,6},{5,7},{6,4},{7,5},{8,10},{9,11},{10,... | collective-permute-start | bytes 417800 | tf_op jit(solution)/shard_map/ppermute | solution.py:651
  19.3 13.7 %collective-permute-start.6 = (bf16[4,136,512]{2,1,0:T(8,128)(2,1)S(1)}, bf16[4,136,512]{2,1,0:T(8,128)(2,1)S(1)}, u32[]{:S(2)}, u32[]{:S(2)}) collective-permute-start(bf16[4,136,512]{2,1,0:T(8,128)(2,1)S(1)} %pad_maximum_fusion.refs_0_.refs_10_), channel_id=1, source_target_pairs={{0,1},{1,0},{2,3},{3,2},{4,5},{5,4},{6,7},{7,6},{8,9},{9,8},{10,11... | collective-permute-start | bytes 1671176 | tf_op jit(solution)/shard_map/ppermute | solution.py:651
  20.9 15.1 %collective-permute-start.3 = (bf16[4,136,512]{2,1,0:T(8,128)(2,1)S(1)}, bf16[4,136,512]{2,1,0:T(8,128)(2,1)S(1)}, u32[]{:S(2)}, u32[]{:S(2)}) collective-permute-start(bf16[4,136,512]{2,1,0:T(8,128)(2,1)S(1)} %pad_maximum_fusion.refs_0_.refs_10_), channel_id=1, source_target_pairs={{0,16},{1,17},{2,18},{3,19},{4,20},{5,21},{6,22},{7,23},{8,24},{9,... | collective-permute-start | bytes 1671176 | tf_op jit(solution)/shard_map/ppermute | solution.py:651
  22.4 12.3 %collective-permute-start.5 = (bf16[1,128,512]{2,1,0:T(8,128)(2,1)S(1)}, bf16[1,128,512]{2,1,0:T(8,128)(2,1)S(1)}, u32[]{:S(2)}, u32[]{:S(2)}) collective-permute-start(bf16[1,128,512]{2,1,0:T(8,128)(2,1)S(1)} %maximum_bitcast_fusion), channel_id=1, source_target_pairs={{0,6},{1,7},{2,4},{3,5},{4,2},{5,3},{6,0},{7,1},{8,14},{9,15},{10,... | collective-permute-start | bytes 393224 | tf_op jit(solution)/shard_map/ppermute | solution.py:651
  24.9 11.1 %collective-permute-start.4 = (bf16[1,128,512]{2,1,0:T(8,128)(2,1)S(1)}, bf16[1,128,512]{2,1,0:T(8,128)(2,1)S(1)}, u32[]{:S(2)}, u32[]{:S(2)}) collective-permute-start(bf16[1,128,512]{2,1,0:T(8,128)(2,1)S(1)} %maximum_bitcast_fusion), channel_id=1, source_target_pairs={{0,4},{1,5},{2,6},{3,7},{4,0},{5,1},{6,2},{7,3},{8,12},{9,13},{10,... | collective-permute-start | bytes 393224 | tf_op jit(solution)/shard_map/ppermute | solution.py:651
  43.5 16.2 %collective-permute-start.17 = (bf16[4,128,512]{2,1,0:T(8,128)(2,1)S(1)}, bf16[4,128,512]{2,1,0:T(8,128)(2,1)S(1)}, u32[]{:S(2)}, u32[]{:S(2)}) collective-permute-start(bf16[4,128,512]{2,1,0:T(8,128)(2,1)S(1)} %constant_dynamic-update-slice_fusion.refs_10_), channel_id=1, source_target_pairs={{0,8},{1,9},{2,10},{3,11},{4,12},{5,13},{6,14},{7,15},{8,0},{9,1},... | collective-permute-start | bytes 1572872 | tf_op jit(solution)/shard_map/ppermute | solution.py:651
  44.1 15.6 %collective-permute-start.16 = (bf16[4,128,512]{2,1,0:T(8,128)(2,1)S(1)}, bf16[4,128,512]{2,1,0:T(8,128)(2,1)S(1)}, u32[]{:S(2)}, u32[]{:S(2)}) collective-permute-start(bf16[4,128,512]{2,1,0:T(8,128)(2,1)S(1)} %constant_dynamic-update-slice_fusion.refs_10_), channel_id=1, source_target_pairs={{0,16},{1,17},{2,18},{3,19},{4,20},{5,21},{6,22},{7,23},{8,24},{9,... | collective-permute-start | bytes 1572872 | tf_op jit(solution)/shard_map/ppermute | solution.py:651
  44.7 15.1 %collective-permute-start.15 = (bf16[4,128,512]{2,1,0:T(8,128)(2,1)S(1)}, bf16[4,128,512]{2,1,0:T(8,128)(2,1)S(1)}, u32[]{:S(2)}, u32[]{:S(2)}) collective-permute-start(bf16[4,128,512]{2,1,0:T(8,128)(2,1)S(1)} %constant_dynamic-update-slice_fusion.refs_10_), channel_id=1, source_target_pairs={{0,1},{1,0},{2,3},{3,2},{4,5},{5,4},{6,7},{7,6},{8,9},{9,8},{10,11... | collective-permute-start | bytes 1572872 | tf_op jit(solution)/shard_map/ppermute | solution.py:651
  59.9 19.6 %collective-permute-start.20 = (bf16[2,128,512]{2,1,0:T(8,128)(2,1)S(1)}, bf16[2,128,512]{2,1,0:T(8,128)(2,1)S(1)}, u32[]{:S(2)}, u32[]{:S(2)}) collective-permute-start(bf16[2,128,512]{2,1,0:T(8,128)(2,1)S(1)} %slice.177), channel_id=1, source_target_pairs={{0,16},{1,17},{2,18},{3,19},{4,20},{5,21},{6,22},{7,23},{8,24},{9,... | collective-permute-start | bytes 786440 | tf_op jit(solution)/shard_map/ppermute | solution.py:651
  61.5 18.1 %collective-permute-start.19 = (bf16[2,128,512]{2,1,0:T(8,128)(2,1)S(1)}, bf16[2,128,512]{2,1,0:T(8,128)(2,1)S(1)}, u32[]{:S(2)}, u32[]{:S(2)}) collective-permute-start(bf16[2,128,512]{2,1,0:T(8,128)(2,1)S(1)} %slice.176), channel_id=1, source_target_pairs={{0,1},{1,0},{2,3},{3,2},{4,5},{5,4},{6,7},{7,6},{8,9},{9,8},{10,11... | collective-permute-start | bytes 786440 | tf_op jit(solution)/shard_map/ppermute | solution.py:651
  80.2 20.1 %collective-permute-start.24 = (bf16[8,128,512]{2,1,0:T(8,128)(2,1)}, bf16[8,128,512]{2,1,0:T(8,128)(2,1)S(1)}, u32[]{:S(2)}, u32[]{:S(2)}) collective-permute-start(bf16[8,128,512]{2,1,0:T(8,128)(2,1)} %get-tuple-element.185), channel_id=1, source_target_pairs={{0,8},{1,9},{2,10},{3,11},{4,12},{5,13},{6,14},{7,15},{8,0},{9,1},... | collective-permute-start | bytes 3145736 | tf_op jit(solution)/shard_map/ppermute | solution.py:651
  105.4 16.8 %collective-permute-start.27 = (bf16[4,160,512]{2,1,0:T(8,128)(2,1)S(1)}, bf16[4,160,512]{2,1,0:T(8,128)(2,1)S(1)}, u32[]{:S(2)}, u32[]{:S(2)}) collective-permute-start(bf16[4,160,512]{2,1,0:T(8,128)(2,1)S(1)} %get-tuple-element.204), channel_id=1, source_target_pairs={{0,16},{1,17},{2,18},{3,19},{4,20},{5,21},{6,22},{7,23},{8,24},{9,... | collective-permute-start | bytes 1966088 | tf_op jit(solution)/shard_map/ppermute | solution.py:651
  106.0 16.5 %collective-permute-start.28 = (bf16[4,160,512]{2,1,0:T(8,128)(2,1)S(1)}, bf16[4,160,512]{2,1,0:T(8,128)(2,1)S(1)}, u32[]{:S(2)}, u32[]{:S(2)}) collective-permute-start(bf16[4,160,512]{2,1,0:T(8,128)(2,1)S(1)} %get-tuple-element.205), channel_id=1, source_target_pairs={{0,1},{1,0},{2,3},{3,2},{4,5},{5,4},{6,7},{7,6},{8,9},{9,8},{10,11... | collective-permute-start | bytes 1966088 | tf_op jit(solution)/shard_map/ppermute | solution.py:651
  123.8 21.0 %collective-permute-start.29 = (bf16[8,96,512]{2,1,0:T(8,128)(2,1)}, bf16[8,96,512]{2,1,0:T(8,128)(2,1)S(1)}, u32[]{:S(2)}, u32[]{:S(2)}) collective-permute-start(bf16[8,96,512]{2,1,0:T(8,128)(2,1)} %get-tuple-element.207), channel_id=1, source_target_pairs={{0,8},{1,9},{2,10},{3,11},{4,12},{5,13},{6,14},{7,15},{8,0},{9,1},... | collective-permute-start | bytes 2359304 | tf_op jit(solution)/shard_map/ppermute | solution.py:651
  125.3 15.3 %collective-permute-start.33 = (bf16[2,160,512]{2,1,0:T(8,128)(2,1)S(1)}, bf16[2,160,512]{2,1,0:T(8,128)(2,1)S(1)}, u32[]{:S(2)}, u32[]{:S(2)}) collective-permute-start(bf16[2,160,512]{2,1,0:T(8,128)(2,1)S(1)} %fusion), channel_id=1, source_target_pairs={{0,16},{1,17},{2,18},{3,19},{4,20},{5,21},{6,22},{7,23},{8,24},{9,... | collective-permute-start | bytes 983048 | tf_op jit(solution)/shard_map/ppermute | solution.py:651
  126.9 13.7 %collective-permute-start.34 = (bf16[2,160,512]{2,1,0:T(8,128)(2,1)S(1)}, bf16[2,160,512]{2,1,0:T(8,128)(2,1)S(1)}, u32[]{:S(2)}, u32[]{:S(2)}) collective-permute-start(bf16[2,160,512]{2,1,0:T(8,128)(2,1)S(1)} %fusion.1), channel_id=1, source_target_pairs={{0,1},{1,0},{2,3},{3,2},{4,5},{5,4},{6,7},{7,6},{8,9},{9,8},{10,11... | collective-permute-start | bytes 983048 | tf_op jit(solution)/shard_map/ppermute | solution.py:651
  128.1 16.6 %collective-permute-start.32 = (bf16[4,96,512]{2,1,0:T(8,128)(2,1)S(1)}, bf16[4,96,512]{2,1,0:T(8,128)(2,1)S(1)}, u32[]{:S(2)}, u32[]{:S(2)}) collective-permute-start(bf16[4,96,512]{2,1,0:T(8,128)(2,1)S(1)} %get-tuple-element.290), channel_id=1, source_target_pairs={{0,1},{1,0},{2,3},{3,2},{4,5},{5,4},{6,7},{7,6},{8,9},{9,8},{10,11... | collective-permute-start | bytes 1179656 | tf_op jit(solution)/shard_map/ppermute | solution.py:651
  129.0 15.8 %collective-permute-start.31 = (bf16[4,96,512]{2,1,0:T(8,128)(2,1)S(1)}, bf16[4,96,512]{2,1,0:T(8,128)(2,1)S(1)}, u32[]{:S(2)}, u32[]{:S(2)}) collective-permute-start(bf16[4,96,512]{2,1,0:T(8,128)(2,1)S(1)} %get-tuple-element.291), channel_id=1, source_target_pairs={{0,16},{1,17},{2,18},{3,19},{4,20},{5,21},{6,22},{7,23},{8,24},{9,... | collective-permute-start | bytes 1179656 | tf_op jit(solution)/shard_map/ppermute | solution.py:651
  148.1 15.6 %collective-permute-start.42 = (bf16[1,160,512]{2,1,0:T(8,128)(2,1)S(1)}, bf16[1,160,512]{2,1,0:T(8,128)(2,1)S(1)}, u32[]{:S(2)}, u32[]{:S(2)}) collective-permute-start(bf16[1,160,512]{2,1,0:T(8,128)(2,1)S(1)} %get-tuple-element.292), channel_id=1, source_target_pairs={{0,6},{1,7},{2,4},{3,5},{4,2},{5,3},{6,0},{7,1},{8,14},{9,15},{10,... | collective-permute-start | bytes 491528 | tf_op jit(solution)/shard_map/ppermute | solution.py:651
  149.7 21.2 %collective-permute-start.41 = (bf16[1,160,512]{2,1,0:T(8,128)(2,1)}, bf16[1,160,512]{2,1,0:T(8,128)(2,1)}, u32[]{:S(2)}, u32[]{:S(2)}) collective-permute-start(bf16[1,160,512]{2,1,0:T(8,128)(2,1)} %get-tuple-element.293), channel_id=1, source_target_pairs={{0,4},{1,5},{2,6},{3,7},{4,0},{5,1},{6,2},{7,3},{8,12},{9,13},{10,... | collective-permute-start | bytes 491528 | tf_op jit(solution)/shard_map/ppermute | solution.py:651
  149.7 21.2 %collective-permute-start.40 = (bf16[1,160,512]{2,1,0:T(8,128)(2,1)}, bf16[1,160,512]{2,1,0:T(8,128)(2,1)}, u32[]{:S(2)}, u32[]{:S(2)}) collective-permute-start(bf16[1,160,512]{2,1,0:T(8,128)(2,1)} %get-tuple-element.294), channel_id=1, source_target_pairs={{0,2},{1,3},{2,0},{3,1},{4,6},{5,7},{6,4},{7,5},{8,10},{9,11},{10,... | collective-permute-start | bytes 491528 | tf_op jit(solution)/shard_map/ppermute | solution.py:651
  156.8 14.0 %all-to-all-start = ((f32[32,1,512]{2,1,0:T(1,128)}), f32[32,1,512]{2,1,0:T(1,128)S(1)}, u32[]{:S(2)}, u32[]{:S(2)}) async-start(f32[32,1,512]{2,1,0:T(1,128)} %copy.22), calls=%async_computation | async-start | bytes 131072 | tf_op jit(solution)/shard_map/all_to_all | solution.py:864
  160.0 10.9 %collective-permute-start.39 = (bf16[1,96,512]{2,1,0:T(8,128)(2,1)S(1)}, bf16[1,96,512]{2,1,0:T(8,128)(2,1)S(1)}, u32[]{:S(2)}, u32[]{:S(2)}) collective-permute-start(bf16[1,96,512]{2,1,0:T(8,128)(2,1)S(1)} %get-tuple-element.295), channel_id=1, source_target_pairs={{0,6},{1,7},{2,4},{3,5},{4,2},{5,3},{6,0},{7,1},{8,14},{9,15},{10,... | collective-permute-start | bytes 294920 | tf_op jit(solution)/shard_map/ppermute | solution.py:651
  (55 other events, 328.0 us)

commit v3 on v2

--- a/solution.py
+++ b/solution.py
@@ -307,13 +307,13 @@
     return x * cdf, slope
 
 
-def ffn_part(part, normed_two, cotangent, shifts, expand, contract, hidden, slope, shift_grad):
+def ffn_part(part, normed_two, cotangent, shifts, base, expand, contract, hidden, slope, shift_grad):
     units = expand.shape[0]
     n2 = normed_two[part]
     ct = cotangent[part]
     for j in range(0, units, 256):
         cols = slice(j, j + 256)
-        act, grad = gelu_both(against(n2, expand[cols]) + shifts[:, cols])
+        act, grad = gelu_both(against(n2, expand[cols]) + shifts[:, base + j : base + j + 256])
         hidden[part, cols] = act.astype(bf16)
         rounded = (against(ct, contract[cols]) * grad).astype(bf16)
         slope[part, cols] = rounded
@@ -366,7 +366,7 @@
     contract = contract[...].reshape(-1, width)
     for part in parts():
         branch[part], grad[part] = ffn_part(
-            part, normed_two, cotangent, shifts, expand, contract, hidden, slope, shift_grad
+            part, normed_two, cotangent, shifts, 0, expand, contract, hidden, slope, shift_grad
         )
         leaving += start([(branch.at[part], branch_h.at[part]), (grad.at[part], grad_h.at[part])], out_sem)
     ffn_grads(normed_two, cotangent, hidden, slope, sent, kept)
@@ -393,7 +393,9 @@
     contract = contract[...].reshape(-1, width)
     leaving = []
     for k, part in enumerate(parts()):
-        one, two = ffn_part(part, normed_two, cotangent, shifts, expand, contract, hidden, slope, shift_grad)
+        one, two = ffn_part(
+            part, normed_two, cotangent, shifts, hidden.shape[1], expand, contract, hidden, slope, shift_grad
+        )
         if k == 0:
             finish(others)
         value = residual[part]
@@ -755,9 +757,8 @@
         normed, share, low, pull_f, pull_i, gain_one, gain_two, all_shifts = gates(
             both, inputs, row_arrays, 0 if unit % 16 else taken, owner_masks, lane_masks, gate_list, gate_lists, gate_size, sizes, hidden
         )
-        shift_halves = jnp.split(all_shifts, 2, axis=1)
         low, rest_y, rest_x, rest_core = tied(low, rest_y, rest_x, rest_core)
-        rest_corner = [swap(rest_x[:cut], wires.y), swap(rest_y[cut:], wires.x)]
+        rest_corner = [swap(rest_x, wires.y)]
 
         def merged(group):
             if not unit % 16:
@@ -773,7 +774,7 @@
             return grads.reshape(2, -1, wide, width).transpose(1, 0, 2, 3).reshape(-1, 2 * wide, width)
 
         residual, normed_two, branch, grad, sent_0, kept_0, shift_0 = ffn_first(
-            zero, gain_two, shift_halves[0], inputs, upstream, low, gate_list, gate_lists, read_size, gate_size, own,
+            zero, gain_two, all_shifts, inputs, upstream, low, gate_list, gate_lists, read_size, gate_size, own,
             ffn_unit,
         )
         residual, normed_two, branch, grad, sent_0, kept_0, shift_0, rest_x, *rest_corner = tied(
@@ -785,7 +786,7 @@
         half = count // 2
         read_plans = [(flat["A"][:half], f32), (flat["A"][half:], bf16)]
         output, residual_grad, rounded, midscale_grad, sent_1, kept_1, shift_1, *read_blocks = ffn_second(
-            zero, gain_two, shift_halves[1], residual, normed_two, branch, grad, upstream, low, own, ffn_unit, unit,
+            zero, gain_two, all_shifts, residual, normed_two, branch, grad, upstream, low, own, ffn_unit, unit,
             None if unit % 16 else read_plans,
         )
         read_kept, read_sent = sorted_blocks(index, read_plans, read_blocks, unit) if unit % 16 else read_blocks

time: 179 us -> 177 us (0.989)
    ppermute x43 -> x41, starting transfers between devices: 37.9 us -> 38.6 us  [swap(): return lax.ppermute(value, AXES, [(i, i ^ mask) for i in range(self.count)])]
    ppermute x43 -> x41, waiting for transfers between devices: 32.5 us -> 31.8 us  [swap(): return lax.ppermute(value, AXES, [(i, i ^ mask) for i in range(self.count)])]
    unnamed x70 -> x66, local copies, waits for them, and re-layouts: 3.88 us -> 3.8 us
  transfers between devices with their start and end apart: 44 -> 42, of which waited for: 14 -> 13; matrix products, arithmetic and copies ran while one was open for 4% -> 3% of each run, Pallas kernels for 48% -> 48%
where the time goes in v3:
time: 177 us; the launch traced here: 176 us
  Pallas kernels  85.2 us (48%)
  starting transfers between devices  41.2 us (23%)
  waiting for transfers between devices  31.8 us (18%)
  other arithmetic  8.43 us (5%)
  local copies, waits for them, and re-layouts  8.28 us (5%)
    ppermute x41, starting transfers between devices, swap(): return lax.ppermute(value, AXES, [(i, i ^ mask) for i in range(self.count)])  38.6 us
    ppermute x41, waiting for transfers between devices, swap(): return lax.ppermute(value, AXES, [(i, i ^ mask) for i in range(self.count)])  31.8 us
    pallas_call x1, Pallas kernels, ffn_second(): pl.pallas_call(partial(second_kernel, plans, len(own)), in_specs=[SCALAR,...  16.3 us
    pallas_call x1, Pallas kernels, back(): pl.pallas_call(partial(back_kernel, lists, size, skip, plans), grid=(hidd...  15.6 us
    pallas_call x1, Pallas kernels, ffn_first(): pl.pallas_call(partial(first_kernel, lists, size, skip), in_specs=[SCALAR...  14.4 us
    pallas_call x1, Pallas kernels, gates(): pl.pallas_call(partial(gates_kernel, lists, size, taken, len(row_arrays),...  13 us
    pallas_call x1, Pallas kernels, inputs_back(): pl.pallas_call(partial(inputs_kernel, lists, size), in_specs=[SCALAR, WHO...  11.1 us
    pallas_call x2, Pallas kernels, sequential(): pl.pallas_call(sequence_kernel, out_shape=jax.ShapeDtypeStruct(values.sha...  6.35 us
  transfers between devices with their start and end apart: 42, of which 13 were waited for; matrix products, arithmetic and copies ran while one was open for 3% of the time, Pallas kernels for 48%

profile of v3, /device:TPU:0, one launch (start us, length us, event | category | flops | bytes accessed | tf_op | source)
XLA Modules:
  0.0 176.2 jit_solution(2495619362070708120)
XLA Ops:
  2.4 5.1 %collective-permute-start.2 = (bf16[1,136,512]{2,1,0:T(8,128)(2,1)S(1)}, bf16[1,136,512]{2,1,0:T(8,128)(2,1)S(1)}, u32[]{:S(2)}, u32[]{:S(2)}) collective-permute-start(bf16[1,136,512]{2,1,0:T(8,128)(2,1)S(1)} %fusion.7), channel_id=1, source_target_pairs={{0,6},{1,7},{2,4},{3,5},{4,2},{5,3},{6,0},{7,1},{8,14},{9,15},{10,... | collective-permute-start | bytes 417800 | tf_op jit(solution)/shard_map/ppermute | solution.py:653
  8.1 2.9 %interleave.2.inputs.inputs_h = bf16[1024,512]{1,0:T(8,128)(2,1)} custom-call(bf16[1024,512]{1,0:T(8,128)(2,1)} %values.1), custom_call_target="tpu_custom_call" | custom-call | flops 1000 | bytes 1000 | tf_op jit(solution)/shard_map/interleave/pallas_call | solution.py:48
  12.1 7.2 %collective-permute-done.1 = bf16[1,136,512]{2,1,0:T(8,128)(2,1)S(1)} collective-permute-done((bf16[1,136,512]{2,1,0:T(8,128)(2,1)S(1)}, bf16[1,136,512]{2,1,0:T(8,128)(2,1)S(1)}, u32[]{:S(2)}, u32[]{:S(2)}) %collective-permute-start.1) | collective-permute-done | bytes 139296 | tf_op jit(solution)/shard_map/ppermute | solution.py:653
  19.3 1.6 collective-permute-start.6
  22.4 2.5 %collective-permute-start.5 = (bf16[1,128,512]{2,1,0:T(8,128)(2,1)S(1)}, bf16[1,128,512]{2,1,0:T(8,128)(2,1)S(1)}, u32[]{:S(2)}, u32[]{:S(2)}) collective-permute-start(bf16[1,128,512]{2,1,0:T(8,128)(2,1)S(1)} %maximum_bitcast_fusion), channel_id=1, source_target_pairs={{0,6},{1,7},{2,4},{3,5},{4,2},{5,3},{6,0},{7,1},{8,14},{9,15},{10,... | collective-permute-start | bytes 393224 | tf_op jit(solution)/shard_map/ppermute | solution.py:653
  25.9 3.0 %interleave.3.cotangent_h = bf16[1024,512]{1,0:T(8,128)(2,1)} custom-call(bf16[1024,512]{1,0:T(8,128)(2,1)} %values.2), custom_call_target="tpu_custom_call" | custom-call | flops 1000 | bytes 1000 | tf_op jit(solution)/shard_map/interleave/pallas_call | solution.py:48
  28.9 4.2 %collective-permute-done.6.refs_2_.refs_12_ = bf16[4,136,512]{2,1,0:T(8,128)(2,1)S(1)} collective-permute-done((bf16[4,136,512]{2,1,0:T(8,128)(2,1)S(1)}, bf16[4,136,512]{2,1,0:T(8,128)(2,1)S(1)}, u32[]{:S(2)}, u32[]{:S(2)}) %collective-permute-start.6) | collective-permute-done | bytes 557088 | tf_op jit(solution)/shard_map/ppermute | solution.py:653
  37.7 2.6 %collective-permute-done.9.refs_4_.refs_14_ = bf16[2,136,512]{2,1,0:T(8,128)(2,1)S(1)} collective-permute-done((bf16[2,136,512]{2,1,0:T(8,128)(2,1)S(1)}, bf16[2,136,512]{2,1,0:T(8,128)(2,1)S(1)}, u32[]{:S(2)}, u32[]{:S(2)}) %collective-permute-start.9) | collective-permute-done | bytes 278560 | tf_op jit(solution)/shard_map/ppermute | solution.py:653
  40.3 3.2 %collective-permute-done.8.refs_3_.refs_13_ = bf16[2,136,512]{2,1,0:T(8,128)(2,1)S(1)} collective-permute-done((bf16[2,136,512]{2,1,0:T(8,128)(2,1)S(1)}, bf16[2,136,512]{2,1,0:T(8,128)(2,1)S(1)}, u32[]{:S(2)}, u32[]{:S(2)}) %collective-permute-start.8) | collective-permute-done | bytes 278560 | tf_op jit(solution)/shard_map/ppermute | solution.py:653
  46.7 13.0 %gates.1 = (bf16[1024,512]{1,0:T(8,128)(2,1)}, f32[1024,1024]{1,0:T(8,128)}, bf16[1024,1024]{1,0:T(8,128)(2,1)}, bf16[1024,1024]{1,0:T(8,128)(2,1)}, bf16[1024,1...) custom-call(s32[2]{0:T(128)} %pad_add_fusion.me, ...), custom_call_target="tpu_custom_call" | custom-call | flops 99999997952 | bytes 100000000 | tf_op jit(solution)/shard_map/gates/pallas_call | solution.py:273
  62.6 14.4 %ffn_first.1 = (f32[1024,512]{1,0:T(8,128)}, bf16[1024,512]{1,0:T(8,128)(2,1)}, f32[1024,512]{1,0:T(8,128)}, f32[1024,512]{1,0:T(8,128)}, bf16[8,128,512]{2,1,0:...) custom-call(s32[1]{0:T(128)} %bitcast.me, f32[1,512]{1,0:T(1,128)} %get-tuple-element.150.gain, ...), custom_call_target="tpu_custom_call" | custom-call | flops 99999997952 | bytes 100000000 | tf_op jit(solution)/shard_map/ffn_first/pallas_call | solution.py:435
  81.3 16.3 %ffn_second.1 = (bf16[1024,512]{1,0:T(8,128)(2,1)}, f32[1024,512]{1,0:T(8,128)}, bf16[1024,512]{1,0:T(8,128)(2,1)}, f32[1,512]{1,0:T(1,128)}, bf16[8,128,512]{2,...) custom-call(s32[1]{0:T(128)} %bitcast.me, ...), custom_call_target="tpu_custom_call" | custom-call | flops 99999997952 | bytes 100000000 | tf_op jit(solution)/shard_map/ffn_second/pallas_call | solution.py:476
  98.3 2.9 %collective-permute-done.24 = bf16[16,32,512]{2,1,0:T(8,128)(2,1)S(1)} collective-permute-done((bf16[16,32,512]{2,1,0:T(8,128)(2,1)}, bf16[16,32,512]{2,1,0:T(8,128)(2,1)S(1)}, u32[]{:S(2)}, u32[]{:S(2)}) %collective-permute-start.24) | collective-permute-done | bytes 524320 | tf_op jit(solution)/shard_map/ppermute | solution.py:653
  105.7 15.6 %back.1 = (bf16[3,1024,1024]{2,1,0:T(8,128)(2,1)}, f32[3,1024]{1,0:T(4,128)}, f32[8,96,512]{2,1,0:T(8,128)}, f32[8,96,512]{2,1,0:T(8,128)}, bf16[8,96,512]{2,1,0:T(8,128)(2,1)}, /*index=5*/bf16[8,96,512]{2,1,0:T(8,128)(2,1)}) custom-call(s32[1]{0:T(128)} %bitcast.me, bf16[1024,512]{1,0:T(8,128)(2,1)} %get-tuple-element.191.rounded, ...), custom_call_target="tpu_custom_call" | custom-call | flops 99999997952 | bytes 100000000 | tf_op jit(solution)/shard_map/back/pallas_call | solution.py:580
  128.4 11.1 %inputs_back.1 = (f32[1024,512]{1,0:T(8,128)}, f32[1,512]{1,0:T(1,128)}) custom-call(s32[1]{0:T(128)} %bitcast.me, bf16[1024,512]{1,0:T(8,128)(2,1)} %interleave.2.inputs.inputs_h, f32[1,512]{1,0:T(1,128)} %get-tuple-element.206.gain, f32[1024,512]{1,0:T(8,128)} %get-tuple-element.207.back, bf16[3,1024,1024]{2,1,0:T(8,128)(2,1)} %get-tuple-element.218.grads_h, ...), custom_call_target="tpu_custom_call" | custom-call | flops 99999997952 | bytes 100000000 | tf_op jit(solution)/shard_map/inputs_back/pallas_call | solution.py:626
  139.6 3.1 %collective-permute-done.30 = bf16[4,96,512]{2,1,0:T(8,128)(2,1)S(1)} collective-permute-done((bf16[4,96,512]{2,1,0:T(8,128)(2,1)S(1)}, bf16[4,96,512]{2,1,0:T(8,128)(2,1)S(1)}, u32[]{:S(2)}, u32[]{:S(2)}) %collective-permute-start.30) | collective-permute-done | bytes 393248 | tf_op jit(solution)/shard_map/ppermute | solution.py:653
  146.6 1.6 collective-permute-start.40
  148.2 2.8 %collective-permute-start.38 = (bf16[1,160,512]{2,1,0:T(8,128)(2,1)}, bf16[1,160,512]{2,1,0:T(8,128)(2,1)}, u32[]{:S(2)}, u32[]{:S(2)}) collective-permute-start(bf16[1,160,512]{2,1,0:T(8,128)(2,1)} %get-tuple-element.292), channel_id=1, source_target_pairs={{0,2},{1,3},{2,0},{3,1},{4,6},{5,7},{6,4},{7,5},{8,10},{9,11},{10,... | collective-permute-start | bytes 491528 | tf_op jit(solution)/shard_map/ppermute | solution.py:653
  151.0 2.7 %vectors.1 = f32[32,512]{1,0:T(8,128)} custom-call(s32[1]{0:T(128)} %bitcast.me, s32[1,2048]{1,0:T(1,128)} %constant.20.clone.lane_masks.masks, f32[3,1024]{1,0:T(4,128)} %get-tuple-element.230.offsets, f32[1,1024]{1,0:T(1,128)} %get-tuple-element.231.shift_0, f32[1,1024]{1,0:T(1,128)} %get-tuple-element.232.shift_1, f32[1,512]{1,0:T(1,128)} %get-tuple-element.237.prescale, ...), custom_call_target="tpu_custom_call" | custom-call | flops 99999997952 | bytes 100000000 | tf_op jit(solution)/shard_map/vectors/pallas_call | solution.py:171
  155.3 2.6 %all-to-all-start = ((f32[32,1,512]{2,1,0:T(1,128)}), f32[32,1,512]{2,1,0:T(1,128)S(1)}, u32[]{:S(2)}, u32[]{:S(2)}) async-start(f32[32,1,512]{2,1,0:T(1,128)} %copy.22), calls=%async_computation | async-start | bytes 131072 | tf_op jit(solution)/shard_map/all_to_all | solution.py:865
  158.0 3.7 %collective-permute-start.37 = (bf16[1,96,512]{2,1,0:T(8,128)(2,1)S(1)}, bf16[1,96,512]{2,1,0:T(8,128)(2,1)S(1)}, u32[]{:S(2)}, u32[]{:S(2)}) collective-permute-start(bf16[1,96,512]{2,1,0:T(8,128)(2,1)S(1)} %get-tuple-element.293), channel_id=1, source_target_pairs={{0,6},{1,7},{2,4},{3,5},{4,2},{5,3},{6,0},{7,1},{8,14},{9,15},{10,... | collective-permute-start | bytes 294920 | tf_op jit(solution)/shard_map/ppermute | solution.py:653
  162.4 3.6 %sequence.2 = f32[1024,512]{1,0:T(8,128)} custom-call(f32[1024,512]{1,0:T(8,128)} %get-tuple-element.244.values), custom_call_target="tpu_custom_call" | custom-call | flops 99999997952 | bytes 100000000 | tf_op jit(solution)/shard_map/sequence/pallas_call | solution.py:68
  166.0 2.8 %sequence.3 = bf16[1024,512]{1,0:T(8,128)(2,1)} custom-call(bf16[1024,512]{1,0:T(8,128)(2,1)} %get-tuple-element.247.values), custom_call_target="tpu_custom_call" | custom-call | flops 1000 | bytes 1000 | tf_op jit(solution)/shard_map/sequence/pallas_call | solution.py:68
  168.9 2.6 %collective-permute-done.36 = bf16[1,96,512]{2,1,0:T(8,128)(2,1)S(1)} collective-permute-done((bf16[1,96,512]{2,1,0:T(8,128)(2,1)S(1)}, bf16[1,96,512]{2,1,0:T(8,128)(2,1)S(1)}, u32[]{:S(2)}, u32[]{:S(2)}) %collective-permute-start.36) | collective-permute-done | bytes 98336 | tf_op jit(solution)/shard_map/ppermute | solution.py:653
  (179 shorter events, 44.0 us)
Async XLA Ops:
  7.5 11.8 %collective-permute-start.1 = (bf16[1,136,512]{2,1,0:T(8,128)(2,1)S(1)}, bf16[1,136,512]{2,1,0:T(8,128)(2,1)S(1)}, u32[]{:S(2)}, u32[]{:S(2)}) collective-permute-start(bf16[1,136,512]{2,1,0:T(8,128)(2,1)S(1)} %fusion.7), channel_id=1, source_target_pairs={{0,4},{1,5},{2,6},{3,7},{4,0},{5,1},{6,2},{7,3},{8,12},{9,13},{10,... | collective-permute-start | bytes 417800 | tf_op jit(solution)/shard_map/ppermute | solution.py:653
  7.5 11.8 %collective-permute-start = (bf16[1,136,512]{2,1,0:T(8,128)(2,1)S(1)}, bf16[1,136,512]{2,1,0:T(8,128)(2,1)S(1)}, u32[]{:S(2)}, u32[]{:S(2)}) collective-permute-start(bf16[1,136,512]{2,1,0:T(8,128)(2,1)S(1)} %fusion.7), channel_id=1, source_target_pairs={{0,2},{1,3},{2,0},{3,1},{4,6},{5,7},{6,4},{7,5},{8,10},{9,11},{10,... | collective-permute-start | bytes 417800 | tf_op jit(solution)/shard_map/ppermute | solution.py:653
  19.3 13.7 %collective-permute-start.6 = (bf16[4,136,512]{2,1,0:T(8,128)(2,1)S(1)}, bf16[4,136,512]{2,1,0:T(8,128)(2,1)S(1)}, u32[]{:S(2)}, u32[]{:S(2)}) collective-permute-start(bf16[4,136,512]{2,1,0:T(8,128)(2,1)S(1)} %pad_maximum_fusion.refs_0_.refs_10_), channel_id=1, source_target_pairs={{0,1},{1,0},{2,3},{3,2},{4,5},{5,4},{6,7},{7,6},{8,9},{9,8},{10,11... | collective-permute-start | bytes 1671176 | tf_op jit(solution)/shard_map/ppermute | solution.py:653
  20.9 15.1 %collective-permute-start.3 = (bf16[4,136,512]{2,1,0:T(8,128)(2,1)S(1)}, bf16[4,136,512]{2,1,0:T(8,128)(2,1)S(1)}, u32[]{:S(2)}, u32[]{:S(2)}) collective-permute-start(bf16[4,136,512]{2,1,0:T(8,128)(2,1)S(1)} %pad_maximum_fusion.refs_0_.refs_10_), channel_id=1, source_target_pairs={{0,16},{1,17},{2,18},{3,19},{4,20},{5,21},{6,22},{7,23},{8,24},{9,... | collective-permute-start | bytes 1671176 | tf_op jit(solution)/shard_map/ppermute | solution.py:653
  22.4 12.3 %collective-permute-start.5 = (bf16[1,128,512]{2,1,0:T(8,128)(2,1)S(1)}, bf16[1,128,512]{2,1,0:T(8,128)(2,1)S(1)}, u32[]{:S(2)}, u32[]{:S(2)}) collective-permute-start(bf16[1,128,512]{2,1,0:T(8,128)(2,1)S(1)} %maximum_bitcast_fusion), channel_id=1, source_target_pairs={{0,6},{1,7},{2,4},{3,5},{4,2},{5,3},{6,0},{7,1},{8,14},{9,15},{10,... | collective-permute-start | bytes 393224 | tf_op jit(solution)/shard_map/ppermute | solution.py:653
  24.9 11.1 %collective-permute-start.4 = (bf16[1,128,512]{2,1,0:T(8,128)(2,1)S(1)}, bf16[1,128,512]{2,1,0:T(8,128)(2,1)S(1)}, u32[]{:S(2)}, u32[]{:S(2)}) collective-permute-start(bf16[1,128,512]{2,1,0:T(8,128)(2,1)S(1)} %maximum_bitcast_fusion), channel_id=1, source_target_pairs={{0,4},{1,5},{2,6},{3,7},{4,0},{5,1},{6,2},{7,3},{8,12},{9,13},{10,... | collective-permute-start | bytes 393224 | tf_op jit(solution)/shard_map/ppermute | solution.py:653
  43.5 16.2 %collective-permute-start.17 = (bf16[4,128,512]{2,1,0:T(8,128)(2,1)S(1)}, bf16[4,128,512]{2,1,0:T(8,128)(2,1)S(1)}, u32[]{:S(2)}, u32[]{:S(2)}) collective-permute-start(bf16[4,128,512]{2,1,0:T(8,128)(2,1)S(1)} %constant_dynamic-update-slice_fusion.refs_10_), channel_id=1, source_target_pairs={{0,8},{1,9},{2,10},{3,11},{4,12},{5,13},{6,14},{7,15},{8,0},{9,1},... | collective-permute-start | bytes 1572872 | tf_op jit(solution)/shard_map/ppermute | solution.py:653
  44.1 15.6 %collective-permute-start.16 = (bf16[4,128,512]{2,1,0:T(8,128)(2,1)S(1)}, bf16[4,128,512]{2,1,0:T(8,128)(2,1)S(1)}, u32[]{:S(2)}, u32[]{:S(2)}) collective-permute-start(bf16[4,128,512]{2,1,0:T(8,128)(2,1)S(1)} %constant_dynamic-update-slice_fusion.refs_10_), channel_id=1, source_target_pairs={{0,16},{1,17},{2,18},{3,19},{4,20},{5,21},{6,22},{7,23},{8,24},{9,... | collective-permute-start | bytes 1572872 | tf_op jit(solution)/shard_map/ppermute | solution.py:653
  44.7 15.1 %collective-permute-start.15 = (bf16[4,128,512]{2,1,0:T(8,128)(2,1)S(1)}, bf16[4,128,512]{2,1,0:T(8,128)(2,1)S(1)}, u32[]{:S(2)}, u32[]{:S(2)}) collective-permute-start(bf16[4,128,512]{2,1,0:T(8,128)(2,1)S(1)} %constant_dynamic-update-slice_fusion.refs_10_), channel_id=1, source_target_pairs={{0,1},{1,0},{2,3},{3,2},{4,5},{5,4},{6,7},{7,6},{8,9},{9,8},{10,11... | collective-permute-start | bytes 1572872 | tf_op jit(solution)/shard_map/ppermute | solution.py:653
  59.9 17.1 %collective-permute-start.19 = (bf16[4,128,512]{2,1,0:T(8,128)(2,1)S(1)}, bf16[4,128,512]{2,1,0:T(8,128)(2,1)S(1)}, u32[]{:S(2)}, u32[]{:S(2)}) collective-permute-start(bf16[4,128,512]{2,1,0:T(8,128)(2,1)S(1)} %collective-permute-done.16.refs_0_), channel_id=1, source_target_pairs={{0,1},{1,0},{2,3},{3,2},{4,5},{5,4},{6,7},{7,6},{8,9},{9,8},{10,11... | collective-permute-start | bytes 1572872 | tf_op jit(solution)/shard_map/ppermute | solution.py:653
  77.6 20.0 %collective-permute-start.22 = (bf16[8,128,512]{2,1,0:T(8,128)(2,1)}, bf16[8,128,512]{2,1,0:T(8,128)(2,1)S(1)}, u32[]{:S(2)}, u32[]{:S(2)}) collective-permute-start(bf16[8,128,512]{2,1,0:T(8,128)(2,1)} %get-tuple-element.183), channel_id=1, source_target_pairs={{0,8},{1,9},{2,10},{3,11},{4,12},{5,13},{6,14},{7,15},{8,0},{9,1},... | collective-permute-start | bytes 3145736 | tf_op jit(solution)/shard_map/ppermute | solution.py:653
  102.6 18.7 %collective-permute-start.25 = (bf16[4,160,512]{2,1,0:T(8,128)(2,1)S(1)}, bf16[4,160,512]{2,1,0:T(8,128)(2,1)S(1)}, u32[]{:S(2)}, u32[]{:S(2)}) collective-permute-start(bf16[4,160,512]{2,1,0:T(8,128)(2,1)S(1)} %get-tuple-element.202), channel_id=1, source_target_pairs={{0,16},{1,17},{2,18},{3,19},{4,20},{5,21},{6,22},{7,23},{8,24},{9,... | collective-permute-start | bytes 1966088 | tf_op jit(solution)/shard_map/ppermute | solution.py:653
  104.2 17.1 %collective-permute-start.26 = (bf16[4,160,512]{2,1,0:T(8,128)(2,1)S(1)}, bf16[4,160,512]{2,1,0:T(8,128)(2,1)S(1)}, u32[]{:S(2)}, u32[]{:S(2)}) collective-permute-start(bf16[4,160,512]{2,1,0:T(8,128)(2,1)S(1)} %get-tuple-element.203), channel_id=1, source_target_pairs={{0,1},{1,0},{2,3},{3,2},{4,5},{5,4},{6,7},{7,6},{8,9},{9,8},{10,11... | collective-permute-start | bytes 1966088 | tf_op jit(solution)/shard_map/ppermute | solution.py:653
  122.7 20.0 %collective-permute-start.27 = (bf16[8,96,512]{2,1,0:T(8,128)(2,1)}, bf16[8,96,512]{2,1,0:T(8,128)(2,1)S(1)}, u32[]{:S(2)}, u32[]{:S(2)}) collective-permute-start(bf16[8,96,512]{2,1,0:T(8,128)(2,1)} %get-tuple-element.205), channel_id=1, source_target_pairs={{0,8},{1,9},{2,10},{3,11},{4,12},{5,13},{6,14},{7,15},{8,0},{9,1},... | collective-permute-start | bytes 2359304 | tf_op jit(solution)/shard_map/ppermute | solution.py:653
  124.2 15.3 %collective-permute-start.31 = (bf16[2,160,512]{2,1,0:T(8,128)(2,1)S(1)}, bf16[2,160,512]{2,1,0:T(8,128)(2,1)S(1)}, u32[]{:S(2)}, u32[]{:S(2)}) collective-permute-start(bf16[2,160,512]{2,1,0:T(8,128)(2,1)S(1)} %fusion), channel_id=1, source_target_pairs={{0,16},{1,17},{2,18},{3,19},{4,20},{5,21},{6,22},{7,23},{8,24},{9,... | collective-permute-start | bytes 983048 | tf_op jit(solution)/shard_map/ppermute | solution.py:653
  124.8 14.8 %collective-permute-start.32 = (bf16[2,160,512]{2,1,0:T(8,128)(2,1)S(1)}, bf16[2,160,512]{2,1,0:T(8,128)(2,1)S(1)}, u32[]{:S(2)}, u32[]{:S(2)}) collective-permute-start(bf16[2,160,512]{2,1,0:T(8,128)(2,1)S(1)} %fusion.1), channel_id=1, source_target_pairs={{0,1},{1,0},{2,3},{3,2},{4,5},{5,4},{6,7},{7,6},{8,9},{9,8},{10,11... | collective-permute-start | bytes 983048 | tf_op jit(solution)/shard_map/ppermute | solution.py:653
  125.7 17.0 %collective-permute-start.30 = (bf16[4,96,512]{2,1,0:T(8,128)(2,1)S(1)}, bf16[4,96,512]{2,1,0:T(8,128)(2,1)S(1)}, u32[]{:S(2)}, u32[]{:S(2)}) collective-permute-start(bf16[4,96,512]{2,1,0:T(8,128)(2,1)S(1)} %get-tuple-element.288), channel_id=1, source_target_pairs={{0,1},{1,0},{2,3},{3,2},{4,5},{5,4},{6,7},{7,6},{8,9},{9,8},{10,11... | collective-permute-start | bytes 1179656 | tf_op jit(solution)/shard_map/ppermute | solution.py:653
  126.9 15.8 %collective-permute-start.29 = (bf16[4,96,512]{2,1,0:T(8,128)(2,1)S(1)}, bf16[4,96,512]{2,1,0:T(8,128)(2,1)S(1)}, u32[]{:S(2)}, u32[]{:S(2)}) collective-permute-start(bf16[4,96,512]{2,1,0:T(8,128)(2,1)S(1)} %get-tuple-element.289), channel_id=1, source_target_pairs={{0,16},{1,17},{2,18},{3,19},{4,20},{5,21},{6,22},{7,23},{8,24},{9,... | collective-permute-start | bytes 1179656 | tf_op jit(solution)/shard_map/ppermute | solution.py:653
  143.5 10.2 %collective-permute-start.33 = (bf16[2,96,512]{2,1,0:T(8,128)(2,1)S(1)}, bf16[2,96,512]{2,1,0:T(8,128)(2,1)S(1)}, u32[]{:S(2)}, u32[]{:S(2)}) collective-permute-start(bf16[2,96,512]{2,1,0:T(8,128)(2,1)S(1)} %get-tuple-element.228), channel_id=1, source_target_pairs={{0,16},{1,17},{2,18},{3,19},{4,20},{5,21},{6,22},{7,23},{8,24},{9,... | collective-permute-start | bytes 589832 | tf_op jit(solution)/shard_map/ppermute | solution.py:653
  146.6 15.1 %collective-permute-start.40 = (bf16[1,160,512]{2,1,0:T(8,128)(2,1)S(1)}, bf16[1,160,512]{2,1,0:T(8,128)(2,1)S(1)}, u32[]{:S(2)}, u32[]{:S(2)}) collective-permute-start(bf16[1,160,512]{2,1,0:T(8,128)(2,1)S(1)} %get-tuple-element.290), channel_id=1, source_target_pairs={{0,6},{1,7},{2,4},{3,5},{4,2},{5,3},{6,0},{7,1},{8,14},{9,15},{10,... | collective-permute-start | bytes 491528 | tf_op jit(solution)/shard_map/ppermute | solution.py:653
  148.2 20.7 %collective-permute-start.39 = (bf16[1,160,512]{2,1,0:T(8,128)(2,1)}, bf16[1,160,512]{2,1,0:T(8,128)(2,1)}, u32[]{:S(2)}, u32[]{:S(2)}) collective-permute-start(bf16[1,160,512]{2,1,0:T(8,128)(2,1)} %get-tuple-element.291), channel_id=1, source_target_pairs={{0,4},{1,5},{2,6},{3,7},{4,0},{5,1},{6,2},{7,3},{8,12},{9,13},{10,... | collective-permute-start | bytes 491528 | tf_op jit(solution)/shard_map/ppermute | solution.py:653
  148.2 20.7 %collective-permute-start.38 = (bf16[1,160,512]{2,1,0:T(8,128)(2,1)}, bf16[1,160,512]{2,1,0:T(8,128)(2,1)}, u32[]{:S(2)}, u32[]{:S(2)}) collective-permute-start(bf16[1,160,512]{2,1,0:T(8,128)(2,1)} %get-tuple-element.292), channel_id=1, source_target_pairs={{0,2},{1,3},{2,0},{3,1},{4,6},{5,7},{6,4},{7,5},{8,10},{9,11},{10,... | collective-permute-start | bytes 491528 | tf_op jit(solution)/shard_map/ppermute | solution.py:653
  155.3 13.5 %all-to-all-start = ((f32[32,1,512]{2,1,0:T(1,128)}), f32[32,1,512]{2,1,0:T(1,128)S(1)}, u32[]{:S(2)}, u32[]{:S(2)}) async-start(f32[32,1,512]{2,1,0:T(1,128)} %copy.22), calls=%async_computation | async-start | bytes 131072 | tf_op jit(solution)/shard_map/all_to_all | solution.py:865
  158.0 10.9 %collective-permute-start.37 = (bf16[1,96,512]{2,1,0:T(8,128)(2,1)S(1)}, bf16[1,96,512]{2,1,0:T(8,128)(2,1)S(1)}, u32[]{:S(2)}, u32[]{:S(2)}) collective-permute-start(bf16[1,96,512]{2,1,0:T(8,128)(2,1)S(1)} %get-tuple-element.293), channel_id=1, source_target_pairs={{0,6},{1,7},{2,4},{3,5},{4,2},{5,3},{6,0},{7,1},{8,14},{9,15},{10,... | collective-permute-start | bytes 294920 | tf_op jit(solution)/shard_map/ppermute | solution.py:653
  (51 other events, 303.8 us)

commit v4 on v3

--- a/solution.py
+++ b/solution.py
@@ -321,14 +321,18 @@
     return matmul(hidden[part], contract[...]), matmul(slope[part], expand[...])
 
 
-def ffn_grads(normed_two, cotangent, hidden, slope, sent, kept):
+def ffn_grads(normed_two, cotangent, hidden, slope, stages, targets, sem):
     units = hidden.shape[1]
-    blocks, rows, width = kept.shape
-    unit = rows // 2
-    for j, target in enumerate((kept, sent)):
+    copies = []
+    for j in (1, 0):
+        stage = stages[j]
+        blocks, rows, width = stage.shape
+        unit = rows // 2
         cols = slice(j * units // 2, (j + 1) * units // 2)
-        target[:, :unit] = across(slope[:, cols], normed_two[...]).astype(target.dtype).reshape(blocks, unit, width)
-        target[:, unit:] = across(hidden[:, cols], cotangent[...]).astype(target.dtype).reshape(blocks, unit, width)
+        stage[:, :unit] = across(slope[:, cols], normed_two[...]).astype(stage.dtype).reshape(blocks, unit, width)
+        stage[:, unit:] = across(hidden[:, cols], cotangent[...]).astype(stage.dtype).reshape(blocks, unit, width)
+        copies += start([(stage, targets[j])], sem)
+    return copies
 
 
 def weight_copies(own, unit, expand, contract):
@@ -342,10 +346,10 @@
 
 
 def first_kernel(lists, size, skip, me, gain, shifts, inputs_h, cotangent_h, low_h, *refs):
-    readers, own, refs = refs[: len(lists)], refs[len(lists) : -22], refs[-22:]
+    readers, own, refs = refs[: len(lists)], refs[len(lists) : -24], refs[-24:]
     (residual_h, normed_h, branch_h, grad_h, sent, kept, shift_grad) = refs[:7]
     (inputs, cotangent, low, readout, expand, contract, residual, normed_two, branch, grad, hidden, slope) = refs[7:19]
-    in_sem, weight_sem, out_sem = refs[19:]
+    in_sem, weight_sem, out_sem, *stages = refs[19:]
     unit = expand.shape[1]
     width = gain.shape[1]
     arriving = start(
@@ -369,16 +373,16 @@
             part, normed_two, cotangent, shifts, 0, expand, contract, hidden, slope, shift_grad
         )
         leaving += start([(branch.at[part], branch_h.at[part]), (grad.at[part], grad_h.at[part])], out_sem)
-    ffn_grads(normed_two, cotangent, hidden, slope, sent, kept)
+    leaving += ffn_grads(normed_two, cotangent, hidden, slope, stages, (kept, sent), out_sem)
     finish(leaving)
 
 
 def second_kernel(plans, count, me, gain, shifts, residual_h, normed_h, branch_h, grad_h, cotangent_h, low_h, *refs):
     own, refs = refs[:count], refs[count:]
     output_h, back_h, rounded_h, gain_grad, sent, kept, shift_grad = refs[:7]
-    targets, refs = refs[7:-18], refs[-18:]
+    targets, refs = refs[7:-20], refs[-20:]
     residual, normed_two, branch, grad, cotangent, low, expand, contract = refs[:8]
-    output, back, rounded, hidden, slope, read_grad, in_sem, part_sem, low_sem, out_sem = refs[8:]
+    output, back, rounded, hidden, slope, read_grad, in_sem, part_sem, low_sem, out_sem, *stages = refs[8:]
     unit = expand.shape[1]
     width = gain.shape[1]
     weights = start(
@@ -412,7 +416,7 @@
         leaving += start(
             [(o.at[part], h.at[part]) for o, h in ((output, output_h), (back, back_h), (rounded, rounded_h))], out_sem
         )
-    ffn_grads(normed_two, cotangent, hidden, slope, sent, kept)
+    leaving += ffn_grads(normed_two, cotangent, hidden, slope, stages, (kept, sent), out_sem)
     finish(last)
     read_grad[...] = across(low[...], rounded[...])
     emit(me[0], plans, read_grad, targets)
@@ -435,7 +439,7 @@
     return pl.pallas_call(
         partial(first_kernel, lists, size, skip),
         in_specs=[SCALAR, WHOLE, WHOLE] + [ANY] * (3 + len(readers) + len(own)),
-        out_specs=[ANY] * 4 + [WHOLE] * 3,
+        out_specs=[ANY] * 6 + [WHOLE],
         out_shape=[
             shape((LEN, width), f32),
             shape((LEN, width), bf16),
@@ -459,7 +463,8 @@
             vmem((LEN, units), bf16),
             vmem((LEN, units), bf16),
         ]
-        + [pltpu.SemaphoreType.DMA] * 3,
+        + [pltpu.SemaphoreType.DMA] * 3
+        + [vmem(kept, f32), vmem(kept, bf16)],
         compiler_params=PARAMS,
         cost_estimate=FILLER,
         name="ffn_first",
@@ -476,7 +481,7 @@
     return pl.pallas_call(
         partial(second_kernel, plans, len(own)),
         in_specs=[SCALAR, WHOLE, WHOLE] + [ANY] * (6 + len(own)),
-        out_specs=[ANY] * 3 + [WHOLE] * (4 + len(targets)),
+        out_specs=[ANY] * 3 + [WHOLE, ANY, ANY] + [WHOLE] * (1 + len(targets)),
         out_shape=[
             shape((LEN, width), bf16),
             shape((LEN, width), f32),
@@ -503,7 +508,8 @@
             vmem((LEN, units), bf16),
             vmem((low.shape[1], width), f32),
         ]
-        + [pltpu.SemaphoreType.DMA] * 4,
+        + [pltpu.SemaphoreType.DMA] * 4
+        + [vmem(kept, f32), vmem(kept, bf16)],
         compiler_params=PARAMS,
         cost_estimate=FILLER,
         name="ffn_second",

time: 177 us -> 177 us (level)
  no operation moved by 1% of the time
where the time goes in v4:
time: 177 us; the launch traced here: 176 us
  Pallas kernels  84.9 us (48%)
  starting transfers between devices  41.2 us (23%)
  waiting for transfers between devices  31.8 us (18%)
  other arithmetic  8.43 us (5%)
  local copies, waits for them, and re-layouts  8.28 us (5%)
    ppermute x41, starting transfers between devices, swap(): return lax.ppermute(value, AXES, [(i, i ^ mask) for i in range(self.count)])  38.6 us
    ppermute x41, waiting for transfers between devices, swap(): return lax.ppermute(value, AXES, [(i, i ^ mask) for i in range(self.count)])  31.8 us
    pallas_call x1, Pallas kernels, back(): pl.pallas_call(partial(back_kernel, lists, size, skip, plans), grid=(hidd...  15.6 us
    pallas_call x1, Pallas kernels, ffn_second(): pl.pallas_call(partial(second_kernel, plans, len(own)), in_specs=[SCALAR,...  15.5 us
    pallas_call x1, Pallas kernels, ffn_first(): pl.pallas_call(partial(first_kernel, lists, size, skip), in_specs=[SCALAR...  14.9 us
    pallas_call x1, Pallas kernels, gates(): pl.pallas_call(partial(gates_kernel, lists, size, taken, len(row_arrays),...  13 us
    pallas_call x1, Pallas kernels, inputs_back(): pl.pallas_call(partial(inputs_kernel, lists, size), in_specs=[SCALAR, WHO...  11.1 us
    pallas_call x2, Pallas kernels, sequential(): pl.pallas_call(sequence_kernel, out_shape=jax.ShapeDtypeStruct(values.sha...  6.35 us
  transfers between devices with their start and end apart: 42, of which 13 were waited for; matrix products, arithmetic and copies ran while one was open for 3% of the time, Pallas kernels for 48%

profile of v4, /device:TPU:0, one launch (start us, length us, event | category | flops | bytes accessed | tf_op | source)
XLA Modules:
  0.0 175.9 jit_solution(12585388467330429106)
XLA Ops:
  2.4 5.1 %collective-permute-start.2 = (bf16[1,136,512]{2,1,0:T(8,128)(2,1)S(1)}, bf16[1,136,512]{2,1,0:T(8,128)(2,1)S(1)}, u32[]{:S(2)}, u32[]{:S(2)}) collective-permute-start(bf16[1,136,512]{2,1,0:T(8,128)(2,1)S(1)} %fusion.7), channel_id=1, source_target_pairs={{0,6},{1,7},{2,4},{3,5},{4,2},{5,3},{6,0},{7,1},{8,14},{9,15},{10,... | collective-permute-start | bytes 417800 | tf_op jit(solution)/shard_map/ppermute | solution.py:659
  8.1 2.9 %interleave.2.inputs.inputs_h = bf16[1024,512]{1,0:T(8,128)(2,1)} custom-call(bf16[1024,512]{1,0:T(8,128)(2,1)} %values.1), custom_call_target="tpu_custom_call" | custom-call | flops 1000 | bytes 1000 | tf_op jit(solution)/shard_map/interleave/pallas_call | solution.py:48
  12.1 7.2 %collective-permute-done.1 = bf16[1,136,512]{2,1,0:T(8,128)(2,1)S(1)} collective-permute-done((bf16[1,136,512]{2,1,0:T(8,128)(2,1)S(1)}, bf16[1,136,512]{2,1,0:T(8,128)(2,1)S(1)}, u32[]{:S(2)}, u32[]{:S(2)}) %collective-permute-start.1) | collective-permute-done | bytes 139296 | tf_op jit(solution)/shard_map/ppermute | solution.py:659
  19.3 1.6 collective-permute-start.6
  22.4 2.5 %collective-permute-start.5 = (bf16[1,128,512]{2,1,0:T(8,128)(2,1)S(1)}, bf16[1,128,512]{2,1,0:T(8,128)(2,1)S(1)}, u32[]{:S(2)}, u32[]{:S(2)}) collective-permute-start(bf16[1,128,512]{2,1,0:T(8,128)(2,1)S(1)} %maximum_bitcast_fusion), channel_id=1, source_target_pairs={{0,6},{1,7},{2,4},{3,5},{4,2},{5,3},{6,0},{7,1},{8,14},{9,15},{10,... | collective-permute-start | bytes 393224 | tf_op jit(solution)/shard_map/ppermute | solution.py:659
  25.9 3.0 %interleave.3.cotangent_h = bf16[1024,512]{1,0:T(8,128)(2,1)} custom-call(bf16[1024,512]{1,0:T(8,128)(2,1)} %values.2), custom_call_target="tpu_custom_call" | custom-call | flops 1000 | bytes 1000 | tf_op jit(solution)/shard_map/interleave/pallas_call | solution.py:48
  28.9 4.2 %collective-permute-done.6.refs_2_.refs_12_ = bf16[4,136,512]{2,1,0:T(8,128)(2,1)S(1)} collective-permute-done((bf16[4,136,512]{2,1,0:T(8,128)(2,1)S(1)}, bf16[4,136,512]{2,1,0:T(8,128)(2,1)S(1)}, u32[]{:S(2)}, u32[]{:S(2)}) %collective-permute-start.6) | collective-permute-done | bytes 557088 | tf_op jit(solution)/shard_map/ppermute | solution.py:659
  37.7 2.6 %collective-permute-done.9.refs_4_.refs_14_ = bf16[2,136,512]{2,1,0:T(8,128)(2,1)S(1)} collective-permute-done((bf16[2,136,512]{2,1,0:T(8,128)(2,1)S(1)}, bf16[2,136,512]{2,1,0:T(8,128)(2,1)S(1)}, u32[]{:S(2)}, u32[]{:S(2)}) %collective-permute-start.9) | collective-permute-done | bytes 278560 | tf_op jit(solution)/shard_map/ppermute | solution.py:659
  40.3 3.2 %collective-permute-done.8.refs_3_.refs_13_ = bf16[2,136,512]{2,1,0:T(8,128)(2,1)S(1)} collective-permute-done((bf16[2,136,512]{2,1,0:T(8,128)(2,1)S(1)}, bf16[2,136,512]{2,1,0:T(8,128)(2,1)S(1)}, u32[]{:S(2)}, u32[]{:S(2)}) %collective-permute-start.8) | collective-permute-done | bytes 278560 | tf_op jit(solution)/shard_map/ppermute | solution.py:659
  46.7 13.0 %gates.1 = (bf16[1024,512]{1,0:T(8,128)(2,1)}, f32[1024,1024]{1,0:T(8,128)}, bf16[1024,1024]{1,0:T(8,128)(2,1)}, bf16[1024,1024]{1,0:T(8,128)(2,1)}, bf16[1024,1...) custom-call(s32[2]{0:T(128)} %pad_add_fusion.me, ...), custom_call_target="tpu_custom_call" | custom-call | flops 99999997952 | bytes 100000000 | tf_op jit(solution)/shard_map/gates/pallas_call | solution.py:273
  59.9 1.6 collective-permute-start.19
  62.6 14.9 %ffn_first.1 = (f32[1024,512]{1,0:T(8,128)}, bf16[1024,512]{1,0:T(8,128)(2,1)}, f32[1024,512]{1,0:T(8,128)}, f32[1024,512]{1,0:T(8,128)}, bf16[8,128,512]{2,1,0:...) custom-call(s32[1]{0:T(128)} %bitcast.me, f32[1,512]{1,0:T(1,128)} %get-tuple-element.150.gain, ...), custom_call_target="tpu_custom_call" | custom-call | flops 99999997952 | bytes 100000000 | tf_op jit(solution)/shard_map/ffn_first/pallas_call | solution.py:439
  81.8 15.5 %ffn_second.1 = (bf16[1024,512]{1,0:T(8,128)(2,1)}, f32[1024,512]{1,0:T(8,128)}, bf16[1024,512]{1,0:T(8,128)(2,1)}, f32[1,512]{1,0:T(1,128)}, bf16[8,128,512]{2,...) custom-call(s32[1]{0:T(128)} %bitcast.me, ...), custom_call_target="tpu_custom_call" | custom-call | flops 99999997952 | bytes 100000000 | tf_op jit(solution)/shard_map/ffn_second/pallas_call | solution.py:481
  98.1 2.9 %collective-permute-done.24 = bf16[16,32,512]{2,1,0:T(8,128)(2,1)S(1)} collective-permute-done((bf16[16,32,512]{2,1,0:T(8,128)(2,1)}, bf16[16,32,512]{2,1,0:T(8,128)(2,1)S(1)}, u32[]{:S(2)}, u32[]{:S(2)}) %collective-permute-start.24) | collective-permute-done | bytes 524320 | tf_op jit(solution)/shard_map/ppermute | solution.py:659
  105.4 15.6 %back.1 = (bf16[3,1024,1024]{2,1,0:T(8,128)(2,1)}, f32[3,1024]{1,0:T(4,128)}, f32[8,96,512]{2,1,0:T(8,128)}, f32[8,96,512]{2,1,0:T(8,128)}, bf16[8,96,512]{2,1,0:T(8,128)(2,1)}, /*index=5*/bf16[8,96,512]{2,1,0:T(8,128)(2,1)}) custom-call(s32[1]{0:T(128)} %bitcast.me, bf16[1024,512]{1,0:T(8,128)(2,1)} %get-tuple-element.191.rounded, ...), custom_call_target="tpu_custom_call" | custom-call | flops 99999997952 | bytes 100000000 | tf_op jit(solution)/shard_map/back/pallas_call | solution.py:586
  128.2 11.1 %inputs_back.1 = (f32[1024,512]{1,0:T(8,128)}, f32[1,512]{1,0:T(1,128)}) custom-call(s32[1]{0:T(128)} %bitcast.me, bf16[1024,512]{1,0:T(8,128)(2,1)} %interleave.2.inputs.inputs_h, f32[1,512]{1,0:T(1,128)} %get-tuple-element.206.gain, f32[1024,512]{1,0:T(8,128)} %get-tuple-element.207.back, bf16[3,1024,1024]{2,1,0:T(8,128)(2,1)} %get-tuple-element.218.grads_h, ...), custom_call_target="tpu_custom_call" | custom-call | flops 99999997952 | bytes 100000000 | tf_op jit(solution)/shard_map/inputs_back/pallas_call | solution.py:632
  139.3 3.1 %collective-permute-done.30 = bf16[4,96,512]{2,1,0:T(8,128)(2,1)S(1)} collective-permute-done((bf16[4,96,512]{2,1,0:T(8,128)(2,1)S(1)}, bf16[4,96,512]{2,1,0:T(8,128)(2,1)S(1)}, u32[]{:S(2)}, u32[]{:S(2)}) %collective-permute-start.30) | collective-permute-done | bytes 393248 | tf_op jit(solution)/shard_map/ppermute | solution.py:659
  147.9 2.8 %collective-permute-start.38 = (bf16[1,160,512]{2,1,0:T(8,128)(2,1)}, bf16[1,160,512]{2,1,0:T(8,128)(2,1)}, u32[]{:S(2)}, u32[]{:S(2)}) collective-permute-start(bf16[1,160,512]{2,1,0:T(8,128)(2,1)} %get-tuple-element.292), channel_id=1, source_target_pairs={{0,2},{1,3},{2,0},{3,1},{4,6},{5,7},{6,4},{7,5},{8,10},{9,11},{10,... | collective-permute-start | bytes 491528 | tf_op jit(solution)/shard_map/ppermute | solution.py:659
  150.7 2.7 %vectors.1 = f32[32,512]{1,0:T(8,128)} custom-call(s32[1]{0:T(128)} %bitcast.me, s32[1,2048]{1,0:T(1,128)} %constant.20.clone.lane_masks.masks, f32[3,1024]{1,0:T(4,128)} %get-tuple-element.230.offsets, f32[1,1024]{1,0:T(1,128)} %get-tuple-element.231.shift_0, f32[1,1024]{1,0:T(1,128)} %get-tuple-element.232.shift_1, f32[1,512]{1,0:T(1,128)} %get-tuple-element.237.prescale, ...), custom_call_target="tpu_custom_call" | custom-call | flops 99999997952 | bytes 100000000 | tf_op jit(solution)/shard_map/vectors/pallas_call | solution.py:171
  155.0 2.6 %all-to-all-start = ((f32[32,1,512]{2,1,0:T(1,128)}), f32[32,1,512]{2,1,0:T(1,128)S(1)}, u32[]{:S(2)}, u32[]{:S(2)}) async-start(f32[32,1,512]{2,1,0:T(1,128)} %copy.22), calls=%async_computation | async-start | bytes 131072 | tf_op jit(solution)/shard_map/all_to_all | solution.py:871
  157.7 3.7 %collective-permute-start.37 = (bf16[1,96,512]{2,1,0:T(8,128)(2,1)S(1)}, bf16[1,96,512]{2,1,0:T(8,128)(2,1)S(1)}, u32[]{:S(2)}, u32[]{:S(2)}) collective-permute-start(bf16[1,96,512]{2,1,0:T(8,128)(2,1)S(1)} %get-tuple-element.293), channel_id=1, source_target_pairs={{0,6},{1,7},{2,4},{3,5},{4,2},{5,3},{6,0},{7,1},{8,14},{9,15},{10,... | collective-permute-start | bytes 294920 | tf_op jit(solution)/shard_map/ppermute | solution.py:659
  162.2 3.6 %sequence.2 = f32[1024,512]{1,0:T(8,128)} custom-call(f32[1024,512]{1,0:T(8,128)} %get-tuple-element.244.values), custom_call_target="tpu_custom_call" | custom-call | flops 99999997952 | bytes 100000000 | tf_op jit(solution)/shard_map/sequence/pallas_call | solution.py:68
  165.7 2.8 %sequence.3 = bf16[1024,512]{1,0:T(8,128)(2,1)} custom-call(bf16[1024,512]{1,0:T(8,128)(2,1)} %get-tuple-element.247.values), custom_call_target="tpu_custom_call" | custom-call | flops 1000 | bytes 1000 | tf_op jit(solution)/shard_map/sequence/pallas_call | solution.py:68
  168.6 2.6 %collective-permute-done.36 = bf16[1,96,512]{2,1,0:T(8,128)(2,1)S(1)} collective-permute-done((bf16[1,96,512]{2,1,0:T(8,128)(2,1)S(1)}, bf16[1,96,512]{2,1,0:T(8,128)(2,1)S(1)}, u32[]{:S(2)}, u32[]{:S(2)}) %collective-permute-start.36) | collective-permute-done | bytes 98336 | tf_op jit(solution)/shard_map/ppermute | solution.py:659
  (179 shorter events, 44.0 us)
Async XLA Ops:
  7.5 11.8 %collective-permute-start.1 = (bf16[1,136,512]{2,1,0:T(8,128)(2,1)S(1)}, bf16[1,136,512]{2,1,0:T(8,128)(2,1)S(1)}, u32[]{:S(2)}, u32[]{:S(2)}) collective-permute-start(bf16[1,136,512]{2,1,0:T(8,128)(2,1)S(1)} %fusion.7), channel_id=1, source_target_pairs={{0,4},{1,5},{2,6},{3,7},{4,0},{5,1},{6,2},{7,3},{8,12},{9,13},{10,... | collective-permute-start | bytes 417800 | tf_op jit(solution)/shard_map/ppermute | solution.py:659
  7.5 11.8 %collective-permute-start = (bf16[1,136,512]{2,1,0:T(8,128)(2,1)S(1)}, bf16[1,136,512]{2,1,0:T(8,128)(2,1)S(1)}, u32[]{:S(2)}, u32[]{:S(2)}) collective-permute-start(bf16[1,136,512]{2,1,0:T(8,128)(2,1)S(1)} %fusion.7), channel_id=1, source_target_pairs={{0,2},{1,3},{2,0},{3,1},{4,6},{5,7},{6,4},{7,5},{8,10},{9,11},{10,... | collective-permute-start | bytes 417800 | tf_op jit(solution)/shard_map/ppermute | solution.py:659
  19.3 13.7 %collective-permute-start.6 = (bf16[4,136,512]{2,1,0:T(8,128)(2,1)S(1)}, bf16[4,136,512]{2,1,0:T(8,128)(2,1)S(1)}, u32[]{:S(2)}, u32[]{:S(2)}) collective-permute-start(bf16[4,136,512]{2,1,0:T(8,128)(2,1)S(1)} %pad_maximum_fusion.refs_0_.refs_10_), channel_id=1, source_target_pairs={{0,1},{1,0},{2,3},{3,2},{4,5},{5,4},{6,7},{7,6},{8,9},{9,8},{10,11... | collective-permute-start | bytes 1671176 | tf_op jit(solution)/shard_map/ppermute | solution.py:659
  20.9 15.1 %collective-permute-start.3 = (bf16[4,136,512]{2,1,0:T(8,128)(2,1)S(1)}, bf16[4,136,512]{2,1,0:T(8,128)(2,1)S(1)}, u32[]{:S(2)}, u32[]{:S(2)}) collective-permute-start(bf16[4,136,512]{2,1,0:T(8,128)(2,1)S(1)} %pad_maximum_fusion.refs_0_.refs_10_), channel_id=1, source_target_pairs={{0,16},{1,17},{2,18},{3,19},{4,20},{5,21},{6,22},{7,23},{8,24},{9,... | collective-permute-start | bytes 1671176 | tf_op jit(solution)/shard_map/ppermute | solution.py:659
  22.4 12.3 %collective-permute-start.5 = (bf16[1,128,512]{2,1,0:T(8,128)(2,1)S(1)}, bf16[1,128,512]{2,1,0:T(8,128)(2,1)S(1)}, u32[]{:S(2)}, u32[]{:S(2)}) collective-permute-start(bf16[1,128,512]{2,1,0:T(8,128)(2,1)S(1)} %maximum_bitcast_fusion), channel_id=1, source_target_pairs={{0,6},{1,7},{2,4},{3,5},{4,2},{5,3},{6,0},{7,1},{8,14},{9,15},{10,... | collective-permute-start | bytes 393224 | tf_op jit(solution)/shard_map/ppermute | solution.py:659
  24.9 11.1 %collective-permute-start.4 = (bf16[1,128,512]{2,1,0:T(8,128)(2,1)S(1)}, bf16[1,128,512]{2,1,0:T(8,128)(2,1)S(1)}, u32[]{:S(2)}, u32[]{:S(2)}) collective-permute-start(bf16[1,128,512]{2,1,0:T(8,128)(2,1)S(1)} %maximum_bitcast_fusion), channel_id=1, source_target_pairs={{0,4},{1,5},{2,6},{3,7},{4,0},{5,1},{6,2},{7,3},{8,12},{9,13},{10,... | collective-permute-start | bytes 393224 | tf_op jit(solution)/shard_map/ppermute | solution.py:659
  43.5 16.2 %collective-permute-start.17 = (bf16[4,128,512]{2,1,0:T(8,128)(2,1)S(1)}, bf16[4,128,512]{2,1,0:T(8,128)(2,1)S(1)}, u32[]{:S(2)}, u32[]{:S(2)}) collective-permute-start(bf16[4,128,512]{2,1,0:T(8,128)(2,1)S(1)} %constant_dynamic-update-slice_fusion.refs_10_), channel_id=1, source_target_pairs={{0,8},{1,9},{2,10},{3,11},{4,12},{5,13},{6,14},{7,15},{8,0},{9,1},... | collective-permute-start | bytes 1572872 | tf_op jit(solution)/shard_map/ppermute | solution.py:659
  44.1 15.6 %collective-permute-start.16 = (bf16[4,128,512]{2,1,0:T(8,128)(2,1)S(1)}, bf16[4,128,512]{2,1,0:T(8,128)(2,1)S(1)}, u32[]{:S(2)}, u32[]{:S(2)}) collective-permute-start(bf16[4,128,512]{2,1,0:T(8,128)(2,1)S(1)} %constant_dynamic-update-slice_fusion.refs_10_), channel_id=1, source_target_pairs={{0,16},{1,17},{2,18},{3,19},{4,20},{5,21},{6,22},{7,23},{8,24},{9,... | collective-permute-start | bytes 1572872 | tf_op jit(solution)/shard_map/ppermute | solution.py:659
  44.7 15.1 %collective-permute-start.15 = (bf16[4,128,512]{2,1,0:T(8,128)(2,1)S(1)}, bf16[4,128,512]{2,1,0:T(8,128)(2,1)S(1)}, u32[]{:S(2)}, u32[]{:S(2)}) collective-permute-start(bf16[4,128,512]{2,1,0:T(8,128)(2,1)S(1)} %constant_dynamic-update-slice_fusion.refs_10_), channel_id=1, source_target_pairs={{0,1},{1,0},{2,3},{3,2},{4,5},{5,4},{6,7},{7,6},{8,9},{9,8},{10,11... | collective-permute-start | bytes 1572872 | tf_op jit(solution)/shard_map/ppermute | solution.py:659
  59.9 17.6 %collective-permute-start.19 = (bf16[4,128,512]{2,1,0:T(8,128)(2,1)S(1)}, bf16[4,128,512]{2,1,0:T(8,128)(2,1)S(1)}, u32[]{:S(2)}, u32[]{:S(2)}) collective-permute-start(bf16[4,128,512]{2,1,0:T(8,128)(2,1)S(1)} %collective-permute-done.16.refs_0_), channel_id=1, source_target_pairs={{0,1},{1,0},{2,3},{3,2},{4,5},{5,4},{6,7},{7,6},{8,9},{9,8},{10,11... | collective-permute-start | bytes 1572872 | tf_op jit(solution)/shard_map/ppermute | solution.py:659
  78.1 19.2 %collective-permute-start.22 = (bf16[8,128,512]{2,1,0:T(8,128)(2,1)}, bf16[8,128,512]{2,1,0:T(8,128)(2,1)S(1)}, u32[]{:S(2)}, u32[]{:S(2)}) collective-permute-start(bf16[8,128,512]{2,1,0:T(8,128)(2,1)} %get-tuple-element.183), channel_id=1, source_target_pairs={{0,8},{1,9},{2,10},{3,11},{4,12},{5,13},{6,14},{7,15},{8,0},{9,1},... | collective-permute-start | bytes 3145736 | tf_op jit(solution)/shard_map/ppermute | solution.py:659
  102.4 18.7 %collective-permute-start.25 = (bf16[4,160,512]{2,1,0:T(8,128)(2,1)S(1)}, bf16[4,160,512]{2,1,0:T(8,128)(2,1)S(1)}, u32[]{:S(2)}, u32[]{:S(2)}) collective-permute-start(bf16[4,160,512]{2,1,0:T(8,128)(2,1)S(1)} %get-tuple-element.202), channel_id=1, source_target_pairs={{0,16},{1,17},{2,18},{3,19},{4,20},{5,21},{6,22},{7,23},{8,24},{9,... | collective-permute-start | bytes 1966088 | tf_op jit(solution)/shard_map/ppermute | solution.py:659
  103.9 17.1 %collective-permute-start.26 = (bf16[4,160,512]{2,1,0:T(8,128)(2,1)S(1)}, bf16[4,160,512]{2,1,0:T(8,128)(2,1)S(1)}, u32[]{:S(2)}, u32[]{:S(2)}) collective-permute-start(bf16[4,160,512]{2,1,0:T(8,128)(2,1)S(1)} %get-tuple-element.203), channel_id=1, source_target_pairs={{0,1},{1,0},{2,3},{3,2},{4,5},{5,4},{6,7},{7,6},{8,9},{9,8},{10,11... | collective-permute-start | bytes 1966088 | tf_op jit(solution)/shard_map/ppermute | solution.py:659
  122.4 20.0 %collective-permute-start.27 = (bf16[8,96,512]{2,1,0:T(8,128)(2,1)}, bf16[8,96,512]{2,1,0:T(8,128)(2,1)S(1)}, u32[]{:S(2)}, u32[]{:S(2)}) collective-permute-start(bf16[8,96,512]{2,1,0:T(8,128)(2,1)} %get-tuple-element.205), channel_id=1, source_target_pairs={{0,8},{1,9},{2,10},{3,11},{4,12},{5,13},{6,14},{7,15},{8,0},{9,1},... | collective-permute-start | bytes 2359304 | tf_op jit(solution)/shard_map/ppermute | solution.py:659
  123.9 15.3 %collective-permute-start.31 = (bf16[2,160,512]{2,1,0:T(8,128)(2,1)S(1)}, bf16[2,160,512]{2,1,0:T(8,128)(2,1)S(1)}, u32[]{:S(2)}, u32[]{:S(2)}) collective-permute-start(bf16[2,160,512]{2,1,0:T(8,128)(2,1)S(1)} %fusion), channel_id=1, source_target_pairs={{0,16},{1,17},{2,18},{3,19},{4,20},{5,21},{6,22},{7,23},{8,24},{9,... | collective-permute-start | bytes 983048 | tf_op jit(solution)/shard_map/ppermute | solution.py:659
  124.5 14.7 %collective-permute-start.32 = (bf16[2,160,512]{2,1,0:T(8,128)(2,1)S(1)}, bf16[2,160,512]{2,1,0:T(8,128)(2,1)S(1)}, u32[]{:S(2)}, u32[]{:S(2)}) collective-permute-start(bf16[2,160,512]{2,1,0:T(8,128)(2,1)S(1)} %fusion.1), channel_id=1, source_target_pairs={{0,1},{1,0},{2,3},{3,2},{4,5},{5,4},{6,7},{7,6},{8,9},{9,8},{10,11... | collective-permute-start | bytes 983048 | tf_op jit(solution)/shard_map/ppermute | solution.py:659
  125.4 17.0 %collective-permute-start.30 = (bf16[4,96,512]{2,1,0:T(8,128)(2,1)S(1)}, bf16[4,96,512]{2,1,0:T(8,128)(2,1)S(1)}, u32[]{:S(2)}, u32[]{:S(2)}) collective-permute-start(bf16[4,96,512]{2,1,0:T(8,128)(2,1)S(1)} %get-tuple-element.288), channel_id=1, source_target_pairs={{0,1},{1,0},{2,3},{3,2},{4,5},{5,4},{6,7},{7,6},{8,9},{9,8},{10,11... | collective-permute-start | bytes 1179656 | tf_op jit(solution)/shard_map/ppermute | solution.py:659
  126.7 15.8 %collective-permute-start.29 = (bf16[4,96,512]{2,1,0:T(8,128)(2,1)S(1)}, bf16[4,96,512]{2,1,0:T(8,128)(2,1)S(1)}, u32[]{:S(2)}, u32[]{:S(2)}) collective-permute-start(bf16[4,96,512]{2,1,0:T(8,128)(2,1)S(1)} %get-tuple-element.289), channel_id=1, source_target_pairs={{0,16},{1,17},{2,18},{3,19},{4,20},{5,21},{6,22},{7,23},{8,24},{9,... | collective-permute-start | bytes 1179656 | tf_op jit(solution)/shard_map/ppermute | solution.py:659
  143.2 10.2 %collective-permute-start.33 = (bf16[2,96,512]{2,1,0:T(8,128)(2,1)S(1)}, bf16[2,96,512]{2,1,0:T(8,128)(2,1)S(1)}, u32[]{:S(2)}, u32[]{:S(2)}) collective-permute-start(bf16[2,96,512]{2,1,0:T(8,128)(2,1)S(1)} %get-tuple-element.228), channel_id=1, source_target_pairs={{0,16},{1,17},{2,18},{3,19},{4,20},{5,21},{6,22},{7,23},{8,24},{9,... | collective-permute-start | bytes 589832 | tf_op jit(solution)/shard_map/ppermute | solution.py:659
  146.3 15.1 %collective-permute-start.40 = (bf16[1,160,512]{2,1,0:T(8,128)(2,1)S(1)}, bf16[1,160,512]{2,1,0:T(8,128)(2,1)S(1)}, u32[]{:S(2)}, u32[]{:S(2)}) collective-permute-start(bf16[1,160,512]{2,1,0:T(8,128)(2,1)S(1)} %get-tuple-element.290), channel_id=1, source_target_pairs={{0,6},{1,7},{2,4},{3,5},{4,2},{5,3},{6,0},{7,1},{8,14},{9,15},{10,... | collective-permute-start | bytes 491528 | tf_op jit(solution)/shard_map/ppermute | solution.py:659
  147.9 20.6 %collective-permute-start.39 = (bf16[1,160,512]{2,1,0:T(8,128)(2,1)}, bf16[1,160,512]{2,1,0:T(8,128)(2,1)}, u32[]{:S(2)}, u32[]{:S(2)}) collective-permute-start(bf16[1,160,512]{2,1,0:T(8,128)(2,1)} %get-tuple-element.291), channel_id=1, source_target_pairs={{0,4},{1,5},{2,6},{3,7},{4,0},{5,1},{6,2},{7,3},{8,12},{9,13},{10,... | collective-permute-start | bytes 491528 | tf_op jit(solution)/shard_map/ppermute | solution.py:659
  147.9 20.7 %collective-permute-start.38 = (bf16[1,160,512]{2,1,0:T(8,128)(2,1)}, bf16[1,160,512]{2,1,0:T(8,128)(2,1)}, u32[]{:S(2)}, u32[]{:S(2)}) collective-permute-start(bf16[1,160,512]{2,1,0:T(8,128)(2,1)} %get-tuple-element.292), channel_id=1, source_target_pairs={{0,2},{1,3},{2,0},{3,1},{4,6},{5,7},{6,4},{7,5},{8,10},{9,11},{10,... | collective-permute-start | bytes 491528 | tf_op jit(solution)/shard_map/ppermute | solution.py:659
  155.0 13.5 %all-to-all-start = ((f32[32,1,512]{2,1,0:T(1,128)}), f32[32,1,512]{2,1,0:T(1,128)S(1)}, u32[]{:S(2)}, u32[]{:S(2)}) async-start(f32[32,1,512]{2,1,0:T(1,128)} %copy.22), calls=%async_computation | async-start | bytes 131072 | tf_op jit(solution)/shard_map/all_to_all | solution.py:871
  157.7 10.9 %collective-permute-start.37 = (bf16[1,96,512]{2,1,0:T(8,128)(2,1)S(1)}, bf16[1,96,512]{2,1,0:T(8,128)(2,1)S(1)}, u32[]{:S(2)}, u32[]{:S(2)}) collective-permute-start(bf16[1,96,512]{2,1,0:T(8,128)(2,1)S(1)} %get-tuple-element.293), channel_id=1, source_target_pairs={{0,6},{1,7},{2,4},{3,5},{4,2},{5,3},{6,0},{7,1},{8,14},{9,15},{10,... | collective-permute-start | bytes 294920 | tf_op jit(solution)/shard_map/ppermute | solution.py:659
  (51 other events, 303.6 us)
